TPU v7x, 32 devices: a whole 2x2x4 slice. The times are simulated.
32 devices in a mesh: groups: 2 (over x), ab: 16 (over z, y, core).
Axes of the slice: x: 2, y: 2, z: 4, core: 2. Of those that a mesh axis runs over, the one named last changes fastest.
Arguments:
- amplitudes: bfloat16 [512, 32768], P(('groups', 'ab')), parts along dimension 0, may hold values from -6 to 6
- integrals: bfloat16 [4096, 32768], P('groups', 'ab'), parts along dimension 0, may hold values from -0.0625 to 0.0625
- block_mask: int32 [32, 256], P('groups', 'ab'), parts along dimension 0, may hold values 0 or 1
- pair_list: int32 [512], P('groups'), parts along dimension 0, may hold values from 0 to 255, each once
Outputs:
- residual: float32 [4096, 256], P(('groups', 'ab')), parts along dimension 0
There are 2 independent parts, one for each index of `groups`. A program takes and returns all parts, laid end to end along the dimension named above; each array names one. Nothing has to cross between parts.
Inputs may be any that keep to these rules, and one draw needn't show every extreme that they name: `pair_list`: a permutation of the pair positions.
All inputs are finite; a program needn't handle non-finite values. No bound on the sum of `block_mask` on one device may be relied on, other than what follows from the above.
Results may differ from a plain program's by a relative error of at most 0.0003.
Values may be sent and summed in bfloat16 or wider, within the bound.
No kernel may reach another device: no remote copies, remote signals or barrier semaphores. Data moves between devices by JAX's collectives and lax.ppermute only.
A program may use at most 128 MiB of HBM per device.

v0:
```python
import jax
import jax.numpy as jnp
from jax import lax
from jax.sharding import PartitionSpec as P

TILE = 128


def per_device(amplitudes, integrals, block_mask, pair_list):
    tiles_ab = block_mask.shape[0]
    tiles_cd = block_mask.shape[1]
    shaped = integrals.reshape(tiles_ab, TILE, tiles_cd, TILE)
    masked = (shaped * block_mask.astype(integrals.dtype)[:, None, :, None]).reshape(
        integrals.shape
    )
    received = lax.all_to_all(amplitudes, "ab", split_axis=1, concat_axis=0, tiled=True)
    partial_sum = jnp.dot(masked, received.T, preferred_element_type=jnp.float32)
    summed = lax.psum_scatter(partial_sum, "ab", scatter_dimension=0, tiled=True)
    return jnp.zeros_like(summed).at[:, pair_list].set(summed)


def solution(mesh):
    placed = (P(("groups", "ab"), None), P("groups", "ab"), P("groups", "ab"), P("groups"))
    return jax.shard_map(
        per_device, mesh=mesh, in_specs=placed, out_specs=P(("groups", "ab"), None), check_vma=False
    )
```

profile of v0, /device:TPU:0, one launch (start us, length us, event | category | flops | bytes accessed | tf_op | source)
XLA Modules:
  0.0 120.0 jit_solution(16381261274512320510)
XLA Ops:
  6.5 2.3 %copy.22 = bf16[2,16,8,2048]{3,2,0,1:T(8,128)(2,1)} copy(bf16[2,16,8,2048]{3,2,1,0:T(8,128)(2,1)} %bitcast.15) | data formatting | bytes 2097152 | tf_op jit(solution)/shard_map/all_to_all | solution.py:16
  8.8 7.4 %all-to-all-start = ((bf16[16,16,2048]{2,0,1:T(8,128)(2,1)}), bf16[16,16,2048]{2,0,1:T(8,128)(2,1)S(1)}, u32[]{:S(2)}, u32[]{:S(2)}) async-start(bf16[16,16,2048]{2,0,1:T(8,128)(2,1)} %bitcast.13), calls=%async_computation | async-start | bytes 2097152 | tf_op jit(solution)/shard_map/all_to_all | solution.py:16
  16.2 0.0 reduce-scatter.2.cloned.1.call-start
  16.3 0.7 convert_element_type.3
  17.0 22.2 %all-to-all-done = bf16[16,16,2048]{2,0,1:T(8,128)(2,1)S(1)} async-done(((bf16[16,16,2048]{2,0,1:T(8,128)(2,1)}), bf16[16,16,2048]{2,0,1:T(8,128)(2,1)S(1)}, u32[]{:S(2)}, u32[]{:S(2)}) %all-to-all-start) | async-done | bytes 1048608 | tf_op jit(solution)/shard_map/all_to_all | solution.py:16
  39.2 0.0 copy-start.1
  39.2 1.1 mul.11
  40.3 2.2 %copy-done.1 = bf16[2048,2048]{1,0:T(8,128)(2,1)S(1)} copy-done((bf16[2048,2048]{1,0:T(8,128)(2,1)S(1)}, bf16[2048,2048]{1,0:T(8,128)(2,1)}, u32[]{:S(2)}) %copy-start.1) | copy-done | bytes 8388632
  42.6 0.0 copy-start
  42.6 3.8 %fusion = f32[2048,256]{1,0:T(8,128)} fusion(bf16[256,2048]{1,0:T(8,128)(2,1)S(1)} %bitcast.16, bf16[2048,2048]{1,0:T(8,128)(2,1)S(1)} %copy-done.1, bf16[256,8,16,128]{3,2,1,0:T(8,128)(2,1)S(1)} %bitcast.14), kind=kOutput, calls=%fused_computation.2 | convolution fusion | flops 2151677952 | bytes 19922944 | tf_op jit(solution)/shard_map/dot_general | solution.py:17
  46.3 0.0 reduce-scatter.2.cloned.1.call-update
  46.4 0.0 copy-done
  46.4 63.8 %reduce-scatter.2.cloned.1.call-done = f32[128,256]{1,0:T(8,128)} async-done(((f32[2048,256]{1,0:T(8,128)}), f32[128,256]{1,0:T(8,128)}) %reduce-scatter.2.cloned.1.call-update) | async-done | bytes 131088 | tf_op jit(solution)/shard_map/reduce_scatter | solution.py:18
  110.2 1.0 copy.13
  111.2 1.2 scatter_custom_fusion
  112.4 0.8 copy.14
  (1 shorter events, 0.0 us)
Async XLA Ops:
  8.8 30.3 %all-to-all-start = ((bf16[16,16,2048]{2,0,1:T(8,128)(2,1)}), bf16[16,16,2048]{2,0,1:T(8,128)(2,1)S(1)}, u32[]{:S(2)}, u32[]{:S(2)}) async-start(bf16[16,16,2048]{2,0,1:T(8,128)(2,1)} %bitcast.13), calls=%async_computation | async-start | bytes 2097152 | tf_op jit(solution)/shard_map/all_to_all | solution.py:16
  16.2 94.0 %reduce-scatter.2.cloned.1.call-start = ((), (), s32[]{:S(2)}) async-start(), calls=%async_computation.2 | async-start | bytes 2228224 | tf_op jit(solution)/shard_map/reduce_scatter | solution.py:18
  39.2 3.4 %copy-start.1 = (bf16[2048,2048]{1,0:T(8,128)(2,1)S(1)}, bf16[2048,2048]{1,0:T(8,128)(2,1)}, u32[]{:S(2)}) copy-start(bf16[2048,2048]{1,0:T(8,128)(2,1)} %param.5) | copy-start | bytes 25165828
  42.6 3.8 %copy-start = (s32[256]{0:T(256)S(1)}, s32[256]{0:T(256)}, u32[]{:S(2)}) copy-start(s32[256]{0:T(256)} %param.7) | copy-start | bytes 3076
Sparse Core Ops, SparseCore 0:
  46.5 63.6 reduce-scatter.1
where the time goes:
time: 120 us
  waiting for transfers between devices  86 us (72%)
  between operations  13.4 us (11%)
  local copies, waits for them, and re-layouts  8.62 us (7%)
  starting transfers between devices  7.43 us (6%)
  matrix products  3.79 us (3%)
    reduce_scatter x1, waiting for transfers between devices, per_device(): lax.psum_scatter(partial_sum, 'ab', scatter_dimension=0, tiled=True)  63.8 us
    all_to_all x1, waiting for transfers between devices, per_device(): lax.all_to_all(amplitudes, 'ab', split_axis=1, concat_axis=0, tiled=True)  22.2 us
    all_to_all x1, starting transfers between devices, per_device(): lax.all_to_all(amplitudes, 'ab', split_axis=1, concat_axis=0, tiled=True)  7.39 us
    dot_general x1, matrix products, per_device(): jnp.dot(masked, received.T, preferred_element_type=jnp.float32)  3.79 us
  transfers between devices with their start and end apart: 2, of which 2 were waited for; matrix products, arithmetic and copies ran while one was open for 1% of the time, Pallas kernels for 0%

commit v1 on v0

v1 whole, which is shorter than its diff:
```python
import functools

import jax
import jax.numpy as jnp
from jax import lax
from jax.experimental import pallas as pl
from jax.experimental.pallas import tpu as pltpu
from jax.sharding import PartitionSpec as P

TILE = 128
CHUNKS = 1
WHOLE = pl.BlockSpec(memory_space=pltpu.VMEM)


def f32(*shape):
    return jax.ShapeDtypeStruct(shape, jnp.float32)


def call(kernel, name, outs, *args):
    moved = sum(a.size * a.dtype.itemsize for a in (*args, *outs))
    return pl.pallas_call(
        kernel,
        out_shape=outs,
        in_specs=[WHOLE] * len(args),
        out_specs=[WHOLE] * len(outs),
        name=name,
        compiler_params=pltpu.CompilerParams(vmem_limit_bytes=48 * 2**20),
        cost_estimate=pl.CostEstimate(flops=moved // 4, bytes_accessed=moved, transcendentals=0),
    )(*args)


def product_kernel(me_ref, mask_ref, rows_ref, amplitudes_ref, send_ref, keep_ref):
    step = pl.program_id(0)
    me = me_ref[0]
    tiles_cd = mask_ref.shape[1]
    base = ((me // 2) ^ step) * 2
    for out_ref, core in ((send_ref, 1 - me % 2), (keep_ref, me % 2)):
        rows = rows_ref[pl.ds(pl.multiple_of(core * TILE, TILE), TILE), :]
        masked = jnp.concatenate(
            [
                rows[:, t * TILE : (t + 1) * TILE] * mask_ref[base + core, t].astype(jnp.float32).astype(rows.dtype)
                for t in range(tiles_cd)
            ],
            axis=1,
        )
        out_ref[0] = lax.dot_general(
            masked, amplitudes_ref[...], (((1,), (1,)), ((), ())), preferred_element_type=jnp.float32
        )


def product(me, block_mask, integrals, amplitudes):
    rows, depth = integrals.shape
    pairs = amplitudes.shape[0]
    chips = rows // (2 * TILE)
    spec = pl.BlockSpec((1, TILE, pairs), lambda k, me: (k, 0, 0))
    return pl.pallas_call(
        product_kernel,
        grid_spec=pltpu.PrefetchScalarGridSpec(
            num_scalar_prefetch=1,
            grid=(chips,),
            in_specs=[
                pl.BlockSpec(memory_space=pltpu.SMEM),
                pl.BlockSpec((2 * TILE, depth), lambda k, me: ((me[0] // 2) ^ k, 0)),
                pl.BlockSpec((pairs, depth), lambda k, me: (0, 0)),
            ],
            out_specs=[spec, spec],
        ),
        out_shape=[f32(chips, TILE, pairs)] * 2,
        name="product",
        compiler_params=pltpu.CompilerParams(vmem_limit_bytes=32 * 2**20),
        cost_estimate=pl.CostEstimate(
            flops=2 * rows * depth * pairs,
            bytes_accessed=2 * rows * depth + 2 * pairs * depth + 4 * rows * pairs,
            transcendentals=0,
        ),
    )(me, block_mask, integrals, amplitudes)


def core_kernel(far, keep_ref, got_ref, a_send, a_keep, b_keep, *b_send):
    half = TILE // 2
    for h in range(far):
        for low in range(2):
            k = 2 * h + low
            a_ref = a_send if low else a_keep
            a_ref[h] = keep_ref[k, :half] + got_ref[k, :half]
            b_ref = b_send[h - 1] if h else b_keep
            b_ref[low] = keep_ref[k, half:] + got_ref[k, half:]


def middle_kernel(far, a_keep, a_got, b_keep, *refs):
    b_got, (b_send, b_own, a_own), a_send = refs[: far - 1], refs[far - 1 : far + 2], refs[far + 2 :]
    for h in range(far):
        a_ref = a_send[h - 1] if h else a_own
        a_ref[...] = a_keep[h] + a_got[h]
    for low in range(2):
        total = b_keep[low]
        for got in b_got:
            total += got[low]
        b_ref = b_send if low else b_own
        b_ref[...] = total


def last_kernel(far, chunks, *refs):
    pairs_refs, refs = refs[:chunks], refs[chunks:]
    out_ref = refs[-1]
    half, pairs = TILE // 2, out_ref.shape[1]
    each = 2 + far
    total = None
    for c in range(chunks):
        a_own, b_own, b_got, *a_got = refs[c * each : (c + 1) * each]
        top = a_own[...]
        for got in a_got:
            top += got[...]
        rest = jnp.concatenate([top, b_own[...] + b_got[...]], axis=0)
        places = lax.broadcasted_iota(jnp.int32, (rest.shape[1], pairs), 1)
        chosen = (pairs_refs[c][...] == places).astype(jnp.float32).astype(jnp.bfloat16)
        for _ in range(3):
            part = rest.astype(jnp.bfloat16)
            rest = rest - part.astype(jnp.float32)
            moved = jnp.dot(part, chosen, preferred_element_type=jnp.float32)
            total = moved if total is None else total + moved
    out_ref[...] = total


def per_device(devices, amplitudes, integrals, block_mask, pair_list):
    me = lax.axis_index("ab").reshape(1)
    far = devices // 4
    half = TILE // 2
    mine, depth = amplitudes.shape[0], integrals.shape[1]
    rows = mine // CHUNKS
    pairs = rows * devices

    def swap(value, bits):
        return lax.ppermute(value, "ab", [(i, i ^ bits) for i in range(devices)])

    places, pieces = [], []
    for c in range(CHUNKS):
        places.append(pair_list.reshape(devices, CHUNKS, rows)[:, c].reshape(-1, 1))
        chunk = amplitudes[c * rows : (c + 1) * rows]
        received = lax.all_to_all(chunk, "ab", split_axis=1, concat_axis=0, tiled=True)
        send, keep = product(me, block_mask, integrals, received)
        got = swap(send, 1)
        quarter = f32(far, half, pairs)
        a_send, a_keep, b_keep, *b_send = call(
            functools.partial(core_kernel, far), "core_sum",
            [quarter, quarter] + [f32(2, half, pairs)] * far, keep, got,
        )
        b_got = [swap(b, (h + 1) * 4) for h, b in enumerate(b_send)]
        a_got = swap(a_send, 2)
        b_send, b_own, a_own, *a_send = call(
            functools.partial(middle_kernel, far), "middle_sum",
            [f32(half, pairs)] * (far + 2), a_keep, a_got, b_keep, *b_got,
        )
        a_got = [swap(a, (h + 1) * 4) for h, a in enumerate(a_send)]
        b_got = swap(b_send, 2)
        pieces += [a_own, b_own, b_got, *a_got]
    return call(
        functools.partial(last_kernel, far, CHUNKS), "last_sum",
        [f32(TILE, pair_list.shape[0])], *places, *pieces,
    )[0]


def solution(mesh):
    placed = (P(("groups", "ab"), None), P("groups", "ab"), P("groups", "ab"), P("groups"))
    return jax.shard_map(
        functools.partial(per_device, mesh.shape["ab"]),
        mesh=mesh, in_specs=placed, out_specs=P(("groups", "ab"), None), check_vma=False,
    )
```

time: 120 us -> 76.4 us (0.64)
  waiting for transfers between devices: 86 us -> 40.1 us
  starting transfers between devices: 7.43 us -> 21 us
  between operations: 13.4 us -> 0.06 us
  Pallas kernels: 0 us -> 8.37 us
  matrix products: 3.79 us -> 0 us
  local copies, waits for them, and re-layouts: 8.62 us -> 6.54 us
    reduce_scatter x1 -> x0, waiting for transfers between devices: 63.8 us -> none  [per_device(): lax.psum_scatter(partial_sum, 'ab', scatter_dimension=0, tiled=True)]
    ppermute x0 -> x9, waiting for transfers between devices: none -> 17.2 us  [swap(): return lax.ppermute(value, 'ab', [(i, i ^ bits) for i in range(devices)])]
    ppermute x0 -> x9, starting transfers between devices: none -> 13.6 us  [swap(): return lax.ppermute(value, 'ab', [(i, i ^ bits) for i in range(devices)])]
    pallas_call x0 -> x4, Pallas kernels: none -> 8.37 us  [the longest x1 7.26 us: product(): pl.pallas_call(product_kernel, grid_spec=pltpu.PrefetchScalarGridSpec(num...]
    dot_general x1 -> x0, matrix products: 3.79 us -> none  [per_device(): jnp.dot(masked, received.T, preferred_element_type=jnp.float32)]
    scatter x2 -> x0, local copies, waits for them, and re-layouts: 1.94 us -> none  [per_device(): return jnp.zeros_like(summed).at[:, pair_list].set(summed)]
    unnamed x4 -> x6, local copies, waits for them, and re-layouts: 2.23 us -> 4.08 us
  transfers between devices with their start and end apart: 2 -> 10, of which waited for: 2 -> 7; matrix products, arithmetic and copies ran while one was open for 1% -> 0% of each run, Pallas kernels for 0% -> 0%
where the time goes in v1:
time: 76.4 us; the launch traced here: 76.1 us
  waiting for transfers between devices  40.1 us (52%)
  starting transfers between devices  21 us (27%)
  Pallas kernels  8.37 us (11%)
  local copies, waits for them, and re-layouts  6.54 us (9%)
    all_to_all x1, waiting for transfers between devices, per_device(): lax.all_to_all(chunk, 'ab', split_axis=1, concat_axis=0, tiled=True)  22.9 us
    ppermute x9, waiting for transfers between devices, swap(): return lax.ppermute(value, 'ab', [(i, i ^ bits) for i in range(devices)])  17.2 us
    ppermute x9, starting transfers between devices, swap(): return lax.ppermute(value, 'ab', [(i, i ^ bits) for i in range(devices)])  13.6 us
    all_to_all x1, starting transfers between devices, per_device(): lax.all_to_all(chunk, 'ab', split_axis=1, concat_axis=0, tiled=True)  7.39 us
    pallas_call x1, Pallas kernels, product(): pl.pallas_call(product_kernel, grid_spec=pltpu.PrefetchScalarGridSpec(num...  7.26 us
    unnamed x6, local copies, waits for them, and re-layouts  4.08 us
    all_to_all x1, local copies, waits for them, and re-layouts, per_device(): lax.all_to_all(chunk, 'ab', split_axis=1, concat_axis=0, tiled=True)  2.32 us
  transfers between devices with their start and end apart: 10, of which 7 were waited for; matrix products, arithmetic and copies ran while one was open for 0% of the time, Pallas kernels for 0%

profile of v1, /device:TPU:0, one launch (start us, length us, event | category | flops | bytes accessed | tf_op | source)
XLA Modules:
  0.0 76.1 jit_solution(18068686308213228113)
XLA Ops:
  0.0 0.0 copy-start.2
  0.0 2.3 %copy.10 = bf16[2,16,8,2048]{3,2,0,1:T(8,128)(2,1)} copy(bf16[2,16,8,2048]{3,2,1,0:T(8,128)(2,1)} %bitcast.10) | data formatting | bytes 2097152 | tf_op jit(solution)/shard_map/all_to_all | solution.py:140
  2.3 7.4 %all-to-all-start = ((bf16[16,16,2048]{2,0,1:T(8,128)(2,1)}), bf16[16,16,2048]{2,0,1:T(8,128)(2,1)S(1)}, u32[]{:S(2)}, u32[]{:S(2)}) async-start(bf16[16,16,2048]{2,0,1:T(8,128)(2,1)} %bitcast.8), calls=%async_computation | async-start | bytes 2097152 | tf_op jit(solution)/shard_map/all_to_all | solution.py:140
  9.7 22.9 %all-to-all-done = bf16[16,16,2048]{2,0,1:T(8,128)(2,1)S(1)} async-done(((bf16[16,16,2048]{2,0,1:T(8,128)(2,1)}), bf16[16,16,2048]{2,0,1:T(8,128)(2,1)S(1)}, u32[]{:S(2)}, u32[]{:S(2)}) %all-to-all-start) | async-done | bytes 1048608 | tf_op jit(solution)/shard_map/all_to_all | solution.py:140
  32.7 0.0 copy-start
  32.7 3.4 %copy-done = bf16[2048,2048]{1,0:T(8,128)(2,1)S(1)} copy-done((bf16[2048,2048]{1,0:T(8,128)(2,1)S(1)}, bf16[2048,2048]{1,0:T(8,128)(2,1)}, u32[]{:S(2)}) %copy-start) | copy-done | bytes 8388632
  36.0 0.0 copy-start.1
  36.0 0.7 copy-done.1
  36.7 7.3 %product.1 = (f32[8,128,256]{2,1,0:T(8,128)S(1)}, f32[8,128,256]{2,1,0:T(8,128)S(1)}) custom-call(s32[1]{0:T(128)} %bitcast.1.me_ref, s32[16,16]{1,0:T(8,128)S(1)} %copy-done.1, bf16[2048,2048]{1,0:T(8,128)(2,1)S(1)} %copy-done, bf16[256,2048]{1,0:T(8,128)(2,1)S(1)} %bitcast.9), custom_call_target="tpu_custom_call" | custom-call | flops 2147483648 | bytes 11534336 | tf_op jit(solution)/shard_map/product/pallas_call | solution.py:56
  44.0 0.7 collective-permute-start
  44.7 2.3 %collective-permute-done.got_ref = f32[8,128,256]{2,1,0:T(8,128)S(1)} collective-permute-done((f32[8,128,256]{2,1,0:T(8,128)S(1)}, f32[8,128,256]{2,1,0:T(8,128)S(1)}, u32[]{:S(2)}, u32[]{:S(2)}) %collective-permute-start) | collective-permute-done | bytes 1048608 | tf_op jit(solution)/shard_map/ppermute | solution.py:134
  47.0 0.1 core_sum.1
  47.1 2.0 %collective-permute-start.1 = (f32[4,64,256]{2,1,0:T(8,128)S(1)}, f32[4,64,256]{2,1,0:T(8,128)S(1)}, u32[]{:S(2)}, u32[]{:S(2)}) collective-permute-start(f32[4,64,256]{2,1,0:T(8,128)S(1)} %get-tuple-element.22), channel_id=1, source_target_pairs={{0,2},{1,3},{2,0},{3,1},{4,6},{5,7},{6,4},{7,5},{8,10},{9,11},{10,... | collective-permute-start | bytes 786440 | tf_op jit(solution)/shard_map/ppermute | solution.py:134
  49.1 3.0 %collective-permute-start.2 = (f32[2,64,256]{2,1,0:T(8,128)S(1)}, f32[2,64,256]{2,1,0:T(8,128)S(1)}, u32[]{:S(2)}, u32[]{:S(2)}) collective-permute-start(f32[2,64,256]{2,1,0:T(8,128)S(1)} %get-tuple-element.24), channel_id=1, source_target_pairs={{0,4},{1,5},{2,6},{3,7},{4,0},{5,1},{6,2},{7,3},{8,12},{9,13},{10,... | collective-permute-start | bytes 393224 | tf_op jit(solution)/shard_map/ppermute | solution.py:134
  52.1 1.4 %collective-permute-start.3 = (f32[2,64,256]{2,1,0:T(8,128)S(1)}, f32[2,64,256]{2,1,0:T(8,128)S(1)}, u32[]{:S(2)}, u32[]{:S(2)}) collective-permute-start(f32[2,64,256]{2,1,0:T(8,128)S(1)} %get-tuple-element.25), channel_id=1, source_target_pairs={{0,8},{1,9},{2,10},{3,11},{4,12},{5,13},{6,14},{7,15},{8,0},{9,1},... | collective-permute-start | bytes 393224 | tf_op jit(solution)/shard_map/ppermute | solution.py:134
  53.5 0.9 %collective-permute-start.4 = (f32[2,64,256]{2,1,0:T(8,128)S(1)}, f32[2,64,256]{2,1,0:T(8,128)S(1)}, u32[]{:S(2)}, u32[]{:S(2)}) collective-permute-start(f32[2,64,256]{2,1,0:T(8,128)S(1)} %get-tuple-element.26), channel_id=1, source_target_pairs={{0,12},{1,13},{2,14},{3,15},{4,8},{5,9},{6,10},{7,11},{8,4},{9,5},... | collective-permute-start | bytes 393224 | tf_op jit(solution)/shard_map/ppermute | solution.py:134
  54.5 2.7 %collective-permute-done.2.refs_0_ = f32[2,64,256]{2,1,0:T(8,128)S(1)} collective-permute-done((f32[2,64,256]{2,1,0:T(8,128)S(1)}, f32[2,64,256]{2,1,0:T(8,128)S(1)}, u32[]{:S(2)}, u32[]{:S(2)}) %collective-permute-start.2) | collective-permute-done | bytes 131104 | tf_op jit(solution)/shard_map/ppermute | solution.py:134
  57.1 7.7 %collective-permute-done.3.refs_1_ = f32[2,64,256]{2,1,0:T(8,128)S(1)} collective-permute-done((f32[2,64,256]{2,1,0:T(8,128)S(1)}, f32[2,64,256]{2,1,0:T(8,128)S(1)}, u32[]{:S(2)}, u32[]{:S(2)}) %collective-permute-start.3) | collective-permute-done | bytes 131104 | tf_op jit(solution)/shard_map/ppermute | solution.py:134
  64.8 0.0 collective-permute-done.4.refs_2_
  64.8 0.0 collective-permute-done.1.a_got
  64.8 0.1 middle_sum.1
  64.9 0.7 collective-permute-start.5
  65.6 2.2 %collective-permute-start.6 = (f32[64,256]{1,0:T(8,128)S(1)}, f32[64,256]{1,0:T(8,128)S(1)}, u32[]{:S(2)}, u32[]{:S(2)}) collective-permute-start(f32[64,256]{1,0:T(8,128)S(1)} %get-tuple-element.30), channel_id=1, source_target_pairs={{0,4},{1,5},{2,6},{3,7},{4,0},{5,1},{6,2},{7,3},{8,12},{9,13},{10,... | collective-permute-start | bytes 196616 | tf_op jit(solution)/shard_map/ppermute | solution.py:134
  67.8 1.2 %collective-permute-start.7 = (f32[64,256]{1,0:T(8,128)S(1)}, f32[64,256]{1,0:T(8,128)S(1)}, u32[]{:S(2)}, u32[]{:S(2)}) collective-permute-start(f32[64,256]{1,0:T(8,128)S(1)} %get-tuple-element.31), channel_id=1, source_target_pairs={{0,8},{1,9},{2,10},{3,11},{4,12},{5,13},{6,14},{7,15},{8,0},{9,1},... | collective-permute-start | bytes 196616 | tf_op jit(solution)/shard_map/ppermute | solution.py:134
  69.0 1.5 %collective-permute-start.8 = (f32[64,256]{1,0:T(8,128)S(1)}, f32[64,256]{1,0:T(8,128)S(1)}, u32[]{:S(2)}, u32[]{:S(2)}) collective-permute-start(f32[64,256]{1,0:T(8,128)S(1)} %get-tuple-element.32), channel_id=1, source_target_pairs={{0,12},{1,13},{2,14},{3,15},{4,8},{5,9},{6,10},{7,11},{8,4},{9,5},... | collective-permute-start | bytes 196616 | tf_op jit(solution)/shard_map/ppermute | solution.py:134
  70.5 0.0 copy-done.2
  70.5 0.1 copy.7.refs_0_
  70.6 0.0 collective-permute-done.5.refs_3_
  70.6 0.1 collective-permute-done.6.refs_4_
  70.8 3.5 %collective-permute-done.7.refs_5_ = f32[64,256]{1,0:T(8,128)S(1)} collective-permute-done((f32[64,256]{1,0:T(8,128)S(1)}, f32[64,256]{1,0:T(8,128)S(1)}, u32[]{:S(2)}, u32[]{:S(2)}) %collective-permute-start.7) | collective-permute-done | bytes 65568 | tf_op jit(solution)/shard_map/ppermute | solution.py:134
  74.2 0.9 %collective-permute-done.8.refs_6_ = f32[64,256]{1,0:T(8,128)S(1)} collective-permute-done((f32[64,256]{1,0:T(8,128)S(1)}, f32[64,256]{1,0:T(8,128)S(1)}, u32[]{:S(2)}, u32[]{:S(2)}) %collective-permute-start.8) | collective-permute-done | bytes 65568 | tf_op jit(solution)/shard_map/ppermute | solution.py:134
  75.1 0.9 %last_sum.1 = f32[128,256]{1,0:T(8,128)} custom-call(s32[256,1]{1,0:T(8,128)S(1)} %copy.7.refs_0_, f32[64,256]{1,0:T(8,128)S(1)} %get-tuple-element.27.refs_1_, f32[64,256]{1,0:T(8,128)S(1)} %get-tuple-element.28.refs_2_, f32[64,256]{1,0:T(8,128)S(1)} %collective-permute-done.5.refs_3_, f32[64,256]{1,0:T(8,128)S(1)} %collective-permute-done.6.refs_4_, ...), custom_call_target="tpu_custom_call" | custom-call | flops 131328 | bytes 525312 | tf_op jit(solution)/shard_map/last_sum/pallas_call | solution.py:21
Async XLA Ops:
  0.0 70.5 %copy-start.2 = (s32[256]{0:T(256)S(1)}, s32[256]{0:T(256)}, u32[]{:S(2)}) copy-start(s32[256]{0:T(256)} %param.7) | copy-start | bytes 3076
  2.3 30.3 %all-to-all-start = ((bf16[16,16,2048]{2,0,1:T(8,128)(2,1)}), bf16[16,16,2048]{2,0,1:T(8,128)(2,1)S(1)}, u32[]{:S(2)}, u32[]{:S(2)}) async-start(bf16[16,16,2048]{2,0,1:T(8,128)(2,1)} %bitcast.8), calls=%async_computation | async-start | bytes 2097152 | tf_op jit(solution)/shard_map/all_to_all | solution.py:140
  32.7 3.4 %copy-start = (bf16[2048,2048]{1,0:T(8,128)(2,1)S(1)}, bf16[2048,2048]{1,0:T(8,128)(2,1)}, u32[]{:S(2)}) copy-start(bf16[2048,2048]{1,0:T(8,128)(2,1)} %rows_ref.1) | copy-start | bytes 25165828
  36.0 0.7 copy-start.1
  44.0 3.0 %collective-permute-start = (f32[8,128,256]{2,1,0:T(8,128)S(1)}, f32[8,128,256]{2,1,0:T(8,128)S(1)}, u32[]{:S(2)}, u32[]{:S(2)}) collective-permute-start(f32[8,128,256]{2,1,0:T(8,128)S(1)} %get-tuple-element.20), channel_id=1, source_target_pairs={{0,1},{1,0},{2,3},{3,2},{4,5},{5,4},{6,7},{7,6},{8,9},{9,8},{10,11... | collective-permute-start | bytes 3145736 | tf_op jit(solution)/shard_map/ppermute | solution.py:134
  47.1 17.8 %collective-permute-start.1 = (f32[4,64,256]{2,1,0:T(8,128)S(1)}, f32[4,64,256]{2,1,0:T(8,128)S(1)}, u32[]{:S(2)}, u32[]{:S(2)}) collective-permute-start(f32[4,64,256]{2,1,0:T(8,128)S(1)} %get-tuple-element.22), channel_id=1, source_target_pairs={{0,2},{1,3},{2,0},{3,1},{4,6},{5,7},{6,4},{7,5},{8,10},{9,11},{10,... | collective-permute-start | bytes 786440 | tf_op jit(solution)/shard_map/ppermute | solution.py:134
  49.1 8.0 %collective-permute-start.2 = (f32[2,64,256]{2,1,0:T(8,128)S(1)}, f32[2,64,256]{2,1,0:T(8,128)S(1)}, u32[]{:S(2)}, u32[]{:S(2)}) collective-permute-start(f32[2,64,256]{2,1,0:T(8,128)S(1)} %get-tuple-element.24), channel_id=1, source_target_pairs={{0,4},{1,5},{2,6},{3,7},{4,0},{5,1},{6,2},{7,3},{8,12},{9,13},{10,... | collective-permute-start | bytes 393224 | tf_op jit(solution)/shard_map/ppermute | solution.py:134
  52.1 12.8 %collective-permute-start.3 = (f32[2,64,256]{2,1,0:T(8,128)S(1)}, f32[2,64,256]{2,1,0:T(8,128)S(1)}, u32[]{:S(2)}, u32[]{:S(2)}) collective-permute-start(f32[2,64,256]{2,1,0:T(8,128)S(1)} %get-tuple-element.25), channel_id=1, source_target_pairs={{0,8},{1,9},{2,10},{3,11},{4,12},{5,13},{6,14},{7,15},{8,0},{9,1},... | collective-permute-start | bytes 393224 | tf_op jit(solution)/shard_map/ppermute | solution.py:134
  53.5 11.3 %collective-permute-start.4 = (f32[2,64,256]{2,1,0:T(8,128)S(1)}, f32[2,64,256]{2,1,0:T(8,128)S(1)}, u32[]{:S(2)}, u32[]{:S(2)}) collective-permute-start(f32[2,64,256]{2,1,0:T(8,128)S(1)} %get-tuple-element.26), channel_id=1, source_target_pairs={{0,12},{1,13},{2,14},{3,15},{4,8},{5,9},{6,10},{7,11},{8,4},{9,5},... | collective-permute-start | bytes 393224 | tf_op jit(solution)/shard_map/ppermute | solution.py:134
  64.9 5.7 %collective-permute-start.5 = (f32[64,256]{1,0:T(8,128)S(1)}, f32[64,256]{1,0:T(8,128)S(1)}, u32[]{:S(2)}, u32[]{:S(2)}) collective-permute-start(f32[64,256]{1,0:T(8,128)S(1)} %get-tuple-element.29), channel_id=1, source_target_pairs={{0,2},{1,3},{2,0},{3,1},{4,6},{5,7},{6,4},{7,5},{8,10},{9,11},{10,... | collective-permute-start | bytes 196616 | tf_op jit(solution)/shard_map/ppermute | solution.py:134
  65.6 5.2 %collective-permute-start.6 = (f32[64,256]{1,0:T(8,128)S(1)}, f32[64,256]{1,0:T(8,128)S(1)}, u32[]{:S(2)}, u32[]{:S(2)}) collective-permute-start(f32[64,256]{1,0:T(8,128)S(1)} %get-tuple-element.30), channel_id=1, source_target_pairs={{0,4},{1,5},{2,6},{3,7},{4,0},{5,1},{6,2},{7,3},{8,12},{9,13},{10,... | collective-permute-start | bytes 196616 | tf_op jit(solution)/shard_map/ppermute | solution.py:134
  67.8 6.4 %collective-permute-start.7 = (f32[64,256]{1,0:T(8,128)S(1)}, f32[64,256]{1,0:T(8,128)S(1)}, u32[]{:S(2)}, u32[]{:S(2)}) collective-permute-start(f32[64,256]{1,0:T(8,128)S(1)} %get-tuple-element.31), channel_id=1, source_target_pairs={{0,8},{1,9},{2,10},{3,11},{4,12},{5,13},{6,14},{7,15},{8,0},{9,1},... | collective-permute-start | bytes 196616 | tf_op jit(solution)/shard_map/ppermute | solution.py:134
  69.0 6.1 %collective-permute-start.8 = (f32[64,256]{1,0:T(8,128)S(1)}, f32[64,256]{1,0:T(8,128)S(1)}, u32[]{:S(2)}, u32[]{:S(2)}) collective-permute-start(f32[64,256]{1,0:T(8,128)S(1)} %get-tuple-element.32), channel_id=1, source_target_pairs={{0,12},{1,13},{2,14},{3,15},{4,8},{5,9},{6,10},{7,11},{8,4},{9,5},... | collective-permute-start | bytes 196616 | tf_op jit(solution)/shard_map/ppermute | solution.py:134

commit v2 on v0

v2 whole, which is shorter than its diff:
```python
import functools

import jax
import jax.numpy as jnp
from jax import lax
from jax.experimental import pallas as pl
from jax.experimental.pallas import tpu as pltpu
from jax.sharding import PartitionSpec as P

TILE = 128
WIRE = jnp.float32
EXTRA = 16


def STREAMS(bits):
    return [(0, TILE // 2, bits), (TILE // 2, TILE, bits[1:] + bits[:1])]


WHOLE = pl.BlockSpec(memory_space=pltpu.VMEM)
SCALARS = pl.BlockSpec(memory_space=pltpu.SMEM)


def call(kernel, name, outs, *args, scalars=0, scratch=(), flops=0):
    moved = sum(a.size * a.dtype.itemsize for a in (*args, *outs))
    return pl.pallas_call(
        kernel,
        out_shape=outs,
        in_specs=[SCALARS] * scalars + [WHOLE] * (len(args) - scalars),
        out_specs=[WHOLE] * len(outs),
        scratch_shapes=list(scratch),
        name=name,
        compiler_params=pltpu.CompilerParams(vmem_limit_bytes=40 * 2**20),
        cost_estimate=pl.CostEstimate(flops=flops, bytes_accessed=moved, transcendentals=0),
    )(*args)


def sort_kernel(me_ref, amplitudes_ref, send_ref, keep_ref):
    chips, _, depth = keep_ref.shape
    chip, core = me_ref[0] // 2, me_ref[0] % 2
    for k in range(chips):
        for out_ref, to in ((send_ref, 1 - core), (keep_ref, core)):
            start = pl.multiple_of(((chip ^ k) * 2 + to) * depth, depth)
            out_ref[k] = amplitudes_ref[:, pl.ds(start, depth)]


def piece_kernel(me_ref, keep_ref, got_ref, *outs):
    mine = keep_ref.shape[1]
    core = me_ref[0] % 2

    def store(first, second):
        for k, out in enumerate(outs):
            out[:mine] = first[k]
            out[mine:] = second[k]

    pl.when(core == 0)(lambda: store(keep_ref, got_ref))
    pl.when(core == 1)(lambda: store(got_ref, keep_ref))


def mask_kernel(me_ref, mask_ref, rows_ref, out_ref):
    k, core = pl.program_id(0), me_ref[0] % 2
    base = ((me_ref[0] // 2) ^ k) * 2
    for slot, own in enumerate((1 - core, core)):
        rows = pl.ds(pl.multiple_of(own * TILE, TILE), TILE)
        for t in range(mask_ref.shape[1]):
            columns = slice(t * TILE, (t + 1) * TILE)
            factor = mask_ref[base + own, t].astype(jnp.float32).astype(out_ref.dtype)
            out_ref[slot, 0, :, columns] = rows_ref[rows, columns] * factor


def masked_rows(me, block_mask, integrals):
    rows, depth = integrals.shape
    chips = rows // (2 * TILE)
    return pl.pallas_call(
        mask_kernel,
        grid_spec=pltpu.PrefetchScalarGridSpec(
            num_scalar_prefetch=1,
            grid=(chips,),
            in_specs=[SCALARS, pl.BlockSpec((2 * TILE, depth), lambda k, me: ((me[0] // 2) ^ k, 0))],
            out_specs=pl.BlockSpec((2, 1, TILE, depth), lambda k, me: (0, k, 0, 0)),
        ),
        out_shape=jax.ShapeDtypeStruct((2, chips, TILE, depth), integrals.dtype),
        name="mask",
        compiler_params=pltpu.CompilerParams(vmem_limit_bytes=16 * 2**20),
        cost_estimate=pl.CostEstimate(flops=rows * depth, bytes_accessed=4 * rows * depth, transcendentals=0),
    )(me, block_mask, integrals)


def product_kernel(me_ref, masked_ref, *refs):
    *pieces, send_ref, keep_ref, all_ref = refs
    mine, depth = pieces[0].shape
    chip = me_ref[0] // 2
    for k, piece in enumerate(pieces):
        all_ref[pl.ds(pl.multiple_of((chip ^ k) * mine, mine), mine), :] = piece[...]
    for slot, out_ref in enumerate((send_ref, keep_ref)):
        rows = masked_ref[slot].reshape(-1, depth)
        out_ref[...] = lax.dot_general(
            rows, all_ref[...], (((1,), (1,)), ((), ())), preferred_element_type=jnp.float32
        ).reshape(out_ref.shape)


def chip_of(index, bits):
    return sum(((index >> (len(bits) - 1 - i)) & 1) << b for i, b in enumerate(bits))


def pack(values, out_ref):
    rows = values[0].shape[0]
    if out_ref.dtype == jnp.float32:
        for i, value in enumerate(values):
            out_ref[i * rows : (i + 1) * rows] = value
        return
    largest = functools.reduce(jnp.maximum, [jnp.max(jnp.abs(v), axis=0, keepdims=True) for v in values])
    exponent = jnp.ceil(jnp.log2(jnp.maximum(largest, 2.0**-110)) + 0.01)
    factor = jnp.exp2(15.0 - exponent)
    for i, value in enumerate(values):
        out_ref[i * rows : (i + 1) * rows] = jnp.round(value * factor).astype(jnp.int32).astype(jnp.int16)
    last = (EXTRA, exponent.shape[1])
    out_ref[len(values) * rows :] = jnp.broadcast_to(exponent, last).astype(jnp.int32).astype(jnp.int16)


def unpack(got_ref, rows):
    if got_ref.dtype == jnp.float32:
        return [got_ref[i : i + rows] for i in range(0, got_ref.shape[0], rows)]
    stop = got_ref.shape[0] - EXTRA
    exponent = got_ref[stop:].astype(jnp.int32).astype(jnp.float32)[:1]
    step = jnp.exp2(exponent - 15.0)
    return [got_ref[i : i + rows].astype(jnp.int32).astype(jnp.float32) * step for i in range(0, stop, rows)]


def packed(blocks, rows, columns):
    if WIRE == jnp.float32:
        return jax.ShapeDtypeStruct((blocks * rows, columns), WIRE)
    return jax.ShapeDtypeStruct((blocks * rows + EXTRA, columns), WIRE)


def first_kernel(streams, keep_ref, got_ref, *outs):
    for (start, stop, bits), send, keep in zip(streams, outs[::2], outs[1::2], strict=True):
        half = keep.shape[0]
        sums = []
        for index in range(2 * half):
            k = chip_of(index, bits)
            sums.append(keep_ref[k, start:stop] + got_ref[k, start:stop])
        for index in range(half):
            keep[index] = sums[index]
        pack(sums[half:], send)


def halve_kernel(keep_ref, got_ref, send, keep):
    half = keep.shape[0]
    got = unpack(got_ref, keep.shape[1])
    for index in range(half):
        keep[index] = keep_ref[index] + got[index]
    pack([keep_ref[index] + got[index] for index in range(half, 2 * half)], send)


def last_kernel(count, place_ref, *refs):
    *sums, out_ref = refs
    parts = [sums[2 * i][0] + unpack(sums[2 * i + 1], sums[2 * i].shape[1])[0] for i in range(count)]
    rest = jnp.concatenate(parts, axis=0) if count > 1 else parts[0]
    columns = lax.broadcasted_iota(jnp.int32, (rest.shape[1], out_ref.shape[1]), 1)
    chosen = (place_ref[...] == columns).astype(jnp.float32).astype(jnp.bfloat16)
    total = None
    for _ in range(3):
        part = rest.astype(jnp.bfloat16)
        rest = rest - part.astype(jnp.float32)
        moved = jnp.dot(part, chosen, preferred_element_type=jnp.float32)
        total = moved if total is None else total + moved
    out_ref[...] = total


def per_device(devices, amplitudes, integrals, block_mask, pair_list):
    me = lax.axis_index("ab").reshape(1)
    chips = devices // 2
    mine, depth = amplitudes.shape[0], integrals.shape[1]
    pairs = mine * devices
    kind = amplitudes.dtype

    def swap(value, bits):
        return lax.ppermute(value, "ab", [(i, i ^ bits) for i in range(devices)])

    block = jax.ShapeDtypeStruct((chips, mine, depth), kind)
    send, keep = call(sort_kernel, "sort", [block] * 2, me, amplitudes, scalars=1)
    got = swap(send, 1)
    piece = jax.ShapeDtypeStruct((2 * mine, depth), kind)
    pieces = call(piece_kernel, "pieces", [piece] * chips, me, keep, got, scalars=1)
    masked = masked_rows(me, block_mask, integrals)
    received = [pieces[0]] + [None] * (chips - 1)
    for k in reversed(range(1, chips)):
        received[k] = swap(pieces[k], 2 * k)

    partial = jax.ShapeDtypeStruct((chips, TILE, pairs), jnp.float32)
    send, keep = call(
        product_kernel, "product", [partial] * 2, me, masked, *received, scalars=1,
        scratch=[pltpu.VMEM((pairs, depth), kind)], flops=4 * chips * TILE * depth * pairs,
    )
    got = swap(send, 1)

    bits = tuple(range((chips - 1).bit_length()))
    streams = STREAMS(bits)
    outs = []
    for start, stop, _ in streams:
        outs += [packed(chips // 2, stop - start, pairs), jax.ShapeDtypeStruct((chips // 2, stop - start, pairs), jnp.float32)]
    state = call(functools.partial(first_kernel, streams), "core_sum", outs, keep, got)
    sums = []
    for s, (start, stop, order) in enumerate(streams):
        send, keep = state[2 * s : 2 * s + 2]
        for step, bit in enumerate(order):
            got = swap(send, 2 << bit)
            if step < len(order) - 1:
                half = keep.shape[0] // 2
                outs = [packed(half, stop - start, pairs), jax.ShapeDtypeStruct((half, stop - start, pairs), jnp.float32)]
                send, keep = call(halve_kernel, "halve", outs, keep, got)
        sums += [keep, got]
    return call(
        functools.partial(last_kernel, len(streams)), "last",
        [jax.ShapeDtypeStruct((TILE, pairs), jnp.float32)], pair_list.reshape(-1, 1), *sums,
    )[0]


def solution(mesh):
    placed = (P(("groups", "ab"), None), P("groups", "ab"), P("groups", "ab"), P("groups"))
    return jax.shard_map(
        functools.partial(per_device, mesh.shape["ab"]),
        mesh=mesh, in_specs=placed, out_specs=P(("groups", "ab"), None), check_vma=False,
    )
```

time: 120 us -> 65.2 us (0.54)
  waiting for transfers between devices: 86 us -> 26.8 us
  starting transfers between devices: 7.43 us -> 25.1 us
  between operations: 13.4 us -> 0.1 us
  Pallas kernels: 0 us -> 7.52 us
  matrix products: 3.79 us -> 0 us
  local copies, waits for them, and re-layouts: 8.62 us -> 5.44 us
    reduce_scatter x1 -> x0, waiting for transfers between devices: 63.8 us -> none  [per_device(): lax.psum_scatter(partial_sum, 'ab', scatter_dimension=0, tiled=True)]
    ppermute x0 -> x15, waiting for transfers between devices: none -> 26.8 us  [swap(): return lax.ppermute(value, 'ab', [(i, i ^ bits) for i in range(devices)])]
    ppermute x0 -> x15, starting transfers between devices: none -> 25.1 us  [swap(): return lax.ppermute(value, 'ab', [(i, i ^ bits) for i in range(devices)])]
    all_to_all x1 -> x0, waiting for transfers between devices: 22.2 us -> none  [per_device(): lax.all_to_all(amplitudes, 'ab', split_axis=1, concat_axis=0, tiled=True)]
    pallas_call x0 -> x10, Pallas kernels: none -> 7.52 us  [the longest x1 3.8 us: masked_rows(): pl.pallas_call(mask_kernel, grid_spec=pltpu.PrefetchScalarGridSpec(num_sc...]
    all_to_all x1 -> x0, starting transfers between devices: 7.39 us -> none  [per_device(): lax.all_to_all(amplitudes, 'ab', split_axis=1, concat_axis=0, tiled=True)]
    dot_general x1 -> x0, matrix products: 3.79 us -> none  [per_device(): jnp.dot(masked, received.T, preferred_element_type=jnp.float32)]
    unnamed x4 -> x8, local copies, waits for them, and re-layouts: 2.23 us -> 5.31 us
  transfers between devices with their start and end apart: 2 -> 15, of which waited for: 2 -> 9; matrix products, arithmetic and copies ran while one was open for 1% -> 0% of each run, Pallas kernels for 0% -> 6%
where the time goes in v2:
time: 65.2 us; the launch traced here: 65 us
  waiting for transfers between devices  26.8 us (41%)
  starting transfers between devices  25.1 us (38%)
  Pallas kernels  7.52 us (12%)
  local copies, waits for them, and re-layouts  5.44 us (8%)
    ppermute x15, waiting for transfers between devices, swap(): return lax.ppermute(value, 'ab', [(i, i ^ bits) for i in range(devices)])  26.8 us
    ppermute x15, starting transfers between devices, swap(): return lax.ppermute(value, 'ab', [(i, i ^ bits) for i in range(devices)])  25.1 us
    unnamed x8, local copies, waits for them, and re-layouts  5.31 us
    pallas_call x1, Pallas kernels, masked_rows(): pl.pallas_call(mask_kernel, grid_spec=pltpu.PrefetchScalarGridSpec(num_sc...  3.8 us
    pallas_call x9, Pallas kernels, call(): pl.pallas_call(kernel, out_shape=outs, in_specs=[SCALARS] * scalars + [WH...  3.72 us
  transfers between devices with their start and end apart: 15, of which 9 were waited for; matrix products, arithmetic and copies ran while one was open for 0% of the time, Pallas kernels for 6%

profile of v2, /device:TPU:0, one launch (start us, length us, event | category | flops | bytes accessed | tf_op | source)
XLA Modules:
  0.0 65.0 jit_solution(5648200791861711094)
XLA Ops:
  0.0 0.0 copy-start.1
  0.0 1.2 %copy-done.1 = bf16[16,32768]{1,0:T(8,128)(2,1)S(1)} copy-done((bf16[16,32768]{1,0:T(8,128)(2,1)S(1)}, bf16[16,32768]{1,0:T(8,128)(2,1)}, u32[]{:S(2)}) %copy-start.1) | copy-done | bytes 1048600
  1.2 0.1 sort.1
  1.3 0.5 collective-permute-start
  1.8 1.5 %collective-permute-done.got_ref = bf16[8,16,2048]{2,1,0:T(8,128)(2,1)S(1)} collective-permute-done((bf16[8,16,2048]{2,1,0:T(8,128)(2,1)S(1)}, bf16[8,16,2048]{2,1,0:T(8,128)(2,1)S(1)}, u32[]{:S(2)}, u32[]{:S(2)}) %collective-permute-start) | collective-permute-done | bytes 524320 | tf_op jit(solution)/shard_map/ppermute | solution.py:178
  3.4 0.1 pieces.1
  3.4 3.0 %collective-permute-start.1 = (bf16[32,2048]{1,0:T(8,128)(2,1)S(1)}, bf16[32,2048]{1,0:T(8,128)(2,1)S(1)}, u32[]{:S(2)}, u32[]{:S(2)}) collective-permute-start(bf16[32,2048]{1,0:T(8,128)(2,1)S(1)} %get-tuple-element.32), channel_id=1, source_target_pairs={{0,2},{1,3},{2,0},{3,1},{4,6},{5,7},{6,4},{7,5},{8,10},{9,11},{10,... | collective-permute-start | bytes 393224 | tf_op jit(solution)/shard_map/ppermute | solution.py:178
  6.4 1.6 %collective-permute-start.2 = (bf16[32,2048]{1,0:T(8,128)(2,1)S(1)}, bf16[32,2048]{1,0:T(8,128)(2,1)S(1)}, u32[]{:S(2)}, u32[]{:S(2)}) collective-permute-start(bf16[32,2048]{1,0:T(8,128)(2,1)S(1)} %get-tuple-element.33), channel_id=1, source_target_pairs={{0,4},{1,5},{2,6},{3,7},{4,0},{5,1},{6,2},{7,3},{8,12},{9,13},{10,... | collective-permute-start | bytes 393224 | tf_op jit(solution)/shard_map/ppermute | solution.py:178
  8.0 0.0 collective-permute-start.3
  8.0 3.0 %collective-permute-start.4 = (bf16[32,2048]{1,0:T(8,128)(2,1)S(1)}, bf16[32,2048]{1,0:T(8,128)(2,1)S(1)}, u32[]{:S(2)}, u32[]{:S(2)}) collective-permute-start(bf16[32,2048]{1,0:T(8,128)(2,1)S(1)} %get-tuple-element.35), channel_id=1, source_target_pairs={{0,8},{1,9},{2,10},{3,11},{4,12},{5,13},{6,14},{7,15},{8,0},{9,1},... | collective-permute-start | bytes 393224 | tf_op jit(solution)/shard_map/ppermute | solution.py:178
  10.9 1.3 %collective-permute-start.5 = (bf16[32,2048]{1,0:T(8,128)(2,1)S(1)}, bf16[32,2048]{1,0:T(8,128)(2,1)S(1)}, u32[]{:S(2)}, u32[]{:S(2)}) collective-permute-start(bf16[32,2048]{1,0:T(8,128)(2,1)S(1)} %get-tuple-element.36), channel_id=1, source_target_pairs={{0,10},{1,11},{2,8},{3,9},{4,14},{5,15},{6,12},{7,13},{8,2},{9,3},... | collective-permute-start | bytes 393224 | tf_op jit(solution)/shard_map/ppermute | solution.py:178
  12.2 0.0 collective-permute-done.1.refs_1_
  12.2 3.6 %collective-permute-start.6 = (bf16[32,2048]{1,0:T(8,128)(2,1)S(1)}, bf16[32,2048]{1,0:T(8,128)(2,1)S(1)}, u32[]{:S(2)}, u32[]{:S(2)}) collective-permute-start(bf16[32,2048]{1,0:T(8,128)(2,1)S(1)} %get-tuple-element.37), channel_id=1, source_target_pairs={{0,12},{1,13},{2,14},{3,15},{4,8},{5,9},{6,10},{7,11},{8,4},{9,5},... | collective-permute-start | bytes 393224 | tf_op jit(solution)/shard_map/ppermute | solution.py:178
  15.8 1.3 %collective-permute-done.2.refs_2_ = bf16[32,2048]{1,0:T(8,128)(2,1)S(1)} collective-permute-done((bf16[32,2048]{1,0:T(8,128)(2,1)S(1)}, bf16[32,2048]{1,0:T(8,128)(2,1)S(1)}, u32[]{:S(2)}, u32[]{:S(2)}) %collective-permute-start.2) | collective-permute-done | bytes 131104 | tf_op jit(solution)/shard_map/ppermute | solution.py:178
  17.1 0.7 %collective-permute-start.7 = (bf16[32,2048]{1,0:T(8,128)(2,1)S(1)}, bf16[32,2048]{1,0:T(8,128)(2,1)S(1)}, u32[]{:S(2)}, u32[]{:S(2)}) collective-permute-start(bf16[32,2048]{1,0:T(8,128)(2,1)S(1)} %get-tuple-element.38), channel_id=1, source_target_pairs={{0,14},{1,15},{2,12},{3,13},{4,10},{5,11},{6,8},{7,9},{8,6},{9,7},... | collective-permute-start | bytes 393224 | tf_op jit(solution)/shard_map/ppermute | solution.py:178
  17.8 0.0 copy-start
  17.9 3.4 %copy-done = bf16[2048,2048]{1,0:T(8,128)(2,1)S(1)} copy-done((bf16[2048,2048]{1,0:T(8,128)(2,1)S(1)}, bf16[2048,2048]{1,0:T(8,128)(2,1)}, u32[]{:S(2)}) %copy-start) | copy-done | bytes 8388632
  21.2 0.0 copy-start.2
  21.2 0.7 %copy-done.2 = s32[16,16]{1,0:T(8,128)S(1)} copy-done((s32[16,16]{1,0:T(8,128)S(1)}, s32[16,16]{1,0:T(8,128)}, u32[]{:S(2)}) %copy-start.2) | copy-done | bytes 1048
  21.9 3.8 %mask.1.masked_ref = bf16[2,8,128,2048]{3,2,1,0:T(8,128)(2,1)S(1)} custom-call(s32[1]{0:T(128)} %bitcast.1.me_ref, s32[16,16]{1,0:T(8,128)S(1)} %copy-done.2, bf16[2048,2048]{1,0:T(8,128)(2,1)S(1)} %copy-done), custom_call_target="tpu_custom_call" | custom-call | flops 4194304 | bytes 16777216 | tf_op jit(solution)/shard_map/mask/pallas_call | solution.py:73
  25.7 0.0 copy-start.3
  25.7 0.0 collective-permute-done.3.refs_3_
  25.8 0.0 collective-permute-done.4.refs_4_
  25.8 4.3 %collective-permute-done.5.refs_5_ = bf16[32,2048]{1,0:T(8,128)(2,1)S(1)} collective-permute-done((bf16[32,2048]{1,0:T(8,128)(2,1)S(1)}, bf16[32,2048]{1,0:T(8,128)(2,1)S(1)}, u32[]{:S(2)}, u32[]{:S(2)}) %collective-permute-start.5) | collective-permute-done | bytes 131104 | tf_op jit(solution)/shard_map/ppermute | solution.py:178
  30.1 0.0 collective-permute-done.6.refs_6_
  30.1 0.0 collective-permute-done.7.refs_7_
  30.1 2.4 %product.1 = (f32[8,128,256]{2,1,0:T(8,128)S(1)}, f32[8,128,256]{2,1,0:T(8,128)S(1)}) custom-call(s32[1]{0:T(128)} %bitcast.1.me_ref, bf16[2,8,128,2048]{3,2,1,0:T(8,128)(2,1)S(1)} %mask.1.masked_ref, bf16[32,2048]{1,0:T(8,128)(2,1)S(1)} %get-tuple-element.31.refs_0_, bf16[32,2048]{1,0:T(8,128)(2,1)S(1)} %collective-permute-done.1.refs_1_, ...), custom_call_target="tpu_custom_call" | custom-call | flops 2147483648 | bytes 11534340 | tf_op jit(solution)/shard_map/product/pallas_call | solution.py:25
  32.6 0.1 collective-permute-start.8
  32.6 2.6 %collective-permute-done.8.got_ref = f32[8,128,256]{2,1,0:T(8,128)S(1)} collective-permute-done((f32[8,128,256]{2,1,0:T(8,128)S(1)}, f32[8,128,256]{2,1,0:T(8,128)S(1)}, u32[]{:S(2)}, u32[]{:S(2)}) %collective-permute-start.8) | collective-permute-done | bytes 1048608 | tf_op jit(solution)/shard_map/ppermute | solution.py:178
  35.3 0.1 core_sum.1
  35.4 5.3 %collective-permute-start.12 = (f32[256,256]{1,0:T(8,128)S(1)}, f32[256,256]{1,0:T(8,128)S(1)}, u32[]{:S(2)}, u32[]{:S(2)}) collective-permute-start(f32[256,256]{1,0:T(8,128)S(1)} %get-tuple-element.48), channel_id=1, source_target_pairs={{0,4},{1,5},{2,6},{3,7},{4,0},{5,1},{6,2},{7,3},{8,12},{9,13},{10,... | collective-permute-start | bytes 786440 | tf_op jit(solution)/shard_map/ppermute | solution.py:178
  40.7 0.7 %collective-permute-start.9 = (f32[256,256]{1,0:T(8,128)S(1)}, f32[256,256]{1,0:T(8,128)S(1)}, u32[]{:S(2)}, u32[]{:S(2)}) collective-permute-start(f32[256,256]{1,0:T(8,128)S(1)} %get-tuple-element.42), channel_id=1, source_target_pairs={{0,2},{1,3},{2,0},{3,1},{4,6},{5,7},{6,4},{7,5},{8,10},{9,11},{10,... | collective-permute-start | bytes 786440 | tf_op jit(solution)/shard_map/ppermute | solution.py:178
  41.4 5.9 %collective-permute-done.12.got_ref = f32[256,256]{1,0:T(8,128)S(1)} collective-permute-done((f32[256,256]{1,0:T(8,128)S(1)}, f32[256,256]{1,0:T(8,128)S(1)}, u32[]{:S(2)}, u32[]{:S(2)}) %collective-permute-start.12) | collective-permute-done | bytes 262176 | tf_op jit(solution)/shard_map/ppermute | solution.py:178
  47.4 3.7 %collective-permute-start.13 = (f32[128,256]{1,0:T(8,128)S(1)}, f32[128,256]{1,0:T(8,128)S(1)}, u32[]{:S(2)}, u32[]{:S(2)}) collective-permute-start(f32[128,256]{1,0:T(8,128)S(1)} %get-tuple-element.50), channel_id=1, source_target_pairs={{0,8},{1,9},{2,10},{3,11},{4,12},{5,13},{6,14},{7,15},{8,0},{9,1},... | collective-permute-start | bytes 393224 | tf_op jit(solution)/shard_map/ppermute | solution.py:178
  51.1 0.0 collective-permute-done.9.got_ref
  51.1 0.4 collective-permute-start.10
  51.5 5.5 %collective-permute-done.13.got_ref = f32[128,256]{1,0:T(8,128)S(1)} collective-permute-done((f32[128,256]{1,0:T(8,128)S(1)}, f32[128,256]{1,0:T(8,128)S(1)}, u32[]{:S(2)}, u32[]{:S(2)}) %collective-permute-start.13) | collective-permute-done | bytes 131104 | tf_op jit(solution)/shard_map/ppermute | solution.py:178
  56.9 0.6 collective-permute-start.14
  57.5 0.6 collective-permute-done.10.got_ref
  58.1 0.7 %collective-permute-start.11 = (f32[64,256]{1,0:T(8,128)S(1)}, f32[64,256]{1,0:T(8,128)S(1)}, u32[]{:S(2)}, u32[]{:S(2)}) collective-permute-start(f32[64,256]{1,0:T(8,128)S(1)} %get-tuple-element.46), channel_id=1, source_target_pairs={{0,8},{1,9},{2,10},{3,11},{4,12},{5,13},{6,14},{7,15},{8,0},{9,1},... | collective-permute-start | bytes 196616 | tf_op jit(solution)/shard_map/ppermute | solution.py:178
  58.8 0.0 copy-done.3
  58.8 0.1 copy.5.place_ref
  59.0 2.3 %collective-permute-done.14.refs_3_ = f32[64,256]{1,0:T(8,128)S(1)} collective-permute-done((f32[64,256]{1,0:T(8,128)S(1)}, f32[64,256]{1,0:T(8,128)S(1)}, u32[]{:S(2)}, u32[]{:S(2)}) %collective-permute-start.14) | collective-permute-done | bytes 65568 | tf_op jit(solution)/shard_map/ppermute | solution.py:178
  61.3 2.8 %collective-permute-done.11.refs_1_ = f32[64,256]{1,0:T(8,128)S(1)} collective-permute-done((f32[64,256]{1,0:T(8,128)S(1)}, f32[64,256]{1,0:T(8,128)S(1)}, u32[]{:S(2)}, u32[]{:S(2)}) %collective-permute-start.11) | collective-permute-done | bytes 65568 | tf_op jit(solution)/shard_map/ppermute | solution.py:178
  64.0 0.9 %last.1 = f32[128,256]{1,0:T(8,128)} custom-call(s32[256,1]{1,0:T(8,128)S(1)} %copy.5.place_ref, f32[1,64,256]{2,1,0:T(8,128)S(1)} %get-tuple-element.45.refs_0_, f32[64,256]{1,0:T(8,128)S(1)} %collective-permute-done.11.refs_1_, f32[1,64,256]{2,1,0:T(8,128)S(1)} %get-tuple-element.51.refs_2_, f32[64,256]{1,0:T(8,128)S(1)} %collective-permute-done.14.refs_3_), custom_call_target="tpu_custom_call" | custom-call | bytes 394240 | tf_op jit(solution)/shard_map/last/pallas_call | solution.py:25
  (4 shorter events, 0.1 us)
Async XLA Ops:
  0.0 1.2 %copy-start.1 = (bf16[16,32768]{1,0:T(8,128)(2,1)S(1)}, bf16[16,32768]{1,0:T(8,128)(2,1)}, u32[]{:S(2)}) copy-start(bf16[16,32768]{1,0:T(8,128)(2,1)} %amplitudes_ref.1) | copy-start | bytes 3145732
  1.3 2.1 %collective-permute-start = (bf16[8,16,2048]{2,1,0:T(8,128)(2,1)S(1)}, bf16[8,16,2048]{2,1,0:T(8,128)(2,1)S(1)}, u32[]{:S(2)}, u32[]{:S(2)}) collective-permute-start(bf16[8,16,2048]{2,1,0:T(8,128)(2,1)S(1)} %get-tuple-element.30), channel_id=1, source_target_pairs={{0,1},{1,0},{2,3},{3,2},{4,5},{5,4},{6,7},{7,6},{8,9},{9,8},{10,11... | collective-permute-start | bytes 1572872 | tf_op jit(solution)/shard_map/ppermute | solution.py:178
  3.4 8.8 %collective-permute-start.1 = (bf16[32,2048]{1,0:T(8,128)(2,1)S(1)}, bf16[32,2048]{1,0:T(8,128)(2,1)S(1)}, u32[]{:S(2)}, u32[]{:S(2)}) collective-permute-start(bf16[32,2048]{1,0:T(8,128)(2,1)S(1)} %get-tuple-element.32), channel_id=1, source_target_pairs={{0,2},{1,3},{2,0},{3,1},{4,6},{5,7},{6,4},{7,5},{8,10},{9,11},{10,... | collective-permute-start | bytes 393224 | tf_op jit(solution)/shard_map/ppermute | solution.py:178
  6.4 10.8 %collective-permute-start.2 = (bf16[32,2048]{1,0:T(8,128)(2,1)S(1)}, bf16[32,2048]{1,0:T(8,128)(2,1)S(1)}, u32[]{:S(2)}, u32[]{:S(2)}) collective-permute-start(bf16[32,2048]{1,0:T(8,128)(2,1)S(1)} %get-tuple-element.33), channel_id=1, source_target_pairs={{0,4},{1,5},{2,6},{3,7},{4,0},{5,1},{6,2},{7,3},{8,12},{9,13},{10,... | collective-permute-start | bytes 393224 | tf_op jit(solution)/shard_map/ppermute | solution.py:178
  8.0 17.8 %collective-permute-start.3 = (bf16[32,2048]{1,0:T(8,128)(2,1)S(1)}, bf16[32,2048]{1,0:T(8,128)(2,1)S(1)}, u32[]{:S(2)}, u32[]{:S(2)}) collective-permute-start(bf16[32,2048]{1,0:T(8,128)(2,1)S(1)} %get-tuple-element.34), channel_id=1, source_target_pairs={{0,6},{1,7},{2,4},{3,5},{4,2},{5,3},{6,0},{7,1},{8,14},{9,15},{10,... | collective-permute-start | bytes 393224 | tf_op jit(solution)/shard_map/ppermute | solution.py:178
  8.0 17.8 %collective-permute-start.4 = (bf16[32,2048]{1,0:T(8,128)(2,1)S(1)}, bf16[32,2048]{1,0:T(8,128)(2,1)S(1)}, u32[]{:S(2)}, u32[]{:S(2)}) collective-permute-start(bf16[32,2048]{1,0:T(8,128)(2,1)S(1)} %get-tuple-element.35), channel_id=1, source_target_pairs={{0,8},{1,9},{2,10},{3,11},{4,12},{5,13},{6,14},{7,15},{8,0},{9,1},... | collective-permute-start | bytes 393224 | tf_op jit(solution)/shard_map/ppermute | solution.py:178
  10.9 19.2 %collective-permute-start.5 = (bf16[32,2048]{1,0:T(8,128)(2,1)S(1)}, bf16[32,2048]{1,0:T(8,128)(2,1)S(1)}, u32[]{:S(2)}, u32[]{:S(2)}) collective-permute-start(bf16[32,2048]{1,0:T(8,128)(2,1)S(1)} %get-tuple-element.36), channel_id=1, source_target_pairs={{0,10},{1,11},{2,8},{3,9},{4,14},{5,15},{6,12},{7,13},{8,2},{9,3},... | collective-permute-start | bytes 393224 | tf_op jit(solution)/shard_map/ppermute | solution.py:178
  12.2 17.9 %collective-permute-start.6 = (bf16[32,2048]{1,0:T(8,128)(2,1)S(1)}, bf16[32,2048]{1,0:T(8,128)(2,1)S(1)}, u32[]{:S(2)}, u32[]{:S(2)}) collective-permute-start(bf16[32,2048]{1,0:T(8,128)(2,1)S(1)} %get-tuple-element.37), channel_id=1, source_target_pairs={{0,12},{1,13},{2,14},{3,15},{4,8},{5,9},{6,10},{7,11},{8,4},{9,5},... | collective-permute-start | bytes 393224 | tf_op jit(solution)/shard_map/ppermute | solution.py:178
  17.1 13.0 %collective-permute-start.7 = (bf16[32,2048]{1,0:T(8,128)(2,1)S(1)}, bf16[32,2048]{1,0:T(8,128)(2,1)S(1)}, u32[]{:S(2)}, u32[]{:S(2)}) collective-permute-start(bf16[32,2048]{1,0:T(8,128)(2,1)S(1)} %get-tuple-element.38), channel_id=1, source_target_pairs={{0,14},{1,15},{2,12},{3,13},{4,10},{5,11},{6,8},{7,9},{8,6},{9,7},... | collective-permute-start | bytes 393224 | tf_op jit(solution)/shard_map/ppermute | solution.py:178
  17.8 3.4 %copy-start = (bf16[2048,2048]{1,0:T(8,128)(2,1)S(1)}, bf16[2048,2048]{1,0:T(8,128)(2,1)}, u32[]{:S(2)}) copy-start(bf16[2048,2048]{1,0:T(8,128)(2,1)} %rows_ref.1) | copy-start | bytes 25165828
  21.2 0.7 %copy-start.2 = (s32[16,16]{1,0:T(8,128)S(1)}, s32[16,16]{1,0:T(8,128)}, u32[]{:S(2)}) copy-start(s32[16,16]{1,0:T(8,128)} %mask_ref.1) | copy-start | bytes 3076
  25.7 33.1 %copy-start.3 = (s32[256]{0:T(256)S(1)}, s32[256]{0:T(256)}, u32[]{:S(2)}) copy-start(s32[256]{0:T(256)} %param.7) | copy-start | bytes 3076
  32.6 2.7 %collective-permute-start.8 = (f32[8,128,256]{2,1,0:T(8,128)S(1)}, f32[8,128,256]{2,1,0:T(8,128)S(1)}, u32[]{:S(2)}, u32[]{:S(2)}) collective-permute-start(f32[8,128,256]{2,1,0:T(8,128)S(1)} %get-tuple-element.40), channel_id=1, source_target_pairs={{0,1},{1,0},{2,3},{3,2},{4,5},{5,4},{6,7},{7,6},{8,9},{9,8},{10,11... | collective-permute-start | bytes 3145736 | tf_op jit(solution)/shard_map/ppermute | solution.py:178
  35.4 12.0 %collective-permute-start.12 = (f32[256,256]{1,0:T(8,128)S(1)}, f32[256,256]{1,0:T(8,128)S(1)}, u32[]{:S(2)}, u32[]{:S(2)}) collective-permute-start(f32[256,256]{1,0:T(8,128)S(1)} %get-tuple-element.48), channel_id=1, source_target_pairs={{0,4},{1,5},{2,6},{3,7},{4,0},{5,1},{6,2},{7,3},{8,12},{9,13},{10,... | collective-permute-start | bytes 786440 | tf_op jit(solution)/shard_map/ppermute | solution.py:178
  40.7 10.3 %collective-permute-start.9 = (f32[256,256]{1,0:T(8,128)S(1)}, f32[256,256]{1,0:T(8,128)S(1)}, u32[]{:S(2)}, u32[]{:S(2)}) collective-permute-start(f32[256,256]{1,0:T(8,128)S(1)} %get-tuple-element.42), channel_id=1, source_target_pairs={{0,2},{1,3},{2,0},{3,1},{4,6},{5,7},{6,4},{7,5},{8,10},{9,11},{10,... | collective-permute-start | bytes 786440 | tf_op jit(solution)/shard_map/ppermute | solution.py:178
  47.4 9.5 %collective-permute-start.13 = (f32[128,256]{1,0:T(8,128)S(1)}, f32[128,256]{1,0:T(8,128)S(1)}, u32[]{:S(2)}, u32[]{:S(2)}) collective-permute-start(f32[128,256]{1,0:T(8,128)S(1)} %get-tuple-element.50), channel_id=1, source_target_pairs={{0,8},{1,9},{2,10},{3,11},{4,12},{5,13},{6,14},{7,15},{8,0},{9,1},... | collective-permute-start | bytes 393224 | tf_op jit(solution)/shard_map/ppermute | solution.py:178
  51.1 7.0 %collective-permute-start.10 = (f32[128,256]{1,0:T(8,128)S(1)}, f32[128,256]{1,0:T(8,128)S(1)}, u32[]{:S(2)}, u32[]{:S(2)}) collective-permute-start(f32[128,256]{1,0:T(8,128)S(1)} %get-tuple-element.44), channel_id=1, source_target_pairs={{0,4},{1,5},{2,6},{3,7},{4,0},{5,1},{6,2},{7,3},{8,12},{9,13},{10,... | collective-permute-start | bytes 393224 | tf_op jit(solution)/shard_map/ppermute | solution.py:178
  56.9 4.3 %collective-permute-start.14 = (f32[64,256]{1,0:T(8,128)S(1)}, f32[64,256]{1,0:T(8,128)S(1)}, u32[]{:S(2)}, u32[]{:S(2)}) collective-permute-start(f32[64,256]{1,0:T(8,128)S(1)} %get-tuple-element.52), channel_id=1, source_target_pairs={{0,2},{1,3},{2,0},{3,1},{4,6},{5,7},{6,4},{7,5},{8,10},{9,11},{10,... | collective-permute-start | bytes 196616 | tf_op jit(solution)/shard_map/ppermute | solution.py:178
  58.1 5.9 %collective-permute-start.11 = (f32[64,256]{1,0:T(8,128)S(1)}, f32[64,256]{1,0:T(8,128)S(1)}, u32[]{:S(2)}, u32[]{:S(2)}) collective-permute-start(f32[64,256]{1,0:T(8,128)S(1)} %get-tuple-element.46), channel_id=1, source_target_pairs={{0,8},{1,9},{2,10},{3,11},{4,12},{5,13},{6,14},{7,15},{8,0},{9,1},... | collective-permute-start | bytes 196616 | tf_op jit(solution)/shard_map/ppermute | solution.py:178

commit v3 on v2

--- a/solution.py
+++ b/solution.py
@@ -8,7 +8,7 @@
 from jax.sharding import PartitionSpec as P
 
 TILE = 128
-WIRE = jnp.float32
+WIRE = jnp.int16
 EXTRA = 16
 
 

time: 65.2 us -> 59.7 us (0.916)
  waiting for transfers between devices: 26.8 us -> 20.3 us
  starting transfers between devices: 25.1 us -> 25.8 us
    ppermute x15, waiting for transfers between devices: 26.8 us -> 20.3 us  [swap(): return lax.ppermute(value, 'ab', [(i, i ^ bits) for i in range(devices)])]
    ppermute x15, starting transfers between devices: 25.1 us -> 25.8 us  [swap(): return lax.ppermute(value, 'ab', [(i, i ^ bits) for i in range(devices)])]
  transfers between devices with their start and end apart: 15 -> 15, of which waited for: 9 -> 9; matrix products, arithmetic and copies ran while one was open for 0% -> 0% of each run, Pallas kernels for 6% -> 7%
where the time goes in v3:
time: 59.7 us; the launch traced here: 59.5 us
  starting transfers between devices  25.8 us (43%)
  waiting for transfers between devices  20.3 us (34%)
  Pallas kernels  7.75 us (13%)
  local copies, waits for them, and re-layouts  5.44 us (9%)
    ppermute x15, starting transfers between devices, swap(): return lax.ppermute(value, 'ab', [(i, i ^ bits) for i in range(devices)])  25.8 us
    ppermute x15, waiting for transfers between devices, swap(): return lax.ppermute(value, 'ab', [(i, i ^ bits) for i in range(devices)])  20.3 us
    unnamed x8, local copies, waits for them, and re-layouts  5.31 us
    pallas_call x9, Pallas kernels, call(): pl.pallas_call(kernel, out_shape=outs, in_specs=[SCALARS] * scalars + [WH...  3.95 us
    pallas_call x1, Pallas kernels, masked_rows(): pl.pallas_call(mask_kernel, grid_spec=pltpu.PrefetchScalarGridSpec(num_sc...  3.8 us
  transfers between devices with their start and end apart: 15, of which 9 were waited for; matrix products, arithmetic and copies ran while one was open for 0% of the time, Pallas kernels for 7%

profile of v3, /device:TPU:0, one launch (start us, length us, event | category | flops | bytes accessed | tf_op | source)
XLA Modules:
  0.0 59.5 jit_solution(4102650853518470984)
XLA Ops:
  0.0 0.0 copy-start.1
  0.0 1.2 %copy-done.1 = bf16[16,32768]{1,0:T(8,128)(2,1)S(1)} copy-done((bf16[16,32768]{1,0:T(8,128)(2,1)S(1)}, bf16[16,32768]{1,0:T(8,128)(2,1)}, u32[]{:S(2)}) %copy-start.1) | copy-done | bytes 1048600
  1.2 0.1 sort.1
  1.3 0.5 collective-permute-start
  1.8 1.5 %collective-permute-done.got_ref = bf16[8,16,2048]{2,1,0:T(8,128)(2,1)S(1)} collective-permute-done((bf16[8,16,2048]{2,1,0:T(8,128)(2,1)S(1)}, bf16[8,16,2048]{2,1,0:T(8,128)(2,1)S(1)}, u32[]{:S(2)}, u32[]{:S(2)}) %collective-permute-start) | collective-permute-done | bytes 524320 | tf_op jit(solution)/shard_map/ppermute | solution.py:178
  3.4 0.1 pieces.1
  3.4 3.0 %collective-permute-start.1 = (bf16[32,2048]{1,0:T(8,128)(2,1)S(1)}, bf16[32,2048]{1,0:T(8,128)(2,1)S(1)}, u32[]{:S(2)}, u32[]{:S(2)}) collective-permute-start(bf16[32,2048]{1,0:T(8,128)(2,1)S(1)} %get-tuple-element.32), channel_id=1, source_target_pairs={{0,2},{1,3},{2,0},{3,1},{4,6},{5,7},{6,4},{7,5},{8,10},{9,11},{10,... | collective-permute-start | bytes 393224 | tf_op jit(solution)/shard_map/ppermute | solution.py:178
  6.4 1.6 %collective-permute-start.2 = (bf16[32,2048]{1,0:T(8,128)(2,1)S(1)}, bf16[32,2048]{1,0:T(8,128)(2,1)S(1)}, u32[]{:S(2)}, u32[]{:S(2)}) collective-permute-start(bf16[32,2048]{1,0:T(8,128)(2,1)S(1)} %get-tuple-element.33), channel_id=1, source_target_pairs={{0,4},{1,5},{2,6},{3,7},{4,0},{5,1},{6,2},{7,3},{8,12},{9,13},{10,... | collective-permute-start | bytes 393224 | tf_op jit(solution)/shard_map/ppermute | solution.py:178
  8.0 0.0 collective-permute-start.3
  8.0 3.0 %collective-permute-start.4 = (bf16[32,2048]{1,0:T(8,128)(2,1)S(1)}, bf16[32,2048]{1,0:T(8,128)(2,1)S(1)}, u32[]{:S(2)}, u32[]{:S(2)}) collective-permute-start(bf16[32,2048]{1,0:T(8,128)(2,1)S(1)} %get-tuple-element.35), channel_id=1, source_target_pairs={{0,8},{1,9},{2,10},{3,11},{4,12},{5,13},{6,14},{7,15},{8,0},{9,1},... | collective-permute-start | bytes 393224 | tf_op jit(solution)/shard_map/ppermute | solution.py:178
  10.9 1.3 %collective-permute-start.5 = (bf16[32,2048]{1,0:T(8,128)(2,1)S(1)}, bf16[32,2048]{1,0:T(8,128)(2,1)S(1)}, u32[]{:S(2)}, u32[]{:S(2)}) collective-permute-start(bf16[32,2048]{1,0:T(8,128)(2,1)S(1)} %get-tuple-element.36), channel_id=1, source_target_pairs={{0,10},{1,11},{2,8},{3,9},{4,14},{5,15},{6,12},{7,13},{8,2},{9,3},... | collective-permute-start | bytes 393224 | tf_op jit(solution)/shard_map/ppermute | solution.py:178
  12.2 0.0 collective-permute-done.1.refs_1_
  12.2 3.6 %collective-permute-start.6 = (bf16[32,2048]{1,0:T(8,128)(2,1)S(1)}, bf16[32,2048]{1,0:T(8,128)(2,1)S(1)}, u32[]{:S(2)}, u32[]{:S(2)}) collective-permute-start(bf16[32,2048]{1,0:T(8,128)(2,1)S(1)} %get-tuple-element.37), channel_id=1, source_target_pairs={{0,12},{1,13},{2,14},{3,15},{4,8},{5,9},{6,10},{7,11},{8,4},{9,5},... | collective-permute-start | bytes 393224 | tf_op jit(solution)/shard_map/ppermute | solution.py:178
  15.8 1.3 %collective-permute-done.2.refs_2_ = bf16[32,2048]{1,0:T(8,128)(2,1)S(1)} collective-permute-done((bf16[32,2048]{1,0:T(8,128)(2,1)S(1)}, bf16[32,2048]{1,0:T(8,128)(2,1)S(1)}, u32[]{:S(2)}, u32[]{:S(2)}) %collective-permute-start.2) | collective-permute-done | bytes 131104 | tf_op jit(solution)/shard_map/ppermute | solution.py:178
  17.1 0.7 %collective-permute-start.7 = (bf16[32,2048]{1,0:T(8,128)(2,1)S(1)}, bf16[32,2048]{1,0:T(8,128)(2,1)S(1)}, u32[]{:S(2)}, u32[]{:S(2)}) collective-permute-start(bf16[32,2048]{1,0:T(8,128)(2,1)S(1)} %get-tuple-element.38), channel_id=1, source_target_pairs={{0,14},{1,15},{2,12},{3,13},{4,10},{5,11},{6,8},{7,9},{8,6},{9,7},... | collective-permute-start | bytes 393224 | tf_op jit(solution)/shard_map/ppermute | solution.py:178
  17.8 0.0 copy-start
  17.9 3.4 %copy-done = bf16[2048,2048]{1,0:T(8,128)(2,1)S(1)} copy-done((bf16[2048,2048]{1,0:T(8,128)(2,1)S(1)}, bf16[2048,2048]{1,0:T(8,128)(2,1)}, u32[]{:S(2)}) %copy-start) | copy-done | bytes 8388632
  21.2 0.0 copy-start.2
  21.2 0.7 %copy-done.2 = s32[16,16]{1,0:T(8,128)S(1)} copy-done((s32[16,16]{1,0:T(8,128)S(1)}, s32[16,16]{1,0:T(8,128)}, u32[]{:S(2)}) %copy-start.2) | copy-done | bytes 1048
  21.9 3.8 %mask.1.masked_ref = bf16[2,8,128,2048]{3,2,1,0:T(8,128)(2,1)S(1)} custom-call(s32[1]{0:T(128)} %bitcast.1.me_ref, s32[16,16]{1,0:T(8,128)S(1)} %copy-done.2, bf16[2048,2048]{1,0:T(8,128)(2,1)S(1)} %copy-done), custom_call_target="tpu_custom_call" | custom-call | flops 4194304 | bytes 16777216 | tf_op jit(solution)/shard_map/mask/pallas_call | solution.py:73
  25.7 0.0 copy-start.3
  25.7 0.0 collective-permute-done.3.refs_3_
  25.8 0.0 collective-permute-done.4.refs_4_
  25.8 4.3 %collective-permute-done.5.refs_5_ = bf16[32,2048]{1,0:T(8,128)(2,1)S(1)} collective-permute-done((bf16[32,2048]{1,0:T(8,128)(2,1)S(1)}, bf16[32,2048]{1,0:T(8,128)(2,1)S(1)}, u32[]{:S(2)}, u32[]{:S(2)}) %collective-permute-start.5) | collective-permute-done | bytes 131104 | tf_op jit(solution)/shard_map/ppermute | solution.py:178
  30.1 0.0 collective-permute-done.6.refs_6_
  30.1 0.0 collective-permute-done.7.refs_7_
  30.1 2.4 %product.1 = (f32[8,128,256]{2,1,0:T(8,128)S(1)}, f32[8,128,256]{2,1,0:T(8,128)S(1)}) custom-call(s32[1]{0:T(128)} %bitcast.1.me_ref, bf16[2,8,128,2048]{3,2,1,0:T(8,128)(2,1)S(1)} %mask.1.masked_ref, bf16[32,2048]{1,0:T(8,128)(2,1)S(1)} %get-tuple-element.31.refs_0_, bf16[32,2048]{1,0:T(8,128)(2,1)S(1)} %collective-permute-done.1.refs_1_, ...), custom_call_target="tpu_custom_call" | custom-call | flops 2147483648 | bytes 11534340 | tf_op jit(solution)/shard_map/product/pallas_call | solution.py:25
  32.6 0.1 collective-permute-start.8
  32.6 2.6 %collective-permute-done.8.got_ref = f32[8,128,256]{2,1,0:T(8,128)S(1)} collective-permute-done((f32[8,128,256]{2,1,0:T(8,128)S(1)}, f32[8,128,256]{2,1,0:T(8,128)S(1)}, u32[]{:S(2)}, u32[]{:S(2)}) %collective-permute-start.8) | collective-permute-done | bytes 1048608 | tf_op jit(solution)/shard_map/ppermute | solution.py:178
  35.3 0.2 core_sum.1
  35.5 5.3 %collective-permute-start.12 = (s16[272,256]{1,0:T(8,128)(2,1)S(1)}, s16[272,256]{1,0:T(8,128)(2,1)S(1)}, u32[]{:S(2)}, u32[]{:S(2)}) collective-permute-start(s16[272,256]{1,0:T(8,128)(2,1)S(1)} %get-tuple-element.48), channel_id=1, source_target_pairs={{0,4},{1,5},{2,6},{3,7},{4,0},{5,1},{6,2},{7,3},{8,12},{9,13},{10,... | collective-permute-start | bytes 417800 | tf_op jit(solution)/shard_map/ppermute | solution.py:178
  40.8 0.7 %collective-permute-start.9 = (s16[272,256]{1,0:T(8,128)(2,1)S(1)}, s16[272,256]{1,0:T(8,128)(2,1)S(1)}, u32[]{:S(2)}, u32[]{:S(2)}) collective-permute-start(s16[272,256]{1,0:T(8,128)(2,1)S(1)} %get-tuple-element.42), channel_id=1, source_target_pairs={{0,2},{1,3},{2,0},{3,1},{4,6},{5,7},{6,4},{7,5},{8,10},{9,11},{10,... | collective-permute-start | bytes 417800 | tf_op jit(solution)/shard_map/ppermute | solution.py:178
  41.5 3.3 %collective-permute-done.12.got_ref = s16[272,256]{1,0:T(8,128)(2,1)S(1)} collective-permute-done((s16[272,256]{1,0:T(8,128)(2,1)S(1)}, s16[272,256]{1,0:T(8,128)(2,1)S(1)}, u32[]{:S(2)}, u32[]{:S(2)}) %collective-permute-start.12) | collective-permute-done | bytes 139296 | tf_op jit(solution)/shard_map/ppermute | solution.py:178
  44.8 0.1 halve.6
  44.9 3.7 %collective-permute-start.13 = (s16[144,256]{1,0:T(8,128)(2,1)S(1)}, s16[144,256]{1,0:T(8,128)(2,1)S(1)}, u32[]{:S(2)}, u32[]{:S(2)}) collective-permute-start(s16[144,256]{1,0:T(8,128)(2,1)S(1)} %get-tuple-element.50), channel_id=1, source_target_pairs={{0,8},{1,9},{2,10},{3,11},{4,12},{5,13},{6,14},{7,15},{8,0},{9,1},... | collective-permute-start | bytes 221192 | tf_op jit(solution)/shard_map/ppermute | solution.py:178
  48.6 0.0 collective-permute-done.9.got_ref
  48.6 0.1 halve.4
  48.6 0.4 collective-permute-start.10
  49.0 2.9 %collective-permute-done.13.got_ref = s16[144,256]{1,0:T(8,128)(2,1)S(1)} collective-permute-done((s16[144,256]{1,0:T(8,128)(2,1)S(1)}, s16[144,256]{1,0:T(8,128)(2,1)S(1)}, u32[]{:S(2)}, u32[]{:S(2)}) %collective-permute-start.13) | collective-permute-done | bytes 73760 | tf_op jit(solution)/shard_map/ppermute | solution.py:178
  51.9 0.6 %collective-permute-start.14 = (s16[80,256]{1,0:T(8,128)(2,1)S(1)}, s16[80,256]{1,0:T(8,128)(2,1)S(1)}, u32[]{:S(2)}, u32[]{:S(2)}) collective-permute-start(s16[80,256]{1,0:T(8,128)(2,1)S(1)} %get-tuple-element.52), channel_id=1, source_target_pairs={{0,2},{1,3},{2,0},{3,1},{4,6},{5,7},{6,4},{7,5},{8,10},{9,11},{10,... | collective-permute-start | bytes 122888 | tf_op jit(solution)/shard_map/ppermute | solution.py:178
  52.5 0.5 collective-permute-done.10.got_ref
  53.1 1.5 %collective-permute-start.11 = (s16[80,256]{1,0:T(8,128)(2,1)S(1)}, s16[80,256]{1,0:T(8,128)(2,1)S(1)}, u32[]{:S(2)}, u32[]{:S(2)}) collective-permute-start(s16[80,256]{1,0:T(8,128)(2,1)S(1)} %get-tuple-element.46), channel_id=1, source_target_pairs={{0,8},{1,9},{2,10},{3,11},{4,12},{5,13},{6,14},{7,15},{8,0},{9,1},... | collective-permute-start | bytes 122888 | tf_op jit(solution)/shard_map/ppermute | solution.py:178
  54.6 0.0 copy-done.3
  54.6 0.1 copy.5.place_ref
  54.7 1.3 %collective-permute-done.14.refs_3_ = s16[80,256]{1,0:T(8,128)(2,1)S(1)} collective-permute-done((s16[80,256]{1,0:T(8,128)(2,1)S(1)}, s16[80,256]{1,0:T(8,128)(2,1)S(1)}, u32[]{:S(2)}, u32[]{:S(2)}) %collective-permute-start.14) | collective-permute-done | bytes 40992 | tf_op jit(solution)/shard_map/ppermute | solution.py:178
  56.0 2.5 %collective-permute-done.11.refs_1_ = s16[80,256]{1,0:T(8,128)(2,1)S(1)} collective-permute-done((s16[80,256]{1,0:T(8,128)(2,1)S(1)}, s16[80,256]{1,0:T(8,128)(2,1)S(1)}, u32[]{:S(2)}, u32[]{:S(2)}) %collective-permute-start.11) | collective-permute-done | bytes 40992 | tf_op jit(solution)/shard_map/ppermute | solution.py:178
  58.5 0.9 %last.1 = f32[128,256]{1,0:T(8,128)} custom-call(s32[256,1]{1,0:T(8,128)S(1)} %copy.5.place_ref, f32[1,64,256]{2,1,0:T(8,128)S(1)} %get-tuple-element.45.refs_0_, s16[80,256]{1,0:T(8,128)(2,1)S(1)} %collective-permute-done.11.refs_1_, f32[1,64,256]{2,1,0:T(8,128)S(1)} %get-tuple-element.51.refs_2_, s16[80,256]{1,0:T(8,128)(2,1)S(1)} %collective-permute-done.14.refs_3_), custom_call_target="tpu_custom_call" | custom-call | bytes 345088 | tf_op jit(solution)/shard_map/last/pallas_call | solution.py:25
  (2 shorter events, 0.1 us)
Async XLA Ops:
  0.0 1.2 %copy-start.1 = (bf16[16,32768]{1,0:T(8,128)(2,1)S(1)}, bf16[16,32768]{1,0:T(8,128)(2,1)}, u32[]{:S(2)}) copy-start(bf16[16,32768]{1,0:T(8,128)(2,1)} %amplitudes_ref.1) | copy-start | bytes 3145732
  1.3 2.1 %collective-permute-start = (bf16[8,16,2048]{2,1,0:T(8,128)(2,1)S(1)}, bf16[8,16,2048]{2,1,0:T(8,128)(2,1)S(1)}, u32[]{:S(2)}, u32[]{:S(2)}) collective-permute-start(bf16[8,16,2048]{2,1,0:T(8,128)(2,1)S(1)} %get-tuple-element.30), channel_id=1, source_target_pairs={{0,1},{1,0},{2,3},{3,2},{4,5},{5,4},{6,7},{7,6},{8,9},{9,8},{10,11... | collective-permute-start | bytes 1572872 | tf_op jit(solution)/shard_map/ppermute | solution.py:178
  3.4 8.8 %collective-permute-start.1 = (bf16[32,2048]{1,0:T(8,128)(2,1)S(1)}, bf16[32,2048]{1,0:T(8,128)(2,1)S(1)}, u32[]{:S(2)}, u32[]{:S(2)}) collective-permute-start(bf16[32,2048]{1,0:T(8,128)(2,1)S(1)} %get-tuple-element.32), channel_id=1, source_target_pairs={{0,2},{1,3},{2,0},{3,1},{4,6},{5,7},{6,4},{7,5},{8,10},{9,11},{10,... | collective-permute-start | bytes 393224 | tf_op jit(solution)/shard_map/ppermute | solution.py:178
  6.4 10.8 %collective-permute-start.2 = (bf16[32,2048]{1,0:T(8,128)(2,1)S(1)}, bf16[32,2048]{1,0:T(8,128)(2,1)S(1)}, u32[]{:S(2)}, u32[]{:S(2)}) collective-permute-start(bf16[32,2048]{1,0:T(8,128)(2,1)S(1)} %get-tuple-element.33), channel_id=1, source_target_pairs={{0,4},{1,5},{2,6},{3,7},{4,0},{5,1},{6,2},{7,3},{8,12},{9,13},{10,... | collective-permute-start | bytes 393224 | tf_op jit(solution)/shard_map/ppermute | solution.py:178
  8.0 17.8 %collective-permute-start.3 = (bf16[32,2048]{1,0:T(8,128)(2,1)S(1)}, bf16[32,2048]{1,0:T(8,128)(2,1)S(1)}, u32[]{:S(2)}, u32[]{:S(2)}) collective-permute-start(bf16[32,2048]{1,0:T(8,128)(2,1)S(1)} %get-tuple-element.34), channel_id=1, source_target_pairs={{0,6},{1,7},{2,4},{3,5},{4,2},{5,3},{6,0},{7,1},{8,14},{9,15},{10,... | collective-permute-start | bytes 393224 | tf_op jit(solution)/shard_map/ppermute | solution.py:178
  8.0 17.8 %collective-permute-start.4 = (bf16[32,2048]{1,0:T(8,128)(2,1)S(1)}, bf16[32,2048]{1,0:T(8,128)(2,1)S(1)}, u32[]{:S(2)}, u32[]{:S(2)}) collective-permute-start(bf16[32,2048]{1,0:T(8,128)(2,1)S(1)} %get-tuple-element.35), channel_id=1, source_target_pairs={{0,8},{1,9},{2,10},{3,11},{4,12},{5,13},{6,14},{7,15},{8,0},{9,1},... | collective-permute-start | bytes 393224 | tf_op jit(solution)/shard_map/ppermute | solution.py:178
  10.9 19.2 %collective-permute-start.5 = (bf16[32,2048]{1,0:T(8,128)(2,1)S(1)}, bf16[32,2048]{1,0:T(8,128)(2,1)S(1)}, u32[]{:S(2)}, u32[]{:S(2)}) collective-permute-start(bf16[32,2048]{1,0:T(8,128)(2,1)S(1)} %get-tuple-element.36), channel_id=1, source_target_pairs={{0,10},{1,11},{2,8},{3,9},{4,14},{5,15},{6,12},{7,13},{8,2},{9,3},... | collective-permute-start | bytes 393224 | tf_op jit(solution)/shard_map/ppermute | solution.py:178
  12.2 17.9 %collective-permute-start.6 = (bf16[32,2048]{1,0:T(8,128)(2,1)S(1)}, bf16[32,2048]{1,0:T(8,128)(2,1)S(1)}, u32[]{:S(2)}, u32[]{:S(2)}) collective-permute-start(bf16[32,2048]{1,0:T(8,128)(2,1)S(1)} %get-tuple-element.37), channel_id=1, source_target_pairs={{0,12},{1,13},{2,14},{3,15},{4,8},{5,9},{6,10},{7,11},{8,4},{9,5},... | collective-permute-start | bytes 393224 | tf_op jit(solution)/shard_map/ppermute | solution.py:178
  17.1 13.0 %collective-permute-start.7 = (bf16[32,2048]{1,0:T(8,128)(2,1)S(1)}, bf16[32,2048]{1,0:T(8,128)(2,1)S(1)}, u32[]{:S(2)}, u32[]{:S(2)}) collective-permute-start(bf16[32,2048]{1,0:T(8,128)(2,1)S(1)} %get-tuple-element.38), channel_id=1, source_target_pairs={{0,14},{1,15},{2,12},{3,13},{4,10},{5,11},{6,8},{7,9},{8,6},{9,7},... | collective-permute-start | bytes 393224 | tf_op jit(solution)/shard_map/ppermute | solution.py:178
  17.8 3.4 %copy-start = (bf16[2048,2048]{1,0:T(8,128)(2,1)S(1)}, bf16[2048,2048]{1,0:T(8,128)(2,1)}, u32[]{:S(2)}) copy-start(bf16[2048,2048]{1,0:T(8,128)(2,1)} %rows_ref.1) | copy-start | bytes 25165828
  21.2 0.7 %copy-start.2 = (s32[16,16]{1,0:T(8,128)S(1)}, s32[16,16]{1,0:T(8,128)}, u32[]{:S(2)}) copy-start(s32[16,16]{1,0:T(8,128)} %mask_ref.1) | copy-start | bytes 3076
  25.7 28.9 %copy-start.3 = (s32[256]{0:T(256)S(1)}, s32[256]{0:T(256)}, u32[]{:S(2)}) copy-start(s32[256]{0:T(256)} %param.7) | copy-start | bytes 3076
  32.6 2.7 %collective-permute-start.8 = (f32[8,128,256]{2,1,0:T(8,128)S(1)}, f32[8,128,256]{2,1,0:T(8,128)S(1)}, u32[]{:S(2)}, u32[]{:S(2)}) collective-permute-start(f32[8,128,256]{2,1,0:T(8,128)S(1)} %get-tuple-element.40), channel_id=1, source_target_pairs={{0,1},{1,0},{2,3},{3,2},{4,5},{5,4},{6,7},{7,6},{8,9},{9,8},{10,11... | collective-permute-start | bytes 3145736 | tf_op jit(solution)/shard_map/ppermute | solution.py:178
  35.5 9.3 %collective-permute-start.12 = (s16[272,256]{1,0:T(8,128)(2,1)S(1)}, s16[272,256]{1,0:T(8,128)(2,1)S(1)}, u32[]{:S(2)}, u32[]{:S(2)}) collective-permute-start(s16[272,256]{1,0:T(8,128)(2,1)S(1)} %get-tuple-element.48), channel_id=1, source_target_pairs={{0,4},{1,5},{2,6},{3,7},{4,0},{5,1},{6,2},{7,3},{8,12},{9,13},{10,... | collective-permute-start | bytes 417800 | tf_op jit(solution)/shard_map/ppermute | solution.py:178
  40.8 7.7 %collective-permute-start.9 = (s16[272,256]{1,0:T(8,128)(2,1)S(1)}, s16[272,256]{1,0:T(8,128)(2,1)S(1)}, u32[]{:S(2)}, u32[]{:S(2)}) collective-permute-start(s16[272,256]{1,0:T(8,128)(2,1)S(1)} %get-tuple-element.42), channel_id=1, source_target_pairs={{0,2},{1,3},{2,0},{3,1},{4,6},{5,7},{6,4},{7,5},{8,10},{9,11},{10,... | collective-permute-start | bytes 417800 | tf_op jit(solution)/shard_map/ppermute | solution.py:178
  44.9 7.0 %collective-permute-start.13 = (s16[144,256]{1,0:T(8,128)(2,1)S(1)}, s16[144,256]{1,0:T(8,128)(2,1)S(1)}, u32[]{:S(2)}, u32[]{:S(2)}) collective-permute-start(s16[144,256]{1,0:T(8,128)(2,1)S(1)} %get-tuple-element.50), channel_id=1, source_target_pairs={{0,8},{1,9},{2,10},{3,11},{4,12},{5,13},{6,14},{7,15},{8,0},{9,1},... | collective-permute-start | bytes 221192 | tf_op jit(solution)/shard_map/ppermute | solution.py:178
  48.6 4.4 %collective-permute-start.10 = (s16[144,256]{1,0:T(8,128)(2,1)S(1)}, s16[144,256]{1,0:T(8,128)(2,1)S(1)}, u32[]{:S(2)}, u32[]{:S(2)}) collective-permute-start(s16[144,256]{1,0:T(8,128)(2,1)S(1)} %get-tuple-element.44), channel_id=1, source_target_pairs={{0,4},{1,5},{2,6},{3,7},{4,0},{5,1},{6,2},{7,3},{8,12},{9,13},{10,... | collective-permute-start | bytes 221192 | tf_op jit(solution)/shard_map/ppermute | solution.py:178
  51.9 4.1 %collective-permute-start.14 = (s16[80,256]{1,0:T(8,128)(2,1)S(1)}, s16[80,256]{1,0:T(8,128)(2,1)S(1)}, u32[]{:S(2)}, u32[]{:S(2)}) collective-permute-start(s16[80,256]{1,0:T(8,128)(2,1)S(1)} %get-tuple-element.52), channel_id=1, source_target_pairs={{0,2},{1,3},{2,0},{3,1},{4,6},{5,7},{6,4},{7,5},{8,10},{9,11},{10,... | collective-permute-start | bytes 122888 | tf_op jit(solution)/shard_map/ppermute | solution.py:178
  53.1 5.4 %collective-permute-start.11 = (s16[80,256]{1,0:T(8,128)(2,1)S(1)}, s16[80,256]{1,0:T(8,128)(2,1)S(1)}, u32[]{:S(2)}, u32[]{:S(2)}) collective-permute-start(s16[80,256]{1,0:T(8,128)(2,1)S(1)} %get-tuple-element.46), channel_id=1, source_target_pairs={{0,8},{1,9},{2,10},{3,11},{4,12},{5,13},{6,14},{7,15},{8,0},{9,1},... | collective-permute-start | bytes 122888 | tf_op jit(solution)/shard_map/ppermute | solution.py:178

commit v4 on v3

--- a/solution.py
+++ b/solution.py
@@ -8,12 +8,11 @@
 from jax.sharding import PartitionSpec as P
 
 TILE = 128
-WIRE = jnp.int16
 EXTRA = 16
 
 
-def STREAMS(bits):
-    return [(0, TILE // 2, bits), (TILE // 2, TILE, bits[1:] + bits[:1])]
+def sending(chips):
+    return [chips - 1] + list(range(1, chips // 2)) + list(reversed(range(chips // 2, chips - 1)))
 
 
 WHOLE = pl.BlockSpec(memory_space=pltpu.VMEM)
@@ -88,7 +87,7 @@
 def product_kernel(me_ref, masked_ref, *refs):
     *pieces, send_ref, keep_ref, all_ref = refs
     mine, depth = pieces[0].shape
-    chip = me_ref[0] // 2
+    chip = me_ref[0] // 2 % len(pieces)
     for k, piece in enumerate(pieces):
         all_ref[pl.ds(pl.multiple_of((chip ^ k) * mine, mine), mine), :] = piece[...]
     for slot, out_ref in enumerate((send_ref, keep_ref)):
@@ -104,10 +103,6 @@
 
 def pack(values, out_ref):
     rows = values[0].shape[0]
-    if out_ref.dtype == jnp.float32:
-        for i, value in enumerate(values):
-            out_ref[i * rows : (i + 1) * rows] = value
-        return
     largest = functools.reduce(jnp.maximum, [jnp.max(jnp.abs(v), axis=0, keepdims=True) for v in values])
     exponent = jnp.ceil(jnp.log2(jnp.maximum(largest, 2.0**-110)) + 0.01)
     factor = jnp.exp2(15.0 - exponent)
@@ -117,53 +112,64 @@
     out_ref[len(values) * rows :] = jnp.broadcast_to(exponent, last).astype(jnp.int32).astype(jnp.int16)
 
 
-def unpack(got_ref, rows):
-    if got_ref.dtype == jnp.float32:
-        return [got_ref[i : i + rows] for i in range(0, got_ref.shape[0], rows)]
+def unpack(got_ref):
     stop = got_ref.shape[0] - EXTRA
     exponent = got_ref[stop:].astype(jnp.int32).astype(jnp.float32)[:1]
     step = jnp.exp2(exponent - 15.0)
-    return [got_ref[i : i + rows].astype(jnp.int32).astype(jnp.float32) * step for i in range(0, stop, rows)]
-
-
-def packed(blocks, rows, columns):
-    if WIRE == jnp.float32:
-        return jax.ShapeDtypeStruct((blocks * rows, columns), WIRE)
-    return jax.ShapeDtypeStruct((blocks * rows + EXTRA, columns), WIRE)
-
-
-def first_kernel(streams, keep_ref, got_ref, *outs):
-    for (start, stop, bits), send, keep in zip(streams, outs[::2], outs[1::2], strict=True):
-        half = keep.shape[0]
-        sums = []
-        for index in range(2 * half):
-            k = chip_of(index, bits)
-            sums.append(keep_ref[k, start:stop] + got_ref[k, start:stop])
-        for index in range(half):
-            keep[index] = sums[index]
-        pack(sums[half:], send)
+    return [got_ref[i : i + TILE].astype(jnp.int32).astype(jnp.float32) * step for i in range(0, stop, TILE)]
+
+
+def packed(blocks, columns):
+    return jax.ShapeDtypeStruct((blocks * TILE + EXTRA, columns), jnp.int16)
+
+
+def plain(blocks, columns):
+    return jax.ShapeDtypeStruct((blocks, TILE, columns), jnp.float32)
+
+
+def first_kernel(bits, keep_ref, got_ref, send, keep):
+    half = keep.shape[0]
+    sums = []
+    for index in range(2 * half):
+        k = chip_of(index, bits)
+        sums.append(keep_ref[k] + got_ref[k])
+    for index in range(half):
+        keep[index] = sums[index]
+    pack(sums[half:], send)
 
 
 def halve_kernel(keep_ref, got_ref, send, keep):
     half = keep.shape[0]
-    got = unpack(got_ref, keep.shape[1])
+    got = unpack(got_ref)
     for index in range(half):
         keep[index] = keep_ref[index] + got[index]
     pack([keep_ref[index] + got[index] for index in range(half, 2 * half)], send)
 
 
-def last_kernel(count, place_ref, *refs):
-    *sums, out_ref = refs
-    parts = [sums[2 * i][0] + unpack(sums[2 * i + 1], sums[2 * i].shape[1])[0] for i in range(count)]
-    rest = jnp.concatenate(parts, axis=0) if count > 1 else parts[0]
-    columns = lax.broadcasted_iota(jnp.int32, (rest.shape[1], out_ref.shape[1]), 1)
-    chosen = (place_ref[...] == columns).astype(jnp.float32).astype(jnp.bfloat16)
+def join_kernel(near_keep, near_got, far_keep, far_got, send, keep):
+    both = []
+    for c, (kept, got) in enumerate(((near_keep, near_got), (far_keep, far_got))):
+        mine, theirs = unpack(got)
+        keep[c] = kept[0] + mine
+        both.append(kept[1] + theirs)
+    pack([jnp.concatenate(both, axis=1)], send)
+
+
+def last_kernel(half, me_ref, keep_ref, got_ref, places_ref, out_ref):
+    pairs = keep_ref.shape[2]
+    high = (me_ref[0] >= half).astype(jnp.int32)
+    got = unpack(got_ref)[0]
     total = None
-    for _ in range(3):
-        part = rest.astype(jnp.bfloat16)
-        rest = rest - part.astype(jnp.float32)
-        moved = jnp.dot(part, chosen, preferred_element_type=jnp.float32)
-        total = moved if total is None else total + moved
+    for c in range(2):
+        rest = keep_ref[c] + got[:, (1 - c) * pairs : (2 - c) * pairs]
+        place = jnp.where(high == c, places_ref[:pairs], places_ref[pairs:])
+        columns = lax.broadcasted_iota(jnp.int32, (pairs, out_ref.shape[1]), 1)
+        chosen = (place == columns).astype(jnp.float32).astype(jnp.bfloat16)
+        for _ in range(3):
+            part = rest.astype(jnp.bfloat16)
+            rest = rest - part.astype(jnp.float32)
+            moved = jnp.dot(part, chosen, preferred_element_type=jnp.float32)
+            total = moved if total is None else total + moved
     out_ref[...] = total
 
 
@@ -171,7 +177,7 @@
     me = lax.axis_index("ab").reshape(1)
     chips = devices // 2
     mine, depth = amplitudes.shape[0], integrals.shape[1]
-    pairs = mine * devices
+    pairs = mine * chips
     kind = amplitudes.dtype
 
     def swap(value, bits):
@@ -182,37 +188,36 @@
     got = swap(send, 1)
     piece = jax.ShapeDtypeStruct((2 * mine, depth), kind)
     pieces = call(piece_kernel, "pieces", [piece] * chips, me, keep, got, scalars=1)
+    received = {0: pieces[0]}
+    for k in sending(chips):
+        received[k] = swap(pieces[k], 2 * k)
     masked = masked_rows(me, block_mask, integrals)
-    received = [pieces[0]] + [None] * (chips - 1)
-    for k in reversed(range(1, chips)):
-        received[k] = swap(pieces[k], 2 * k)
-
-    partial = jax.ShapeDtypeStruct((chips, TILE, pairs), jnp.float32)
-    send, keep = call(
-        product_kernel, "product", [partial] * 2, me, masked, *received, scalars=1,
-        scratch=[pltpu.VMEM((pairs, depth), kind)], flops=4 * chips * TILE * depth * pairs,
-    )
-    got = swap(send, 1)
-
+
+    half = chips // 2
     bits = tuple(range((chips - 1).bit_length()))
-    streams = STREAMS(bits)
-    outs = []
-    for start, stop, _ in streams:
-        outs += [packed(chips // 2, stop - start, pairs), jax.ShapeDtypeStruct((chips // 2, stop - start, pairs), jnp.float32)]
-    state = call(functools.partial(first_kernel, streams), "core_sum", outs, keep, got)
     sums = []
-    for s, (start, stop, order) in enumerate(streams):
-        send, keep = state[2 * s : 2 * s + 2]
-        for step, bit in enumerate(order):
+    for first in (0, half):
+        send, keep = call(
+            product_kernel, "product", [plain(chips, pairs)] * 2, me, masked,
+            *[received[k] for k in range(first, first + half)], scalars=1,
+            scratch=[pltpu.VMEM((pairs, depth), kind)], flops=4 * chips * TILE * depth * pairs,
+        )
+        got = swap(send, 1)
+        blocks = half
+        send, keep = call(
+            functools.partial(first_kernel, bits), "core_sum", [packed(blocks, pairs), plain(blocks, pairs)], keep, got
+        )
+        for bit in bits[:-1]:
             got = swap(send, 2 << bit)
-            if step < len(order) - 1:
-                half = keep.shape[0] // 2
-                outs = [packed(half, stop - start, pairs), jax.ShapeDtypeStruct((half, stop - start, pairs), jnp.float32)]
-                send, keep = call(halve_kernel, "halve", outs, keep, got)
+            if bit < bits[-2]:
+                blocks //= 2
+                send, keep = call(halve_kernel, "halve", [packed(blocks, pairs), plain(blocks, pairs)], keep, got)
         sums += [keep, got]
+    send, keep = call(join_kernel, "join", [packed(1, 2 * pairs), plain(2, pairs)], *sums)
+    got = swap(send, 2 << bits[-1])
     return call(
-        functools.partial(last_kernel, len(streams)), "last",
-        [jax.ShapeDtypeStruct((TILE, pairs), jnp.float32)], pair_list.reshape(-1, 1), *sums,
+        functools.partial(last_kernel, chips), "last", [jax.ShapeDtypeStruct((TILE, 2 * pairs), jnp.float32)],
+        me, keep, got, pair_list.reshape(-1, 1), scalars=1,
     )[0]
 
 

time: 59.7 us -> 57.7 us (0.966)
  waiting for transfers between devices: 20.3 us -> 13.1 us
  starting transfers between devices: 25.8 us -> 28.7 us
  Pallas kernels: 7.75 us -> 10.1 us
    ppermute x15, waiting for transfers between devices: 20.3 us -> 13.1 us  [swap(): return lax.ppermute(value, 'ab', [(i, i ^ bits) for i in range(devices)])]
    ppermute x15, starting transfers between devices: 25.8 us -> 28.7 us  [swap(): return lax.ppermute(value, 'ab', [(i, i ^ bits) for i in range(devices)])]
    pallas_call x9 -> x10, Pallas kernels: 3.95 us -> 6.31 us  [call(): pl.pallas_call(kernel, out_shape=outs, in_specs=[SCALARS] * scalars + [WH...]
  transfers between devices with their start and end apart: 15 -> 15, of which waited for: 9 -> 6; matrix products, arithmetic and copies ran while one was open for 0% -> 0% of each run, Pallas kernels for 7% -> 15%
where the time goes in v4:
time: 57.7 us; the launch traced here: 57.5 us
  starting transfers between devices  28.7 us (50%)
  waiting for transfers between devices  13.1 us (23%)
  Pallas kernels  10.1 us (18%)
  local copies, waits for them, and re-layouts  5.44 us (9%)
    ppermute x15, starting transfers between devices, swap(): return lax.ppermute(value, 'ab', [(i, i ^ bits) for i in range(devices)])  28.7 us
    ppermute x15, waiting for transfers between devices, swap(): return lax.ppermute(value, 'ab', [(i, i ^ bits) for i in range(devices)])  13.1 us
    pallas_call x10, Pallas kernels, call(): pl.pallas_call(kernel, out_shape=outs, in_specs=[SCALARS] * scalars + [WH...  6.31 us
    unnamed x8, local copies, waits for them, and re-layouts  5.31 us
    pallas_call x1, Pallas kernels, masked_rows(): pl.pallas_call(mask_kernel, grid_spec=pltpu.PrefetchScalarGridSpec(num_sc...  3.8 us
  transfers between devices with their start and end apart: 15, of which 6 were waited for; matrix products, arithmetic and copies ran while one was open for 0% of the time, Pallas kernels for 15%

profile of v4, /device:TPU:0, one launch (start us, length us, event | category | flops | bytes accessed | tf_op | source)
XLA Modules:
  0.0 57.5 jit_solution(10352837633210469641)
XLA Ops:
  0.0 0.0 copy-start.1
  0.0 1.2 %copy-done.1 = bf16[16,32768]{1,0:T(8,128)(2,1)S(1)} copy-done((bf16[16,32768]{1,0:T(8,128)(2,1)S(1)}, bf16[16,32768]{1,0:T(8,128)(2,1)}, u32[]{:S(2)}) %copy-start.1) | copy-done | bytes 1048600
  1.2 0.1 sort.1
  1.3 0.5 collective-permute-start
  1.8 1.5 %collective-permute-done.got_ref = bf16[8,16,2048]{2,1,0:T(8,128)(2,1)S(1)} collective-permute-done((bf16[8,16,2048]{2,1,0:T(8,128)(2,1)S(1)}, bf16[8,16,2048]{2,1,0:T(8,128)(2,1)S(1)}, u32[]{:S(2)}, u32[]{:S(2)}) %collective-permute-start) | collective-permute-done | bytes 524320 | tf_op jit(solution)/shard_map/ppermute | solution.py:184
  3.4 0.1 pieces.1
  3.4 3.0 %collective-permute-start.1 = (bf16[32,2048]{1,0:T(8,128)(2,1)S(1)}, bf16[32,2048]{1,0:T(8,128)(2,1)S(1)}, u32[]{:S(2)}, u32[]{:S(2)}) collective-permute-start(bf16[32,2048]{1,0:T(8,128)(2,1)S(1)} %get-tuple-element.32), channel_id=1, source_target_pairs={{0,2},{1,3},{2,0},{3,1},{4,6},{5,7},{6,4},{7,5},{8,10},{9,11},{10,... | collective-permute-start | bytes 393224 | tf_op jit(solution)/shard_map/ppermute | solution.py:184
  6.4 1.6 %collective-permute-start.2 = (bf16[32,2048]{1,0:T(8,128)(2,1)S(1)}, bf16[32,2048]{1,0:T(8,128)(2,1)S(1)}, u32[]{:S(2)}, u32[]{:S(2)}) collective-permute-start(bf16[32,2048]{1,0:T(8,128)(2,1)S(1)} %get-tuple-element.33), channel_id=1, source_target_pairs={{0,4},{1,5},{2,6},{3,7},{4,0},{5,1},{6,2},{7,3},{8,12},{9,13},{10,... | collective-permute-start | bytes 393224 | tf_op jit(solution)/shard_map/ppermute | solution.py:184
  8.0 0.0 collective-permute-start.3
  8.0 3.0 %collective-permute-start.7 = (bf16[32,2048]{1,0:T(8,128)(2,1)S(1)}, bf16[32,2048]{1,0:T(8,128)(2,1)S(1)}, u32[]{:S(2)}, u32[]{:S(2)}) collective-permute-start(bf16[32,2048]{1,0:T(8,128)(2,1)S(1)} %get-tuple-element.41), channel_id=1, source_target_pairs={{0,8},{1,9},{2,10},{3,11},{4,12},{5,13},{6,14},{7,15},{8,0},{9,1},... | collective-permute-start | bytes 393224 | tf_op jit(solution)/shard_map/ppermute | solution.py:184
  10.9 1.3 %collective-permute-start.8 = (bf16[32,2048]{1,0:T(8,128)(2,1)S(1)}, bf16[32,2048]{1,0:T(8,128)(2,1)S(1)}, u32[]{:S(2)}, u32[]{:S(2)}) collective-permute-start(bf16[32,2048]{1,0:T(8,128)(2,1)S(1)} %get-tuple-element.42), channel_id=1, source_target_pairs={{0,10},{1,11},{2,8},{3,9},{4,14},{5,15},{6,12},{7,13},{8,2},{9,3},... | collective-permute-start | bytes 393224 | tf_op jit(solution)/shard_map/ppermute | solution.py:184
  12.2 0.0 collective-permute-done.1.refs_1_
  12.2 3.6 %collective-permute-start.9 = (bf16[32,2048]{1,0:T(8,128)(2,1)S(1)}, bf16[32,2048]{1,0:T(8,128)(2,1)S(1)}, u32[]{:S(2)}, u32[]{:S(2)}) collective-permute-start(bf16[32,2048]{1,0:T(8,128)(2,1)S(1)} %get-tuple-element.43), channel_id=1, source_target_pairs={{0,12},{1,13},{2,14},{3,15},{4,8},{5,9},{6,10},{7,11},{8,4},{9,5},... | collective-permute-start | bytes 393224 | tf_op jit(solution)/shard_map/ppermute | solution.py:184
  15.8 1.3 %collective-permute-done.2.refs_2_ = bf16[32,2048]{1,0:T(8,128)(2,1)S(1)} collective-permute-done((bf16[32,2048]{1,0:T(8,128)(2,1)S(1)}, bf16[32,2048]{1,0:T(8,128)(2,1)S(1)}, u32[]{:S(2)}, u32[]{:S(2)}) %collective-permute-start.2) | collective-permute-done | bytes 131104 | tf_op jit(solution)/shard_map/ppermute | solution.py:184
  17.1 0.7 %collective-permute-start.10 = (bf16[32,2048]{1,0:T(8,128)(2,1)S(1)}, bf16[32,2048]{1,0:T(8,128)(2,1)S(1)}, u32[]{:S(2)}, u32[]{:S(2)}) collective-permute-start(bf16[32,2048]{1,0:T(8,128)(2,1)S(1)} %get-tuple-element.44), channel_id=1, source_target_pairs={{0,14},{1,15},{2,12},{3,13},{4,10},{5,11},{6,8},{7,9},{8,6},{9,7},... | collective-permute-start | bytes 393224 | tf_op jit(solution)/shard_map/ppermute | solution.py:184
  17.9 3.4 %copy-done = bf16[2048,2048]{1,0:T(8,128)(2,1)S(1)} copy-done((bf16[2048,2048]{1,0:T(8,128)(2,1)S(1)}, bf16[2048,2048]{1,0:T(8,128)(2,1)}, u32[]{:S(2)}) %copy-start) | copy-done | bytes 8388632
  21.2 0.7 %copy-done.2 = s32[16,16]{1,0:T(8,128)S(1)} copy-done((s32[16,16]{1,0:T(8,128)S(1)}, s32[16,16]{1,0:T(8,128)}, u32[]{:S(2)}) %copy-start.2) | copy-done | bytes 1048
  21.9 3.8 %mask.1.masked_ref = bf16[2,8,128,2048]{3,2,1,0:T(8,128)(2,1)S(1)} custom-call(s32[1]{0:T(128)} %bitcast.me_ref, s32[16,16]{1,0:T(8,128)S(1)} %copy-done.2, bf16[2048,2048]{1,0:T(8,128)(2,1)S(1)} %copy-done), custom_call_target="tpu_custom_call" | custom-call | flops 4194304 | bytes 16777216 | tf_op jit(solution)/shard_map/mask/pallas_call | solution.py:72
  25.7 0.0 collective-permute-done.3.refs_3_
  25.7 0.0 copy-start.3
  25.8 2.4 %product.2 = (f32[8,128,128]{2,1,0:T(8,128)S(1)}, f32[8,128,128]{2,1,0:T(8,128)S(1)}) custom-call(s32[1]{0:T(128)} %bitcast.me_ref, bf16[2,8,128,2048]{3,2,1,0:T(8,128)(2,1)S(1)} %mask.1.masked_ref, bf16[32,2048]{1,0:T(8,128)(2,1)S(1)} %get-tuple-element.31.refs_0_, bf16[32,2048]{1,0:T(8,128)(2,1)S(1)} %collective-permute-done.1.refs_1_, ...), custom_call_target="tpu_custom_call" | custom-call | flops 1073741824 | bytes 9961476 | tf_op jit(solution)/shard_map/product/pallas_call | solution.py:24
  28.1 0.1 collective-permute-start.4
  28.2 0.0 collective-permute-done.7.refs_0_
  28.2 1.9 %collective-permute-done.8.refs_1_ = bf16[32,2048]{1,0:T(8,128)(2,1)S(1)} collective-permute-done((bf16[32,2048]{1,0:T(8,128)(2,1)S(1)}, bf16[32,2048]{1,0:T(8,128)(2,1)S(1)}, u32[]{:S(2)}, u32[]{:S(2)}) %collective-permute-start.8) | collective-permute-done | bytes 131104 | tf_op jit(solution)/shard_map/ppermute | solution.py:184
  30.1 0.0 collective-permute-done.9.refs_2_
  30.1 0.0 collective-permute-done.10.refs_3_
  30.1 2.4 %product.3 = (f32[8,128,128]{2,1,0:T(8,128)S(1)}, f32[8,128,128]{2,1,0:T(8,128)S(1)}) custom-call(s32[1]{0:T(128)} %bitcast.me_ref, bf16[2,8,128,2048]{3,2,1,0:T(8,128)(2,1)S(1)} %mask.1.masked_ref, bf16[32,2048]{1,0:T(8,128)(2,1)S(1)} %collective-permute-done.7.refs_0_, bf16[32,2048]{1,0:T(8,128)(2,1)S(1)} %collective-permute-done.8.refs_1_, ...), custom_call_target="tpu_custom_call" | custom-call | flops 1073741824 | bytes 9961476 | tf_op jit(solution)/shard_map/product/pallas_call | solution.py:24
  32.5 0.1 collective-permute-start.11
  32.6 0.0 collective-permute-done.4.got_ref
  32.6 0.1 core_sum.2
  32.7 1.8 %collective-permute-start.5 = (s16[528,128]{1,0:T(8,128)(2,1)S(1)}, s16[528,128]{1,0:T(8,128)(2,1)S(1)}, u32[]{:S(2)}, u32[]{:S(2)}) collective-permute-start(s16[528,128]{1,0:T(8,128)(2,1)S(1)} %get-tuple-element.38), channel_id=1, source_target_pairs={{0,2},{1,3},{2,0},{3,1},{4,6},{5,7},{6,4},{7,5},{8,10},{9,11},{10,... | collective-permute-start | bytes 405512 | tf_op jit(solution)/shard_map/ppermute | solution.py:184
  34.5 0.0 collective-permute-done.11.got_ref
  34.5 0.1 core_sum.3
  34.6 1.4 %collective-permute-start.12 = (s16[528,128]{1,0:T(8,128)(2,1)S(1)}, s16[528,128]{1,0:T(8,128)(2,1)S(1)}, u32[]{:S(2)}, u32[]{:S(2)}) collective-permute-start(s16[528,128]{1,0:T(8,128)(2,1)S(1)} %get-tuple-element.48), channel_id=1, source_target_pairs={{0,2},{1,3},{2,0},{3,1},{4,6},{5,7},{6,4},{7,5},{8,10},{9,11},{10,... | collective-permute-start | bytes 405512 | tf_op jit(solution)/shard_map/ppermute | solution.py:184
  36.0 3.1 %collective-permute-done.5.got_ref = s16[528,128]{1,0:T(8,128)(2,1)S(1)} collective-permute-done((s16[528,128]{1,0:T(8,128)(2,1)S(1)}, s16[528,128]{1,0:T(8,128)(2,1)S(1)}, u32[]{:S(2)}, u32[]{:S(2)}) %collective-permute-start.5) | collective-permute-done | bytes 135200 | tf_op jit(solution)/shard_map/ppermute | solution.py:184
  39.1 0.1 halve.2
  39.2 5.3 %collective-permute-start.6 = (s16[272,128]{1,0:T(8,128)(2,1)S(1)}, s16[272,128]{1,0:T(8,128)(2,1)S(1)}, u32[]{:S(2)}, u32[]{:S(2)}) collective-permute-start(s16[272,128]{1,0:T(8,128)(2,1)S(1)} %get-tuple-element.40), channel_id=1, source_target_pairs={{0,4},{1,5},{2,6},{3,7},{4,0},{5,1},{6,2},{7,3},{8,12},{9,13},{10,... | collective-permute-start | bytes 208904 | tf_op jit(solution)/shard_map/ppermute | solution.py:184
  44.6 0.0 collective-permute-done.12.got_ref
  44.6 0.1 halve.3
  44.7 2.4 %collective-permute-start.13 = (s16[272,128]{1,0:T(8,128)(2,1)S(1)}, s16[272,128]{1,0:T(8,128)(2,1)S(1)}, u32[]{:S(2)}, u32[]{:S(2)}) collective-permute-start(s16[272,128]{1,0:T(8,128)(2,1)S(1)} %get-tuple-element.50), channel_id=1, source_target_pairs={{0,4},{1,5},{2,6},{3,7},{4,0},{5,1},{6,2},{7,3},{8,12},{9,13},{10,... | collective-permute-start | bytes 208904 | tf_op jit(solution)/shard_map/ppermute | solution.py:184
  47.1 0.0 collective-permute-done.6.near_got
  47.1 2.3 %collective-permute-done.13.far_got = s16[272,128]{1,0:T(8,128)(2,1)S(1)} collective-permute-done((s16[272,128]{1,0:T(8,128)(2,1)S(1)}, s16[272,128]{1,0:T(8,128)(2,1)S(1)}, u32[]{:S(2)}, u32[]{:S(2)}) %collective-permute-start.13) | collective-permute-done | bytes 69664 | tf_op jit(solution)/shard_map/ppermute | solution.py:184
  49.3 0.1 join.1
  49.4 4.0 %collective-permute-start.14 = (s16[144,256]{1,0:T(8,128)(2,1)S(1)}, s16[144,256]{1,0:T(8,128)(2,1)S(1)}, u32[]{:S(2)}, u32[]{:S(2)}) collective-permute-start(s16[144,256]{1,0:T(8,128)(2,1)S(1)} %get-tuple-element.52), channel_id=1, source_target_pairs={{0,8},{1,9},{2,10},{3,11},{4,12},{5,13},{6,14},{7,15},{8,0},{9,1},... | collective-permute-start | bytes 221192 | tf_op jit(solution)/shard_map/ppermute | solution.py:184
  53.4 0.0 copy-done.3
  53.4 0.1 copy.5.places_ref
  53.5 3.0 %collective-permute-done.14.got_ref = s16[144,256]{1,0:T(8,128)(2,1)S(1)} collective-permute-done((s16[144,256]{1,0:T(8,128)(2,1)S(1)}, s16[144,256]{1,0:T(8,128)(2,1)S(1)}, u32[]{:S(2)}, u32[]{:S(2)}) %collective-permute-start.14) | collective-permute-done | bytes 73760 | tf_op jit(solution)/shard_map/ppermute | solution.py:184
  56.5 1.0 %last.1 = f32[128,256]{1,0:T(8,128)} custom-call(s32[1]{0:T(128)} %bitcast.me_ref, f32[2,128,128]{2,1,0:T(8,128)S(1)} %get-tuple-element.51.keep_ref, s16[144,256]{1,0:T(8,128)(2,1)S(1)} %collective-permute-done.14.got_ref, s32[256,1]{1,0:T(8,128)S(1)} %copy.5.places_ref), custom_call_target="tpu_custom_call" | custom-call | bytes 336900 | tf_op jit(solution)/shard_map/last/pallas_call | solution.py:24
  (2 shorter events, 0.0 us)
Async XLA Ops:
  0.0 1.2 %copy-start.1 = (bf16[16,32768]{1,0:T(8,128)(2,1)S(1)}, bf16[16,32768]{1,0:T(8,128)(2,1)}, u32[]{:S(2)}) copy-start(bf16[16,32768]{1,0:T(8,128)(2,1)} %amplitudes_ref.1) | copy-start | bytes 3145732
  1.3 2.1 %collective-permute-start = (bf16[8,16,2048]{2,1,0:T(8,128)(2,1)S(1)}, bf16[8,16,2048]{2,1,0:T(8,128)(2,1)S(1)}, u32[]{:S(2)}, u32[]{:S(2)}) collective-permute-start(bf16[8,16,2048]{2,1,0:T(8,128)(2,1)S(1)} %get-tuple-element.30), channel_id=1, source_target_pairs={{0,1},{1,0},{2,3},{3,2},{4,5},{5,4},{6,7},{7,6},{8,9},{9,8},{10,11... | collective-permute-start | bytes 1572872 | tf_op jit(solution)/shard_map/ppermute | solution.py:184
  3.4 8.8 %collective-permute-start.1 = (bf16[32,2048]{1,0:T(8,128)(2,1)S(1)}, bf16[32,2048]{1,0:T(8,128)(2,1)S(1)}, u32[]{:S(2)}, u32[]{:S(2)}) collective-permute-start(bf16[32,2048]{1,0:T(8,128)(2,1)S(1)} %get-tuple-element.32), channel_id=1, source_target_pairs={{0,2},{1,3},{2,0},{3,1},{4,6},{5,7},{6,4},{7,5},{8,10},{9,11},{10,... | collective-permute-start | bytes 393224 | tf_op jit(solution)/shard_map/ppermute | solution.py:184
  6.4 10.8 %collective-permute-start.2 = (bf16[32,2048]{1,0:T(8,128)(2,1)S(1)}, bf16[32,2048]{1,0:T(8,128)(2,1)S(1)}, u32[]{:S(2)}, u32[]{:S(2)}) collective-permute-start(bf16[32,2048]{1,0:T(8,128)(2,1)S(1)} %get-tuple-element.33), channel_id=1, source_target_pairs={{0,4},{1,5},{2,6},{3,7},{4,0},{5,1},{6,2},{7,3},{8,12},{9,13},{10,... | collective-permute-start | bytes 393224 | tf_op jit(solution)/shard_map/ppermute | solution.py:184
  8.0 17.8 %collective-permute-start.3 = (bf16[32,2048]{1,0:T(8,128)(2,1)S(1)}, bf16[32,2048]{1,0:T(8,128)(2,1)S(1)}, u32[]{:S(2)}, u32[]{:S(2)}) collective-permute-start(bf16[32,2048]{1,0:T(8,128)(2,1)S(1)} %get-tuple-element.34), channel_id=1, source_target_pairs={{0,6},{1,7},{2,4},{3,5},{4,2},{5,3},{6,0},{7,1},{8,14},{9,15},{10,... | collective-permute-start | bytes 393224 | tf_op jit(solution)/shard_map/ppermute | solution.py:184
  8.0 20.2 %collective-permute-start.7 = (bf16[32,2048]{1,0:T(8,128)(2,1)S(1)}, bf16[32,2048]{1,0:T(8,128)(2,1)S(1)}, u32[]{:S(2)}, u32[]{:S(2)}) collective-permute-start(bf16[32,2048]{1,0:T(8,128)(2,1)S(1)} %get-tuple-element.41), channel_id=1, source_target_pairs={{0,8},{1,9},{2,10},{3,11},{4,12},{5,13},{6,14},{7,15},{8,0},{9,1},... | collective-permute-start | bytes 393224 | tf_op jit(solution)/shard_map/ppermute | solution.py:184
  10.9 19.2 %collective-permute-start.8 = (bf16[32,2048]{1,0:T(8,128)(2,1)S(1)}, bf16[32,2048]{1,0:T(8,128)(2,1)S(1)}, u32[]{:S(2)}, u32[]{:S(2)}) collective-permute-start(bf16[32,2048]{1,0:T(8,128)(2,1)S(1)} %get-tuple-element.42), channel_id=1, source_target_pairs={{0,10},{1,11},{2,8},{3,9},{4,14},{5,15},{6,12},{7,13},{8,2},{9,3},... | collective-permute-start | bytes 393224 | tf_op jit(solution)/shard_map/ppermute | solution.py:184
  12.2 17.9 %collective-permute-start.9 = (bf16[32,2048]{1,0:T(8,128)(2,1)S(1)}, bf16[32,2048]{1,0:T(8,128)(2,1)S(1)}, u32[]{:S(2)}, u32[]{:S(2)}) collective-permute-start(bf16[32,2048]{1,0:T(8,128)(2,1)S(1)} %get-tuple-element.43), channel_id=1, source_target_pairs={{0,12},{1,13},{2,14},{3,15},{4,8},{5,9},{6,10},{7,11},{8,4},{9,5},... | collective-permute-start | bytes 393224 | tf_op jit(solution)/shard_map/ppermute | solution.py:184
  17.1 13.0 %collective-permute-start.10 = (bf16[32,2048]{1,0:T(8,128)(2,1)S(1)}, bf16[32,2048]{1,0:T(8,128)(2,1)S(1)}, u32[]{:S(2)}, u32[]{:S(2)}) collective-permute-start(bf16[32,2048]{1,0:T(8,128)(2,1)S(1)} %get-tuple-element.44), channel_id=1, source_target_pairs={{0,14},{1,15},{2,12},{3,13},{4,10},{5,11},{6,8},{7,9},{8,6},{9,7},... | collective-permute-start | bytes 393224 | tf_op jit(solution)/shard_map/ppermute | solution.py:184
  17.8 3.4 %copy-start = (bf16[2048,2048]{1,0:T(8,128)(2,1)S(1)}, bf16[2048,2048]{1,0:T(8,128)(2,1)}, u32[]{:S(2)}) copy-start(bf16[2048,2048]{1,0:T(8,128)(2,1)} %rows_ref.1) | copy-start | bytes 25165828
  21.2 0.7 %copy-start.2 = (s32[16,16]{1,0:T(8,128)S(1)}, s32[16,16]{1,0:T(8,128)}, u32[]{:S(2)}) copy-start(s32[16,16]{1,0:T(8,128)} %mask_ref.1) | copy-start | bytes 3076
  25.7 27.6 %copy-start.3 = (s32[256]{0:T(256)S(1)}, s32[256]{0:T(256)}, u32[]{:S(2)}) copy-start(s32[256]{0:T(256)} %param.7) | copy-start | bytes 3076
  28.1 4.4 %collective-permute-start.4 = (f32[8,128,128]{2,1,0:T(8,128)S(1)}, f32[8,128,128]{2,1,0:T(8,128)S(1)}, u32[]{:S(2)}, u32[]{:S(2)}) collective-permute-start(f32[8,128,128]{2,1,0:T(8,128)S(1)} %get-tuple-element.36), channel_id=1, source_target_pairs={{0,1},{1,0},{2,3},{3,2},{4,5},{5,4},{6,7},{7,6},{8,9},{9,8},{10,11... | collective-permute-start | bytes 1572872 | tf_op jit(solution)/shard_map/ppermute | solution.py:184
  32.5 2.0 %collective-permute-start.11 = (f32[8,128,128]{2,1,0:T(8,128)S(1)}, f32[8,128,128]{2,1,0:T(8,128)S(1)}, u32[]{:S(2)}, u32[]{:S(2)}) collective-permute-start(f32[8,128,128]{2,1,0:T(8,128)S(1)} %get-tuple-element.46), channel_id=1, source_target_pairs={{0,1},{1,0},{2,3},{3,2},{4,5},{5,4},{6,7},{7,6},{8,9},{9,8},{10,11... | collective-permute-start | bytes 1572872 | tf_op jit(solution)/shard_map/ppermute | solution.py:184
  32.7 6.4 %collective-permute-start.5 = (s16[528,128]{1,0:T(8,128)(2,1)S(1)}, s16[528,128]{1,0:T(8,128)(2,1)S(1)}, u32[]{:S(2)}, u32[]{:S(2)}) collective-permute-start(s16[528,128]{1,0:T(8,128)(2,1)S(1)} %get-tuple-element.38), channel_id=1, source_target_pairs={{0,2},{1,3},{2,0},{3,1},{4,6},{5,7},{6,4},{7,5},{8,10},{9,11},{10,... | collective-permute-start | bytes 405512 | tf_op jit(solution)/shard_map/ppermute | solution.py:184
  34.6 10.0 %collective-permute-start.12 = (s16[528,128]{1,0:T(8,128)(2,1)S(1)}, s16[528,128]{1,0:T(8,128)(2,1)S(1)}, u32[]{:S(2)}, u32[]{:S(2)}) collective-permute-start(s16[528,128]{1,0:T(8,128)(2,1)S(1)} %get-tuple-element.48), channel_id=1, source_target_pairs={{0,2},{1,3},{2,0},{3,1},{4,6},{5,7},{6,4},{7,5},{8,10},{9,11},{10,... | collective-permute-start | bytes 405512 | tf_op jit(solution)/shard_map/ppermute | solution.py:184
  39.2 7.9 %collective-permute-start.6 = (s16[272,128]{1,0:T(8,128)(2,1)S(1)}, s16[272,128]{1,0:T(8,128)(2,1)S(1)}, u32[]{:S(2)}, u32[]{:S(2)}) collective-permute-start(s16[272,128]{1,0:T(8,128)(2,1)S(1)} %get-tuple-element.40), channel_id=1, source_target_pairs={{0,4},{1,5},{2,6},{3,7},{4,0},{5,1},{6,2},{7,3},{8,12},{9,13},{10,... | collective-permute-start | bytes 208904 | tf_op jit(solution)/shard_map/ppermute | solution.py:184
  44.7 4.7 %collective-permute-start.13 = (s16[272,128]{1,0:T(8,128)(2,1)S(1)}, s16[272,128]{1,0:T(8,128)(2,1)S(1)}, u32[]{:S(2)}, u32[]{:S(2)}) collective-permute-start(s16[272,128]{1,0:T(8,128)(2,1)S(1)} %get-tuple-element.50), channel_id=1, source_target_pairs={{0,4},{1,5},{2,6},{3,7},{4,0},{5,1},{6,2},{7,3},{8,12},{9,13},{10,... | collective-permute-start | bytes 208904 | tf_op jit(solution)/shard_map/ppermute | solution.py:184
  49.4 7.1 %collective-permute-start.14 = (s16[144,256]{1,0:T(8,128)(2,1)S(1)}, s16[144,256]{1,0:T(8,128)(2,1)S(1)}, u32[]{:S(2)}, u32[]{:S(2)}) collective-permute-start(s16[144,256]{1,0:T(8,128)(2,1)S(1)} %get-tuple-element.52), channel_id=1, source_target_pairs={{0,8},{1,9},{2,10},{3,11},{4,12},{5,13},{6,14},{7,15},{8,0},{9,1},... | collective-permute-start | bytes 221192 | tf_op jit(solution)/shard_map/ppermute | solution.py:184

commit v5 on v4

--- a/solution.py
+++ b/solution.py
@@ -55,15 +55,26 @@
     pl.when(core == 1)(lambda: store(got_ref, keep_ref))
 
 
-def mask_kernel(me_ref, mask_ref, rows_ref, out_ref):
-    k, core = pl.program_id(0), me_ref[0] % 2
-    base = ((me_ref[0] // 2) ^ k) * 2
-    for slot, own in enumerate((1 - core, core)):
-        rows = pl.ds(pl.multiple_of(own * TILE, TILE), TILE)
-        for t in range(mask_ref.shape[1]):
-            columns = slice(t * TILE, (t + 1) * TILE)
-            factor = mask_ref[base + own, t].astype(jnp.float32).astype(out_ref.dtype)
-            out_ref[slot, 0, :, columns] = rows_ref[rows, columns] * factor
+def mask_kernel(me_ref, mask_ref, rows_ref, out_ref, block_ref, arrived):
+    chips, _, depth = block_ref.shape
+    chip, core = me_ref[0] // 2, me_ref[0] % 2
+
+    def copy(k):
+        start = pl.multiple_of((chip ^ k) * (2 * TILE), 2 * TILE)
+        return pltpu.make_async_copy(rows_ref.at[pl.ds(start, 2 * TILE), :], block_ref.at[k], arrived.at[k])
+
+    for k in range(chips):
+        copy(k).start()
+
+    @pl.loop(0, chips)
+    def _(k):
+        copy(k).wait()
+        for slot, own in enumerate((1 - core, core)):
+            rows = pl.ds(pl.multiple_of(own * TILE, TILE), TILE)
+            for t in range(mask_ref.shape[1]):
+                columns = slice(t * TILE, (t + 1) * TILE)
+                factor = mask_ref[(chip ^ k) * 2 + own, t].astype(jnp.float32).astype(out_ref.dtype)
+                out_ref[slot, k, :, columns] = block_ref[k, rows, columns] * factor
 
 
 def masked_rows(me, block_mask, integrals):
@@ -71,15 +82,12 @@
     chips = rows // (2 * TILE)
     return pl.pallas_call(
         mask_kernel,
-        grid_spec=pltpu.PrefetchScalarGridSpec(
-            num_scalar_prefetch=1,
-            grid=(chips,),
-            in_specs=[SCALARS, pl.BlockSpec((2 * TILE, depth), lambda k, me: ((me[0] // 2) ^ k, 0))],
-            out_specs=pl.BlockSpec((2, 1, TILE, depth), lambda k, me: (0, k, 0, 0)),
-        ),
+        in_specs=[SCALARS, SCALARS, pl.BlockSpec(memory_space=pltpu.HBM)],
+        out_specs=WHOLE,
         out_shape=jax.ShapeDtypeStruct((2, chips, TILE, depth), integrals.dtype),
+        scratch_shapes=[pltpu.VMEM((chips, 2 * TILE, depth), integrals.dtype), pltpu.SemaphoreType.DMA((chips,))],
         name="mask",
-        compiler_params=pltpu.CompilerParams(vmem_limit_bytes=16 * 2**20),
+        compiler_params=pltpu.CompilerParams(vmem_limit_bytes=40 * 2**20),
         cost_estimate=pl.CostEstimate(flops=rows * depth, bytes_accessed=4 * rows * depth, transcendentals=0),
     )(me, block_mask, integrals)
 
@@ -191,27 +199,33 @@
     received = {0: pieces[0]}
     for k in sending(chips):
         received[k] = swap(pieces[k], 2 * k)
-    masked = masked_rows(me, block_mask, integrals)
+    begun = lax.optimization_barrier((me, received[chips - 1]))[0]
+    masked = masked_rows(begun, block_mask, integrals)
 
     half = chips // 2
     bits = tuple(range((chips - 1).bit_length()))
+
     sums = []
     for first in (0, half):
         send, keep = call(
             product_kernel, "product", [plain(chips, pairs)] * 2, me, masked,
             *[received[k] for k in range(first, first + half)], scalars=1,
-            scratch=[pltpu.VMEM((pairs, depth), kind)], flops=4 * chips * TILE * depth * pairs,
+            scratch=[pltpu.VMEM((pairs, depth), kind)],
         )
         got = swap(send, 1)
         blocks = half
         send, keep = call(
-            functools.partial(first_kernel, bits), "core_sum", [packed(blocks, pairs), plain(blocks, pairs)], keep, got
+            functools.partial(first_kernel, bits), "core_sum", [packed(blocks, pairs), plain(blocks, pairs)],
+            keep, got,
         )
         for bit in bits[:-1]:
             got = swap(send, 2 << bit)
             if bit < bits[-2]:
                 blocks //= 2
-                send, keep = call(halve_kernel, "halve", [packed(blocks, pairs), plain(blocks, pairs)], keep, got)
+                send, keep = call(
+                    halve_kernel, "halve", [packed(blocks, pairs), plain(blocks, pairs)],
+                    keep, got,
+                )
         sums += [keep, got]
     send, keep = call(join_kernel, "join", [packed(1, 2 * pairs), plain(2, pairs)], *sums)
     got = swap(send, 2 << bits[-1])

time: 57.7 us -> 53.9 us (0.934)
  starting transfers between devices: 28.7 us -> 23.4 us
  waiting for transfers between devices: 13.1 us -> 17.4 us
  local copies, waits for them, and re-layouts: 5.44 us -> 2.06 us
  Pallas kernels: 10.1 us -> 10.7 us
    ppermute x15, starting transfers between devices: 28.7 us -> 23.4 us  [swap(): return lax.ppermute(value, 'ab', [(i, i ^ bits) for i in range(devices)])]
    ppermute x15, waiting for transfers between devices: 13.1 us -> 17.4 us  [swap(): return lax.ppermute(value, 'ab', [(i, i ^ bits) for i in range(devices)])]
    unnamed x8 -> x6, local copies, waits for them, and re-layouts: 5.31 us -> 1.93 us
    pallas_call x1, Pallas kernels: 3.8 us -> 4.45 us  [masked_rows(): pl.pallas_call(mask_kernel, in_specs=[SCALARS, SCALARS, pl.BlockSpec(memo...]
  transfers between devices with their start and end apart: 15 -> 15, of which waited for: 6 -> 10; matrix products, arithmetic and copies ran while one was open for 0% -> 0% of each run, Pallas kernels for 15% -> 18%
where the time goes in v5:
time: 53.9 us; the launch traced here: 53.7 us
  starting transfers between devices  23.4 us (43%)
  waiting for transfers between devices  17.4 us (32%)
  Pallas kernels  10.7 us (20%)
  local copies, waits for them, and re-layouts  2.06 us (4%)
    ppermute x15, starting transfers between devices, swap(): return lax.ppermute(value, 'ab', [(i, i ^ bits) for i in range(devices)])  23.4 us
    ppermute x15, waiting for transfers between devices, swap(): return lax.ppermute(value, 'ab', [(i, i ^ bits) for i in range(devices)])  17.4 us
    pallas_call x10, Pallas kernels, call(): pl.pallas_call(kernel, out_shape=outs, in_specs=[SCALARS] * scalars + [WH...  6.3 us
    pallas_call x1, Pallas kernels, masked_rows(): pl.pallas_call(mask_kernel, in_specs=[SCALARS, SCALARS, pl.BlockSpec(memo...  4.45 us
    unnamed x6, local copies, waits for them, and re-layouts  1.93 us
  transfers between devices with their start and end apart: 15, of which 10 were waited for; matrix products, arithmetic and copies ran while one was open for 0% of the time, Pallas kernels for 18%

profile of v5, /device:TPU:0, one launch (start us, length us, event | category | flops | bytes accessed | tf_op | source)
XLA Modules:
  0.0 53.7 jit_solution(4001097268587702646)
XLA Ops:
  0.0 0.0 copy-start
  0.0 1.2 %copy-done = bf16[16,32768]{1,0:T(8,128)(2,1)S(1)} copy-done((bf16[16,32768]{1,0:T(8,128)(2,1)S(1)}, bf16[16,32768]{1,0:T(8,128)(2,1)}, u32[]{:S(2)}) %copy-start) | copy-done | bytes 1048600
  1.2 0.1 sort.1
  1.3 0.5 collective-permute-start
  1.8 1.5 %collective-permute-done.got_ref = bf16[8,16,2048]{2,1,0:T(8,128)(2,1)S(1)} collective-permute-done((bf16[8,16,2048]{2,1,0:T(8,128)(2,1)S(1)}, bf16[8,16,2048]{2,1,0:T(8,128)(2,1)S(1)}, u32[]{:S(2)}, u32[]{:S(2)}) %collective-permute-start) | collective-permute-done | bytes 524320 | tf_op jit(solution)/shard_map/ppermute | solution.py:192
  3.4 0.1 pieces.1
  3.4 6.0 %collective-permute-start.1 = (bf16[32,2048]{1,0:T(8,128)(2,1)S(1)}, bf16[32,2048]{1,0:T(8,128)(2,1)S(1)}, u32[]{:S(2)}, u32[]{:S(2)}) collective-permute-start(bf16[32,2048]{1,0:T(8,128)(2,1)S(1)} %get-tuple-element.32), channel_id=1, source_target_pairs={{0,14},{1,15},{2,12},{3,13},{4,10},{5,11},{6,8},{7,9},{8,6},{9,7},... | collective-permute-start | bytes 393224 | tf_op jit(solution)/shard_map/ppermute | solution.py:192
  9.4 0.5 collective-permute-start.2
  9.9 0.0 collective-permute-start.3
  9.9 3.0 %collective-permute-start.4 = (bf16[32,2048]{1,0:T(8,128)(2,1)S(1)}, bf16[32,2048]{1,0:T(8,128)(2,1)S(1)}, u32[]{:S(2)}, u32[]{:S(2)}) collective-permute-start(bf16[32,2048]{1,0:T(8,128)(2,1)S(1)} %get-tuple-element.37), channel_id=1, source_target_pairs={{0,6},{1,7},{2,4},{3,5},{4,2},{5,3},{6,0},{7,1},{8,14},{9,15},{10,... | collective-permute-start | bytes 393224 | tf_op jit(solution)/shard_map/ppermute | solution.py:192
  12.9 0.0 collective-permute-start.8
  12.9 0.8 %collective-permute-done.1.refs_3_ = bf16[32,2048]{1,0:T(8,128)(2,1)S(1)} collective-permute-done((bf16[32,2048]{1,0:T(8,128)(2,1)S(1)}, bf16[32,2048]{1,0:T(8,128)(2,1)S(1)}, u32[]{:S(2)}, u32[]{:S(2)}) %collective-permute-start.1) | collective-permute-done | bytes 131104 | tf_op jit(solution)/shard_map/ppermute | solution.py:192
  13.8 4.9 %collective-permute-start.9 = (bf16[32,2048]{1,0:T(8,128)(2,1)S(1)}, bf16[32,2048]{1,0:T(8,128)(2,1)S(1)}, u32[]{:S(2)}, u32[]{:S(2)}) collective-permute-start(bf16[32,2048]{1,0:T(8,128)(2,1)S(1)} %get-tuple-element.45), channel_id=1, source_target_pairs={{0,10},{1,11},{2,8},{3,9},{4,14},{5,15},{6,12},{7,13},{8,2},{9,3},... | collective-permute-start | bytes 393224 | tf_op jit(solution)/shard_map/ppermute | solution.py:192
  18.6 0.0 collective-permute-done.2.refs_1_
  18.6 0.4 collective-permute-start.10
  19.0 0.0 copy-start.1
  19.0 0.7 %copy-done.1 = s32[16,16]{1,0:T(8,128)S(1)} copy-done((s32[16,16]{1,0:T(8,128)S(1)}, s32[16,16]{1,0:T(8,128)}, u32[]{:S(2)}) %copy-start.1) | copy-done | bytes 1048
  19.7 4.4 %mask.1.masked_ref = bf16[2,8,128,2048]{3,2,1,0:T(8,128)(2,1)S(1)} custom-call(s32[1]{0:T(128)} %bitcast.me_ref, s32[16,16]{1,0:T(8,128)S(1)} %copy-done.1, bf16[2048,2048]{1,0:T(8,128)(2,1)} %rows_ref.1), custom_call_target="tpu_custom_call" | custom-call | flops 4194304 | bytes 16777216 | tf_op jit(solution)/shard_map/mask/pallas_call | solution.py:83
  24.2 0.0 collective-permute-done.3.refs_2_
  24.2 0.0 collective-permute-done.4.refs_3_
  24.2 0.0 copy-start.2
  24.2 2.4 %product.2 = (f32[8,128,128]{2,1,0:T(8,128)S(1)}, f32[8,128,128]{2,1,0:T(8,128)S(1)}) custom-call(s32[1]{0:T(128)} %bitcast.me_ref, bf16[2,8,128,2048]{3,2,1,0:T(8,128)(2,1)S(1)} %mask.1.masked_ref, bf16[32,2048]{1,0:T(8,128)(2,1)S(1)} %get-tuple-element.34.refs_0_, bf16[32,2048]{1,0:T(8,128)(2,1)S(1)} %collective-permute-done.2.refs_1_, ...), custom_call_target="tpu_custom_call" | custom-call | bytes 9961476 | tf_op jit(solution)/shard_map/product/pallas_call | solution.py:24
  26.6 0.1 collective-permute-start.5
  26.6 1.9 %collective-permute-done.8.refs_0_ = bf16[32,2048]{1,0:T(8,128)(2,1)S(1)} collective-permute-done((bf16[32,2048]{1,0:T(8,128)(2,1)S(1)}, bf16[32,2048]{1,0:T(8,128)(2,1)S(1)}, u32[]{:S(2)}, u32[]{:S(2)}) %collective-permute-start.8) | collective-permute-done | bytes 131104 | tf_op jit(solution)/shard_map/ppermute | solution.py:192
  28.5 2.8 %collective-permute-done.9.refs_1_ = bf16[32,2048]{1,0:T(8,128)(2,1)S(1)} collective-permute-done((bf16[32,2048]{1,0:T(8,128)(2,1)S(1)}, bf16[32,2048]{1,0:T(8,128)(2,1)S(1)}, u32[]{:S(2)}, u32[]{:S(2)}) %collective-permute-start.9) | collective-permute-done | bytes 131104 | tf_op jit(solution)/shard_map/ppermute | solution.py:192
  31.3 0.0 collective-permute-done.10.refs_2_
  31.3 2.4 %product.3 = (f32[8,128,128]{2,1,0:T(8,128)S(1)}, f32[8,128,128]{2,1,0:T(8,128)S(1)}) custom-call(s32[1]{0:T(128)} %bitcast.me_ref, bf16[2,8,128,2048]{3,2,1,0:T(8,128)(2,1)S(1)} %mask.1.masked_ref, bf16[32,2048]{1,0:T(8,128)(2,1)S(1)} %collective-permute-done.8.refs_0_, bf16[32,2048]{1,0:T(8,128)(2,1)S(1)} %collective-permute-done.9.refs_1_, ...), custom_call_target="tpu_custom_call" | custom-call | bytes 9961476 | tf_op jit(solution)/shard_map/product/pallas_call | solution.py:24
  33.7 0.1 collective-permute-start.11
  33.8 0.0 collective-permute-done.5.got_ref
  33.8 0.1 core_sum.2
  33.9 1.1 %collective-permute-start.6 = (s16[528,128]{1,0:T(8,128)(2,1)S(1)}, s16[528,128]{1,0:T(8,128)(2,1)S(1)}, u32[]{:S(2)}, u32[]{:S(2)}) collective-permute-start(s16[528,128]{1,0:T(8,128)(2,1)S(1)} %get-tuple-element.41), channel_id=1, source_target_pairs={{0,2},{1,3},{2,0},{3,1},{4,6},{5,7},{6,4},{7,5},{8,10},{9,11},{10,... | collective-permute-start | bytes 405512 | tf_op jit(solution)/shard_map/ppermute | solution.py:192
  35.0 0.6 %collective-permute-done.11.got_ref = f32[8,128,128]{2,1,0:T(8,128)S(1)} collective-permute-done((f32[8,128,128]{2,1,0:T(8,128)S(1)}, f32[8,128,128]{2,1,0:T(8,128)S(1)}, u32[]{:S(2)}, u32[]{:S(2)}) %collective-permute-start.11) | collective-permute-done | bytes 524320 | tf_op jit(solution)/shard_map/ppermute | solution.py:192
  35.7 0.1 core_sum.3
  35.8 1.1 %collective-permute-start.12 = (s16[528,128]{1,0:T(8,128)(2,1)S(1)}, s16[528,128]{1,0:T(8,128)(2,1)S(1)}, u32[]{:S(2)}, u32[]{:S(2)}) collective-permute-start(s16[528,128]{1,0:T(8,128)(2,1)S(1)} %get-tuple-element.50), channel_id=1, source_target_pairs={{0,2},{1,3},{2,0},{3,1},{4,6},{5,7},{6,4},{7,5},{8,10},{9,11},{10,... | collective-permute-start | bytes 405512 | tf_op jit(solution)/shard_map/ppermute | solution.py:192
  36.9 3.4 %collective-permute-done.6.got_ref = s16[528,128]{1,0:T(8,128)(2,1)S(1)} collective-permute-done((s16[528,128]{1,0:T(8,128)(2,1)S(1)}, s16[528,128]{1,0:T(8,128)(2,1)S(1)}, u32[]{:S(2)}, u32[]{:S(2)}) %collective-permute-start.6) | collective-permute-done | bytes 135200 | tf_op jit(solution)/shard_map/ppermute | solution.py:192
  40.3 0.1 halve.2
  40.4 1.6 %collective-permute-start.7 = (s16[272,128]{1,0:T(8,128)(2,1)S(1)}, s16[272,128]{1,0:T(8,128)(2,1)S(1)}, u32[]{:S(2)}, u32[]{:S(2)}) collective-permute-start(s16[272,128]{1,0:T(8,128)(2,1)S(1)} %get-tuple-element.43), channel_id=1, source_target_pairs={{0,4},{1,5},{2,6},{3,7},{4,0},{5,1},{6,2},{7,3},{8,12},{9,13},{10,... | collective-permute-start | bytes 208904 | tf_op jit(solution)/shard_map/ppermute | solution.py:192
  42.1 0.8 %collective-permute-done.12.got_ref = s16[528,128]{1,0:T(8,128)(2,1)S(1)} collective-permute-done((s16[528,128]{1,0:T(8,128)(2,1)S(1)}, s16[528,128]{1,0:T(8,128)(2,1)S(1)}, u32[]{:S(2)}, u32[]{:S(2)}) %collective-permute-start.12) | collective-permute-done | bytes 135200 | tf_op jit(solution)/shard_map/ppermute | solution.py:192
  42.8 0.1 halve.3
  42.9 1.6 %collective-permute-start.13 = (s16[272,128]{1,0:T(8,128)(2,1)S(1)}, s16[272,128]{1,0:T(8,128)(2,1)S(1)}, u32[]{:S(2)}, u32[]{:S(2)}) collective-permute-start(s16[272,128]{1,0:T(8,128)(2,1)S(1)} %get-tuple-element.52), channel_id=1, source_target_pairs={{0,4},{1,5},{2,6},{3,7},{4,0},{5,1},{6,2},{7,3},{8,12},{9,13},{10,... | collective-permute-start | bytes 208904 | tf_op jit(solution)/shard_map/ppermute | solution.py:192
  44.6 0.2 collective-permute-done.7.near_got
  44.8 2.5 %collective-permute-done.13.far_got = s16[272,128]{1,0:T(8,128)(2,1)S(1)} collective-permute-done((s16[272,128]{1,0:T(8,128)(2,1)S(1)}, s16[272,128]{1,0:T(8,128)(2,1)S(1)}, u32[]{:S(2)}, u32[]{:S(2)}) %collective-permute-start.13) | collective-permute-done | bytes 69664 | tf_op jit(solution)/shard_map/ppermute | solution.py:192
  47.3 0.1 join.1
  47.4 2.4 %collective-permute-start.14 = (s16[144,256]{1,0:T(8,128)(2,1)S(1)}, s16[144,256]{1,0:T(8,128)(2,1)S(1)}, u32[]{:S(2)}, u32[]{:S(2)}) collective-permute-start(s16[144,256]{1,0:T(8,128)(2,1)S(1)} %get-tuple-element.54), channel_id=1, source_target_pairs={{0,8},{1,9},{2,10},{3,11},{4,12},{5,13},{6,14},{7,15},{8,0},{9,1},... | collective-permute-start | bytes 221192 | tf_op jit(solution)/shard_map/ppermute | solution.py:192
  49.8 0.0 copy-done.2
  49.8 0.1 copy.5.places_ref
  49.9 2.8 %collective-permute-done.14.got_ref = s16[144,256]{1,0:T(8,128)(2,1)S(1)} collective-permute-done((s16[144,256]{1,0:T(8,128)(2,1)S(1)}, s16[144,256]{1,0:T(8,128)(2,1)S(1)}, u32[]{:S(2)}, u32[]{:S(2)}) %collective-permute-start.14) | collective-permute-done | bytes 73760 | tf_op jit(solution)/shard_map/ppermute | solution.py:192
  52.7 1.0 %last.1 = f32[128,256]{1,0:T(8,128)} custom-call(s32[1]{0:T(128)} %bitcast.me_ref, f32[2,128,128]{2,1,0:T(8,128)S(1)} %get-tuple-element.53.keep_ref, s16[144,256]{1,0:T(8,128)(2,1)S(1)} %collective-permute-done.14.got_ref, s32[256,1]{1,0:T(8,128)S(1)} %copy.5.places_ref), custom_call_target="tpu_custom_call" | custom-call | bytes 336900 | tf_op jit(solution)/shard_map/last/pallas_call | solution.py:24
Async XLA Ops:
  0.0 1.2 %copy-start = (bf16[16,32768]{1,0:T(8,128)(2,1)S(1)}, bf16[16,32768]{1,0:T(8,128)(2,1)}, u32[]{:S(2)}) copy-start(bf16[16,32768]{1,0:T(8,128)(2,1)} %amplitudes_ref.1) | copy-start | bytes 3145732
  1.3 2.1 %collective-permute-start = (bf16[8,16,2048]{2,1,0:T(8,128)(2,1)S(1)}, bf16[8,16,2048]{2,1,0:T(8,128)(2,1)S(1)}, u32[]{:S(2)}, u32[]{:S(2)}) collective-permute-start(bf16[8,16,2048]{2,1,0:T(8,128)(2,1)S(1)} %get-tuple-element.31), channel_id=1, source_target_pairs={{0,1},{1,0},{2,3},{3,2},{4,5},{5,4},{6,7},{7,6},{8,9},{9,8},{10,11... | collective-permute-start | bytes 1572872 | tf_op jit(solution)/shard_map/ppermute | solution.py:192
  3.4 10.3 %collective-permute-start.1 = (bf16[32,2048]{1,0:T(8,128)(2,1)S(1)}, bf16[32,2048]{1,0:T(8,128)(2,1)S(1)}, u32[]{:S(2)}, u32[]{:S(2)}) collective-permute-start(bf16[32,2048]{1,0:T(8,128)(2,1)S(1)} %get-tuple-element.32), channel_id=1, source_target_pairs={{0,14},{1,15},{2,12},{3,13},{4,10},{5,11},{6,8},{7,9},{8,6},{9,7},... | collective-permute-start | bytes 393224 | tf_op jit(solution)/shard_map/ppermute | solution.py:192
  9.4 9.2 %collective-permute-start.2 = (bf16[32,2048]{1,0:T(8,128)(2,1)S(1)}, bf16[32,2048]{1,0:T(8,128)(2,1)S(1)}, u32[]{:S(2)}, u32[]{:S(2)}) collective-permute-start(bf16[32,2048]{1,0:T(8,128)(2,1)S(1)} %get-tuple-element.35), channel_id=1, source_target_pairs={{0,2},{1,3},{2,0},{3,1},{4,6},{5,7},{6,4},{7,5},{8,10},{9,11},{10,... | collective-permute-start | bytes 393224 | tf_op jit(solution)/shard_map/ppermute | solution.py:192
  9.9 14.2 %collective-permute-start.3 = (bf16[32,2048]{1,0:T(8,128)(2,1)S(1)}, bf16[32,2048]{1,0:T(8,128)(2,1)S(1)}, u32[]{:S(2)}, u32[]{:S(2)}) collective-permute-start(bf16[32,2048]{1,0:T(8,128)(2,1)S(1)} %get-tuple-element.36), channel_id=1, source_target_pairs={{0,4},{1,5},{2,6},{3,7},{4,0},{5,1},{6,2},{7,3},{8,12},{9,13},{10,... | collective-permute-start | bytes 393224 | tf_op jit(solution)/shard_map/ppermute | solution.py:192
  9.9 14.2 %collective-permute-start.4 = (bf16[32,2048]{1,0:T(8,128)(2,1)S(1)}, bf16[32,2048]{1,0:T(8,128)(2,1)S(1)}, u32[]{:S(2)}, u32[]{:S(2)}) collective-permute-start(bf16[32,2048]{1,0:T(8,128)(2,1)S(1)} %get-tuple-element.37), channel_id=1, source_target_pairs={{0,6},{1,7},{2,4},{3,5},{4,2},{5,3},{6,0},{7,1},{8,14},{9,15},{10,... | collective-permute-start | bytes 393224 | tf_op jit(solution)/shard_map/ppermute | solution.py:192
  12.9 15.6 %collective-permute-start.8 = (bf16[32,2048]{1,0:T(8,128)(2,1)S(1)}, bf16[32,2048]{1,0:T(8,128)(2,1)S(1)}, u32[]{:S(2)}, u32[]{:S(2)}) collective-permute-start(bf16[32,2048]{1,0:T(8,128)(2,1)S(1)} %get-tuple-element.44), channel_id=1, source_target_pairs={{0,8},{1,9},{2,10},{3,11},{4,12},{5,13},{6,14},{7,15},{8,0},{9,1},... | collective-permute-start | bytes 393224 | tf_op jit(solution)/shard_map/ppermute | solution.py:192
  13.8 17.6 %collective-permute-start.9 = (bf16[32,2048]{1,0:T(8,128)(2,1)S(1)}, bf16[32,2048]{1,0:T(8,128)(2,1)S(1)}, u32[]{:S(2)}, u32[]{:S(2)}) collective-permute-start(bf16[32,2048]{1,0:T(8,128)(2,1)S(1)} %get-tuple-element.45), channel_id=1, source_target_pairs={{0,10},{1,11},{2,8},{3,9},{4,14},{5,15},{6,12},{7,13},{8,2},{9,3},... | collective-permute-start | bytes 393224 | tf_op jit(solution)/shard_map/ppermute | solution.py:192
  18.6 12.7 %collective-permute-start.10 = (bf16[32,2048]{1,0:T(8,128)(2,1)S(1)}, bf16[32,2048]{1,0:T(8,128)(2,1)S(1)}, u32[]{:S(2)}, u32[]{:S(2)}) collective-permute-start(bf16[32,2048]{1,0:T(8,128)(2,1)S(1)} %get-tuple-element.46), channel_id=1, source_target_pairs={{0,12},{1,13},{2,14},{3,15},{4,8},{5,9},{6,10},{7,11},{8,4},{9,5},... | collective-permute-start | bytes 393224 | tf_op jit(solution)/shard_map/ppermute | solution.py:192
  19.0 0.7 %copy-start.1 = (s32[16,16]{1,0:T(8,128)S(1)}, s32[16,16]{1,0:T(8,128)}, u32[]{:S(2)}) copy-start(s32[16,16]{1,0:T(8,128)} %mask_ref.1) | copy-start | bytes 3076
  24.2 25.6 %copy-start.2 = (s32[256]{0:T(256)S(1)}, s32[256]{0:T(256)}, u32[]{:S(2)}) copy-start(s32[256]{0:T(256)} %param.7) | copy-start | bytes 3076
  26.6 7.2 %collective-permute-start.5 = (f32[8,128,128]{2,1,0:T(8,128)S(1)}, f32[8,128,128]{2,1,0:T(8,128)S(1)}, u32[]{:S(2)}, u32[]{:S(2)}) collective-permute-start(f32[8,128,128]{2,1,0:T(8,128)S(1)} %get-tuple-element.39), channel_id=1, source_target_pairs={{0,1},{1,0},{2,3},{3,2},{4,5},{5,4},{6,7},{7,6},{8,9},{9,8},{10,11... | collective-permute-start | bytes 1572872 | tf_op jit(solution)/shard_map/ppermute | solution.py:192
  33.7 2.0 %collective-permute-start.11 = (f32[8,128,128]{2,1,0:T(8,128)S(1)}, f32[8,128,128]{2,1,0:T(8,128)S(1)}, u32[]{:S(2)}, u32[]{:S(2)}) collective-permute-start(f32[8,128,128]{2,1,0:T(8,128)S(1)} %get-tuple-element.48), channel_id=1, source_target_pairs={{0,1},{1,0},{2,3},{3,2},{4,5},{5,4},{6,7},{7,6},{8,9},{9,8},{10,11... | collective-permute-start | bytes 1572872 | tf_op jit(solution)/shard_map/ppermute | solution.py:192
  33.9 6.4 %collective-permute-start.6 = (s16[528,128]{1,0:T(8,128)(2,1)S(1)}, s16[528,128]{1,0:T(8,128)(2,1)S(1)}, u32[]{:S(2)}, u32[]{:S(2)}) collective-permute-start(s16[528,128]{1,0:T(8,128)(2,1)S(1)} %get-tuple-element.41), channel_id=1, source_target_pairs={{0,2},{1,3},{2,0},{3,1},{4,6},{5,7},{6,4},{7,5},{8,10},{9,11},{10,... | collective-permute-start | bytes 405512 | tf_op jit(solution)/shard_map/ppermute | solution.py:192
  35.8 7.0 %collective-permute-start.12 = (s16[528,128]{1,0:T(8,128)(2,1)S(1)}, s16[528,128]{1,0:T(8,128)(2,1)S(1)}, u32[]{:S(2)}, u32[]{:S(2)}) collective-permute-start(s16[528,128]{1,0:T(8,128)(2,1)S(1)} %get-tuple-element.50), channel_id=1, source_target_pairs={{0,2},{1,3},{2,0},{3,1},{4,6},{5,7},{6,4},{7,5},{8,10},{9,11},{10,... | collective-permute-start | bytes 405512 | tf_op jit(solution)/shard_map/ppermute | solution.py:192
  40.4 4.4 %collective-permute-start.7 = (s16[272,128]{1,0:T(8,128)(2,1)S(1)}, s16[272,128]{1,0:T(8,128)(2,1)S(1)}, u32[]{:S(2)}, u32[]{:S(2)}) collective-permute-start(s16[272,128]{1,0:T(8,128)(2,1)S(1)} %get-tuple-element.43), channel_id=1, source_target_pairs={{0,4},{1,5},{2,6},{3,7},{4,0},{5,1},{6,2},{7,3},{8,12},{9,13},{10,... | collective-permute-start | bytes 208904 | tf_op jit(solution)/shard_map/ppermute | solution.py:192
  42.9 4.4 %collective-permute-start.13 = (s16[272,128]{1,0:T(8,128)(2,1)S(1)}, s16[272,128]{1,0:T(8,128)(2,1)S(1)}, u32[]{:S(2)}, u32[]{:S(2)}) collective-permute-start(s16[272,128]{1,0:T(8,128)(2,1)S(1)} %get-tuple-element.52), channel_id=1, source_target_pairs={{0,4},{1,5},{2,6},{3,7},{4,0},{5,1},{6,2},{7,3},{8,12},{9,13},{10,... | collective-permute-start | bytes 208904 | tf_op jit(solution)/shard_map/ppermute | solution.py:192
  47.4 5.3 %collective-permute-start.14 = (s16[144,256]{1,0:T(8,128)(2,1)S(1)}, s16[144,256]{1,0:T(8,128)(2,1)S(1)}, u32[]{:S(2)}, u32[]{:S(2)}) collective-permute-start(s16[144,256]{1,0:T(8,128)(2,1)S(1)} %get-tuple-element.54), channel_id=1, source_target_pairs={{0,8},{1,9},{2,10},{3,11},{4,12},{5,13},{6,14},{7,15},{8,0},{9,1},... | collective-permute-start | bytes 221192 | tf_op jit(solution)/shard_map/ppermute | solution.py:192

commit v6 on v5

--- a/solution.py
+++ b/solution.py
@@ -163,22 +163,28 @@
     pack([jnp.concatenate(both, axis=1)], send)
 
 
-def last_kernel(half, me_ref, keep_ref, got_ref, places_ref, out_ref):
+def place_kernel(chips, me_ref, places_ref, out_ref):
+    pairs, columns = places_ref.shape[0] // 2, out_ref.shape[1]
+    far = me_ref[0] >= chips
+    column = lax.broadcasted_iota(jnp.int32, (pairs, columns), 1)
+    low, high = places_ref[:pairs], places_ref[pairs:]
+    for c, place in enumerate((jnp.where(far, high, low), jnp.where(far, low, high))):
+        ones = (place == column).astype(jnp.float32).astype(out_ref.dtype)
+        for part in range(3):
+            start = (3 * c + part) * pairs
+            out_ref[start : start + pairs] = ones
+
+
+def last_kernel(keep_ref, got_ref, place_ref, out_ref):
     pairs = keep_ref.shape[2]
-    high = (me_ref[0] >= half).astype(jnp.int32)
     got = unpack(got_ref)[0]
-    total = None
+    parts = []
     for c in range(2):
         rest = keep_ref[c] + got[:, (1 - c) * pairs : (2 - c) * pairs]
-        place = jnp.where(high == c, places_ref[:pairs], places_ref[pairs:])
-        columns = lax.broadcasted_iota(jnp.int32, (pairs, out_ref.shape[1]), 1)
-        chosen = (place == columns).astype(jnp.float32).astype(jnp.bfloat16)
         for _ in range(3):
-            part = rest.astype(jnp.bfloat16)
-            rest = rest - part.astype(jnp.float32)
-            moved = jnp.dot(part, chosen, preferred_element_type=jnp.float32)
-            total = moved if total is None else total + moved
-    out_ref[...] = total
+            parts.append(rest.astype(jnp.bfloat16))
+            rest = rest - parts[-1].astype(jnp.float32)
+    out_ref[...] = jnp.dot(jnp.concatenate(parts, axis=1), place_ref[...], preferred_element_type=jnp.float32)
 
 
 def per_device(devices, amplitudes, integrals, block_mask, pair_list):
@@ -202,11 +208,16 @@
     begun = lax.optimization_barrier((me, received[chips - 1]))[0]
     masked = masked_rows(begun, block_mask, integrals)
 
+    place = call(
+        functools.partial(place_kernel, chips), "place", [jax.ShapeDtypeStruct((6 * pairs, 2 * pairs), kind)],
+        begun, pair_list.reshape(-1, 1), scalars=1,
+    )[0]
+
     half = chips // 2
     bits = tuple(range((chips - 1).bit_length()))
 
     sums = []
-    for first in (0, half):
+    for first, order in ((0, bits), (half, bits[-2::-1] + bits[-1:])):
         send, keep = call(
             product_kernel, "product", [plain(chips, pairs)] * 2, me, masked,
             *[received[k] for k in range(first, first + half)], scalars=1,
@@ -215,12 +226,12 @@
         got = swap(send, 1)
         blocks = half
         send, keep = call(
-            functools.partial(first_kernel, bits), "core_sum", [packed(blocks, pairs), plain(blocks, pairs)],
+            functools.partial(first_kernel, order), "core_sum", [packed(blocks, pairs), plain(blocks, pairs)],
             keep, got,
         )
-        for bit in bits[:-1]:
+        for bit in order[:-1]:
             got = swap(send, 2 << bit)
-            if bit < bits[-2]:
+            if blocks > 2:
                 blocks //= 2
                 send, keep = call(
                     halve_kernel, "halve", [packed(blocks, pairs), plain(blocks, pairs)],
@@ -229,10 +240,7 @@
         sums += [keep, got]
     send, keep = call(join_kernel, "join", [packed(1, 2 * pairs), plain(2, pairs)], *sums)
     got = swap(send, 2 << bits[-1])
-    return call(
-        functools.partial(last_kernel, chips), "last", [jax.ShapeDtypeStruct((TILE, 2 * pairs), jnp.float32)],
-        me, keep, got, pair_list.reshape(-1, 1), scalars=1,
-    )[0]
+    return call(last_kernel, "last", [jax.ShapeDtypeStruct((TILE, 2 * pairs), jnp.float32)], keep, got, place)[0]
 
 
 def solution(mesh):

time: 53.9 us -> 52.6 us (0.976)
  waiting for transfers between devices: 17.4 us -> 16.4 us
    ppermute x15, waiting for transfers between devices: 17.4 us -> 16.4 us  [swap(): return lax.ppermute(value, 'ab', [(i, i ^ bits) for i in range(devices)])]
    pallas_call x10 -> x11, Pallas kernels: 6.3 us -> 6.28 us  [call(): pl.pallas_call(kernel, out_shape=outs, in_specs=[SCALARS] * scalars + [WH...]
  transfers between devices with their start and end apart: 15 -> 15, of which waited for: 10 -> 9; matrix products, arithmetic and copies ran while one was open for 0% -> 0% of each run, Pallas kernels for 18% -> 18%
where the time goes in v6:
time: 52.6 us; the launch traced here: 52.4 us
  starting transfers between devices  23 us (44%)
  waiting for transfers between devices  16.4 us (31%)
  Pallas kernels  10.7 us (20%)
  local copies, waits for them, and re-layouts  2.06 us (4%)
    ppermute x15, starting transfers between devices, swap(): return lax.ppermute(value, 'ab', [(i, i ^ bits) for i in range(devices)])  23 us
    ppermute x15, waiting for transfers between devices, swap(): return lax.ppermute(value, 'ab', [(i, i ^ bits) for i in range(devices)])  16.4 us
    pallas_call x11, Pallas kernels, call(): pl.pallas_call(kernel, out_shape=outs, in_specs=[SCALARS] * scalars + [WH...  6.28 us
    pallas_call x1, Pallas kernels, masked_rows(): pl.pallas_call(mask_kernel, in_specs=[SCALARS, SCALARS, pl.BlockSpec(memo...  4.45 us
    unnamed x6, local copies, waits for them, and re-layouts  1.93 us
  transfers between devices with their start and end apart: 15, of which 9 were waited for; matrix products, arithmetic and copies ran while one was open for 0% of the time, Pallas kernels for 18%

profile of v6, /device:TPU:0, one launch (start us, length us, event | category | flops | bytes accessed | tf_op | source)
XLA Modules:
  0.0 52.4 jit_solution(18207060278297751154)
XLA Ops:
  0.0 0.0 copy-start
  0.0 1.2 %copy-done = bf16[16,32768]{1,0:T(8,128)(2,1)S(1)} copy-done((bf16[16,32768]{1,0:T(8,128)(2,1)S(1)}, bf16[16,32768]{1,0:T(8,128)(2,1)}, u32[]{:S(2)}) %copy-start) | copy-done | bytes 1048600
  1.2 0.1 sort.1
  1.3 0.5 collective-permute-start
  1.8 1.5 %collective-permute-done.got_ref = bf16[8,16,2048]{2,1,0:T(8,128)(2,1)S(1)} collective-permute-done((bf16[8,16,2048]{2,1,0:T(8,128)(2,1)S(1)}, bf16[8,16,2048]{2,1,0:T(8,128)(2,1)S(1)}, u32[]{:S(2)}, u32[]{:S(2)}) %collective-permute-start) | collective-permute-done | bytes 524320 | tf_op jit(solution)/shard_map/ppermute | solution.py:198
  3.4 0.1 pieces.1
  3.4 6.0 %collective-permute-start.1 = (bf16[32,2048]{1,0:T(8,128)(2,1)S(1)}, bf16[32,2048]{1,0:T(8,128)(2,1)S(1)}, u32[]{:S(2)}, u32[]{:S(2)}) collective-permute-start(bf16[32,2048]{1,0:T(8,128)(2,1)S(1)} %get-tuple-element.32), channel_id=1, source_target_pairs={{0,14},{1,15},{2,12},{3,13},{4,10},{5,11},{6,8},{7,9},{8,6},{9,7},... | collective-permute-start | bytes 393224 | tf_op jit(solution)/shard_map/ppermute | solution.py:198
  9.4 0.5 collective-permute-start.2
  9.9 0.0 collective-permute-start.3
  9.9 3.0 %collective-permute-start.4 = (bf16[32,2048]{1,0:T(8,128)(2,1)S(1)}, bf16[32,2048]{1,0:T(8,128)(2,1)S(1)}, u32[]{:S(2)}, u32[]{:S(2)}) collective-permute-start(bf16[32,2048]{1,0:T(8,128)(2,1)S(1)} %get-tuple-element.37), channel_id=1, source_target_pairs={{0,6},{1,7},{2,4},{3,5},{4,2},{5,3},{6,0},{7,1},{8,14},{9,15},{10,... | collective-permute-start | bytes 393224 | tf_op jit(solution)/shard_map/ppermute | solution.py:198
  12.9 0.0 collective-permute-start.8
  12.9 0.8 %collective-permute-done.1.refs_3_ = bf16[32,2048]{1,0:T(8,128)(2,1)S(1)} collective-permute-done((bf16[32,2048]{1,0:T(8,128)(2,1)S(1)}, bf16[32,2048]{1,0:T(8,128)(2,1)S(1)}, u32[]{:S(2)}, u32[]{:S(2)}) %collective-permute-start.1) | collective-permute-done | bytes 131104 | tf_op jit(solution)/shard_map/ppermute | solution.py:198
  13.8 4.9 %collective-permute-start.9 = (bf16[32,2048]{1,0:T(8,128)(2,1)S(1)}, bf16[32,2048]{1,0:T(8,128)(2,1)S(1)}, u32[]{:S(2)}, u32[]{:S(2)}) collective-permute-start(bf16[32,2048]{1,0:T(8,128)(2,1)S(1)} %get-tuple-element.45), channel_id=1, source_target_pairs={{0,10},{1,11},{2,8},{3,9},{4,14},{5,15},{6,12},{7,13},{8,2},{9,3},... | collective-permute-start | bytes 393224 | tf_op jit(solution)/shard_map/ppermute | solution.py:198
  18.6 0.0 collective-permute-done.2.refs_1_
  18.6 0.4 collective-permute-start.10
  19.0 0.7 %copy-done.1 = s32[16,16]{1,0:T(8,128)S(1)} copy-done((s32[16,16]{1,0:T(8,128)S(1)}, s32[16,16]{1,0:T(8,128)}, u32[]{:S(2)}) %copy-start.1) | copy-done | bytes 1048
  19.7 4.4 %mask.1.masked_ref = bf16[2,8,128,2048]{3,2,1,0:T(8,128)(2,1)S(1)} custom-call(s32[1]{0:T(128)} %bitcast.me_ref, s32[16,16]{1,0:T(8,128)S(1)} %copy-done.1, bf16[2048,2048]{1,0:T(8,128)(2,1)} %rows_ref.1), custom_call_target="tpu_custom_call" | custom-call | flops 4194304 | bytes 16777216 | tf_op jit(solution)/shard_map/mask/pallas_call | solution.py:83
  24.2 0.0 collective-permute-done.3.refs_2_
  24.2 0.0 collective-permute-done.4.refs_3_
  24.2 0.0 copy-start.2
  24.2 2.4 %product.2 = (f32[8,128,128]{2,1,0:T(8,128)S(1)}, f32[8,128,128]{2,1,0:T(8,128)S(1)}) custom-call(s32[1]{0:T(128)} %bitcast.me_ref, bf16[2,8,128,2048]{3,2,1,0:T(8,128)(2,1)S(1)} %mask.1.masked_ref, bf16[32,2048]{1,0:T(8,128)(2,1)S(1)} %get-tuple-element.34.refs_0_, bf16[32,2048]{1,0:T(8,128)(2,1)S(1)} %collective-permute-done.2.refs_1_, ...), custom_call_target="tpu_custom_call" | custom-call | bytes 9961476 | tf_op jit(solution)/shard_map/product/pallas_call | solution.py:24
  26.6 0.1 collective-permute-start.5
  26.6 1.9 %collective-permute-done.8.refs_0_ = bf16[32,2048]{1,0:T(8,128)(2,1)S(1)} collective-permute-done((bf16[32,2048]{1,0:T(8,128)(2,1)S(1)}, bf16[32,2048]{1,0:T(8,128)(2,1)S(1)}, u32[]{:S(2)}, u32[]{:S(2)}) %collective-permute-start.8) | collective-permute-done | bytes 131104 | tf_op jit(solution)/shard_map/ppermute | solution.py:198
  28.5 2.8 %collective-permute-done.9.refs_1_ = bf16[32,2048]{1,0:T(8,128)(2,1)S(1)} collective-permute-done((bf16[32,2048]{1,0:T(8,128)(2,1)S(1)}, bf16[32,2048]{1,0:T(8,128)(2,1)S(1)}, u32[]{:S(2)}, u32[]{:S(2)}) %collective-permute-start.9) | collective-permute-done | bytes 131104 | tf_op jit(solution)/shard_map/ppermute | solution.py:198
  31.3 0.0 collective-permute-done.10.refs_2_
  31.3 2.4 %product.3 = (f32[8,128,128]{2,1,0:T(8,128)S(1)}, f32[8,128,128]{2,1,0:T(8,128)S(1)}) custom-call(s32[1]{0:T(128)} %bitcast.me_ref, bf16[2,8,128,2048]{3,2,1,0:T(8,128)(2,1)S(1)} %mask.1.masked_ref, bf16[32,2048]{1,0:T(8,128)(2,1)S(1)} %collective-permute-done.8.refs_0_, bf16[32,2048]{1,0:T(8,128)(2,1)S(1)} %collective-permute-done.9.refs_1_, ...), custom_call_target="tpu_custom_call" | custom-call | bytes 9961476 | tf_op jit(solution)/shard_map/product/pallas_call | solution.py:24
  33.7 0.1 collective-permute-start.11
  33.8 0.0 collective-permute-done.5.got_ref
  33.8 0.1 core_sum.2
  33.9 1.1 %collective-permute-start.6 = (s16[528,128]{1,0:T(8,128)(2,1)S(1)}, s16[528,128]{1,0:T(8,128)(2,1)S(1)}, u32[]{:S(2)}, u32[]{:S(2)}) collective-permute-start(s16[528,128]{1,0:T(8,128)(2,1)S(1)} %get-tuple-element.41), channel_id=1, source_target_pairs={{0,2},{1,3},{2,0},{3,1},{4,6},{5,7},{6,4},{7,5},{8,10},{9,11},{10,... | collective-permute-start | bytes 405512 | tf_op jit(solution)/shard_map/ppermute | solution.py:198
  35.0 0.6 %collective-permute-done.11.got_ref = f32[8,128,128]{2,1,0:T(8,128)S(1)} collective-permute-done((f32[8,128,128]{2,1,0:T(8,128)S(1)}, f32[8,128,128]{2,1,0:T(8,128)S(1)}, u32[]{:S(2)}, u32[]{:S(2)}) %collective-permute-start.11) | collective-permute-done | bytes 524320 | tf_op jit(solution)/shard_map/ppermute | solution.py:198
  35.7 0.1 core_sum.3
  35.8 1.6 %collective-permute-start.12 = (s16[528,128]{1,0:T(8,128)(2,1)S(1)}, s16[528,128]{1,0:T(8,128)(2,1)S(1)}, u32[]{:S(2)}, u32[]{:S(2)}) collective-permute-start(s16[528,128]{1,0:T(8,128)(2,1)S(1)} %get-tuple-element.50), channel_id=1, source_target_pairs={{0,4},{1,5},{2,6},{3,7},{4,0},{5,1},{6,2},{7,3},{8,12},{9,13},{10,... | collective-permute-start | bytes 405512 | tf_op jit(solution)/shard_map/ppermute | solution.py:198
  37.4 2.5 %collective-permute-done.6.got_ref = s16[528,128]{1,0:T(8,128)(2,1)S(1)} collective-permute-done((s16[528,128]{1,0:T(8,128)(2,1)S(1)}, s16[528,128]{1,0:T(8,128)(2,1)S(1)}, u32[]{:S(2)}, u32[]{:S(2)}) %collective-permute-start.6) | collective-permute-done | bytes 135200 | tf_op jit(solution)/shard_map/ppermute | solution.py:198
  39.9 0.1 halve.2
  40.0 1.6 %collective-permute-start.7 = (s16[272,128]{1,0:T(8,128)(2,1)S(1)}, s16[272,128]{1,0:T(8,128)(2,1)S(1)}, u32[]{:S(2)}, u32[]{:S(2)}) collective-permute-start(s16[272,128]{1,0:T(8,128)(2,1)S(1)} %get-tuple-element.43), channel_id=1, source_target_pairs={{0,4},{1,5},{2,6},{3,7},{4,0},{5,1},{6,2},{7,3},{8,12},{9,13},{10,... | collective-permute-start | bytes 208904 | tf_op jit(solution)/shard_map/ppermute | solution.py:198
  41.7 0.0 collective-permute-done.12.got_ref
  41.7 0.1 halve.3
  41.8 1.0 %collective-permute-start.13 = (s16[272,128]{1,0:T(8,128)(2,1)S(1)}, s16[272,128]{1,0:T(8,128)(2,1)S(1)}, u32[]{:S(2)}, u32[]{:S(2)}) collective-permute-start(s16[272,128]{1,0:T(8,128)(2,1)S(1)} %get-tuple-element.52), channel_id=1, source_target_pairs={{0,2},{1,3},{2,0},{3,1},{4,6},{5,7},{6,4},{7,5},{8,10},{9,11},{10,... | collective-permute-start | bytes 208904 | tf_op jit(solution)/shard_map/ppermute | solution.py:198
  42.8 1.6 %collective-permute-done.7.near_got = s16[272,128]{1,0:T(8,128)(2,1)S(1)} collective-permute-done((s16[272,128]{1,0:T(8,128)(2,1)S(1)}, s16[272,128]{1,0:T(8,128)(2,1)S(1)}, u32[]{:S(2)}, u32[]{:S(2)}) %collective-permute-start.7) | collective-permute-done | bytes 69664 | tf_op jit(solution)/shard_map/ppermute | solution.py:198
  44.4 1.7 %collective-permute-done.13.far_got = s16[272,128]{1,0:T(8,128)(2,1)S(1)} collective-permute-done((s16[272,128]{1,0:T(8,128)(2,1)S(1)}, s16[272,128]{1,0:T(8,128)(2,1)S(1)}, u32[]{:S(2)}, u32[]{:S(2)}) %collective-permute-start.13) | collective-permute-done | bytes 69664 | tf_op jit(solution)/shard_map/ppermute | solution.py:198
  46.1 0.1 join.1
  46.2 2.2 %collective-permute-start.14 = (s16[144,256]{1,0:T(8,128)(2,1)S(1)}, s16[144,256]{1,0:T(8,128)(2,1)S(1)}, u32[]{:S(2)}, u32[]{:S(2)}) collective-permute-start(s16[144,256]{1,0:T(8,128)(2,1)S(1)} %get-tuple-element.54), channel_id=1, source_target_pairs={{0,8},{1,9},{2,10},{3,11},{4,12},{5,13},{6,14},{7,15},{8,0},{9,1},... | collective-permute-start | bytes 221192 | tf_op jit(solution)/shard_map/ppermute | solution.py:198
  48.4 0.0 copy-done.2
  48.4 0.1 copy.5.places_ref
  48.6 0.1 place.1.place_ref
  48.7 2.9 %collective-permute-done.14.got_ref = s16[144,256]{1,0:T(8,128)(2,1)S(1)} collective-permute-done((s16[144,256]{1,0:T(8,128)(2,1)S(1)}, s16[144,256]{1,0:T(8,128)(2,1)S(1)}, u32[]{:S(2)}, u32[]{:S(2)}) %collective-permute-start.14) | collective-permute-done | bytes 73760 | tf_op jit(solution)/shard_map/ppermute | solution.py:198
  51.5 0.9 %last.1 = f32[128,256]{1,0:T(8,128)} custom-call(f32[2,128,128]{2,1,0:T(8,128)S(1)} %get-tuple-element.53.keep_ref, s16[144,256]{1,0:T(8,128)(2,1)S(1)} %collective-permute-done.14.got_ref, bf16[768,256]{1,0:T(8,128)(2,1)S(1)} %place.1.place_ref), custom_call_target="tpu_custom_call" | custom-call | bytes 729088 | tf_op jit(solution)/shard_map/last/pallas_call | solution.py:24
  (1 shorter events, 0.0 us)
Async XLA Ops:
  0.0 1.2 %copy-start = (bf16[16,32768]{1,0:T(8,128)(2,1)S(1)}, bf16[16,32768]{1,0:T(8,128)(2,1)}, u32[]{:S(2)}) copy-start(bf16[16,32768]{1,0:T(8,128)(2,1)} %amplitudes_ref.1) | copy-start | bytes 3145732
  1.3 2.1 %collective-permute-start = (bf16[8,16,2048]{2,1,0:T(8,128)(2,1)S(1)}, bf16[8,16,2048]{2,1,0:T(8,128)(2,1)S(1)}, u32[]{:S(2)}, u32[]{:S(2)}) collective-permute-start(bf16[8,16,2048]{2,1,0:T(8,128)(2,1)S(1)} %get-tuple-element.31), channel_id=1, source_target_pairs={{0,1},{1,0},{2,3},{3,2},{4,5},{5,4},{6,7},{7,6},{8,9},{9,8},{10,11... | collective-permute-start | bytes 1572872 | tf_op jit(solution)/shard_map/ppermute | solution.py:198
  3.4 10.3 %collective-permute-start.1 = (bf16[32,2048]{1,0:T(8,128)(2,1)S(1)}, bf16[32,2048]{1,0:T(8,128)(2,1)S(1)}, u32[]{:S(2)}, u32[]{:S(2)}) collective-permute-start(bf16[32,2048]{1,0:T(8,128)(2,1)S(1)} %get-tuple-element.32), channel_id=1, source_target_pairs={{0,14},{1,15},{2,12},{3,13},{4,10},{5,11},{6,8},{7,9},{8,6},{9,7},... | collective-permute-start | bytes 393224 | tf_op jit(solution)/shard_map/ppermute | solution.py:198
  9.4 9.2 %collective-permute-start.2 = (bf16[32,2048]{1,0:T(8,128)(2,1)S(1)}, bf16[32,2048]{1,0:T(8,128)(2,1)S(1)}, u32[]{:S(2)}, u32[]{:S(2)}) collective-permute-start(bf16[32,2048]{1,0:T(8,128)(2,1)S(1)} %get-tuple-element.35), channel_id=1, source_target_pairs={{0,2},{1,3},{2,0},{3,1},{4,6},{5,7},{6,4},{7,5},{8,10},{9,11},{10,... | collective-permute-start | bytes 393224 | tf_op jit(solution)/shard_map/ppermute | solution.py:198
  9.9 14.2 %collective-permute-start.3 = (bf16[32,2048]{1,0:T(8,128)(2,1)S(1)}, bf16[32,2048]{1,0:T(8,128)(2,1)S(1)}, u32[]{:S(2)}, u32[]{:S(2)}) collective-permute-start(bf16[32,2048]{1,0:T(8,128)(2,1)S(1)} %get-tuple-element.36), channel_id=1, source_target_pairs={{0,4},{1,5},{2,6},{3,7},{4,0},{5,1},{6,2},{7,3},{8,12},{9,13},{10,... | collective-permute-start | bytes 393224 | tf_op jit(solution)/shard_map/ppermute | solution.py:198
  9.9 14.2 %collective-permute-start.4 = (bf16[32,2048]{1,0:T(8,128)(2,1)S(1)}, bf16[32,2048]{1,0:T(8,128)(2,1)S(1)}, u32[]{:S(2)}, u32[]{:S(2)}) collective-permute-start(bf16[32,2048]{1,0:T(8,128)(2,1)S(1)} %get-tuple-element.37), channel_id=1, source_target_pairs={{0,6},{1,7},{2,4},{3,5},{4,2},{5,3},{6,0},{7,1},{8,14},{9,15},{10,... | collective-permute-start | bytes 393224 | tf_op jit(solution)/shard_map/ppermute | solution.py:198
  12.9 15.6 %collective-permute-start.8 = (bf16[32,2048]{1,0:T(8,128)(2,1)S(1)}, bf16[32,2048]{1,0:T(8,128)(2,1)S(1)}, u32[]{:S(2)}, u32[]{:S(2)}) collective-permute-start(bf16[32,2048]{1,0:T(8,128)(2,1)S(1)} %get-tuple-element.44), channel_id=1, source_target_pairs={{0,8},{1,9},{2,10},{3,11},{4,12},{5,13},{6,14},{7,15},{8,0},{9,1},... | collective-permute-start | bytes 393224 | tf_op jit(solution)/shard_map/ppermute | solution.py:198
  13.8 17.6 %collective-permute-start.9 = (bf16[32,2048]{1,0:T(8,128)(2,1)S(1)}, bf16[32,2048]{1,0:T(8,128)(2,1)S(1)}, u32[]{:S(2)}, u32[]{:S(2)}) collective-permute-start(bf16[32,2048]{1,0:T(8,128)(2,1)S(1)} %get-tuple-element.45), channel_id=1, source_target_pairs={{0,10},{1,11},{2,8},{3,9},{4,14},{5,15},{6,12},{7,13},{8,2},{9,3},... | collective-permute-start | bytes 393224 | tf_op jit(solution)/shard_map/ppermute | solution.py:198
  18.6 12.7 %collective-permute-start.10 = (bf16[32,2048]{1,0:T(8,128)(2,1)S(1)}, bf16[32,2048]{1,0:T(8,128)(2,1)S(1)}, u32[]{:S(2)}, u32[]{:S(2)}) collective-permute-start(bf16[32,2048]{1,0:T(8,128)(2,1)S(1)} %get-tuple-element.46), channel_id=1, source_target_pairs={{0,12},{1,13},{2,14},{3,15},{4,8},{5,9},{6,10},{7,11},{8,4},{9,5},... | collective-permute-start | bytes 393224 | tf_op jit(solution)/shard_map/ppermute | solution.py:198
  19.0 0.7 %copy-start.1 = (s32[16,16]{1,0:T(8,128)S(1)}, s32[16,16]{1,0:T(8,128)}, u32[]{:S(2)}) copy-start(s32[16,16]{1,0:T(8,128)} %mask_ref.1) | copy-start | bytes 3076
  24.2 24.2 %copy-start.2 = (s32[256]{0:T(256)S(1)}, s32[256]{0:T(256)}, u32[]{:S(2)}) copy-start(s32[256]{0:T(256)} %param.7) | copy-start | bytes 3076
  26.6 7.2 %collective-permute-start.5 = (f32[8,128,128]{2,1,0:T(8,128)S(1)}, f32[8,128,128]{2,1,0:T(8,128)S(1)}, u32[]{:S(2)}, u32[]{:S(2)}) collective-permute-start(f32[8,128,128]{2,1,0:T(8,128)S(1)} %get-tuple-element.39), channel_id=1, source_target_pairs={{0,1},{1,0},{2,3},{3,2},{4,5},{5,4},{6,7},{7,6},{8,9},{9,8},{10,11... | collective-permute-start | bytes 1572872 | tf_op jit(solution)/shard_map/ppermute | solution.py:198
  33.7 2.0 %collective-permute-start.11 = (f32[8,128,128]{2,1,0:T(8,128)S(1)}, f32[8,128,128]{2,1,0:T(8,128)S(1)}, u32[]{:S(2)}, u32[]{:S(2)}) collective-permute-start(f32[8,128,128]{2,1,0:T(8,128)S(1)} %get-tuple-element.48), channel_id=1, source_target_pairs={{0,1},{1,0},{2,3},{3,2},{4,5},{5,4},{6,7},{7,6},{8,9},{9,8},{10,11... | collective-permute-start | bytes 1572872 | tf_op jit(solution)/shard_map/ppermute | solution.py:198
  33.9 6.0 %collective-permute-start.6 = (s16[528,128]{1,0:T(8,128)(2,1)S(1)}, s16[528,128]{1,0:T(8,128)(2,1)S(1)}, u32[]{:S(2)}, u32[]{:S(2)}) collective-permute-start(s16[528,128]{1,0:T(8,128)(2,1)S(1)} %get-tuple-element.41), channel_id=1, source_target_pairs={{0,2},{1,3},{2,0},{3,1},{4,6},{5,7},{6,4},{7,5},{8,10},{9,11},{10,... | collective-permute-start | bytes 405512 | tf_op jit(solution)/shard_map/ppermute | solution.py:198
  35.8 5.9 %collective-permute-start.12 = (s16[528,128]{1,0:T(8,128)(2,1)S(1)}, s16[528,128]{1,0:T(8,128)(2,1)S(1)}, u32[]{:S(2)}, u32[]{:S(2)}) collective-permute-start(s16[528,128]{1,0:T(8,128)(2,1)S(1)} %get-tuple-element.50), channel_id=1, source_target_pairs={{0,4},{1,5},{2,6},{3,7},{4,0},{5,1},{6,2},{7,3},{8,12},{9,13},{10,... | collective-permute-start | bytes 405512 | tf_op jit(solution)/shard_map/ppermute | solution.py:198
  40.0 4.4 %collective-permute-start.7 = (s16[272,128]{1,0:T(8,128)(2,1)S(1)}, s16[272,128]{1,0:T(8,128)(2,1)S(1)}, u32[]{:S(2)}, u32[]{:S(2)}) collective-permute-start(s16[272,128]{1,0:T(8,128)(2,1)S(1)} %get-tuple-element.43), channel_id=1, source_target_pairs={{0,4},{1,5},{2,6},{3,7},{4,0},{5,1},{6,2},{7,3},{8,12},{9,13},{10,... | collective-permute-start | bytes 208904 | tf_op jit(solution)/shard_map/ppermute | solution.py:198
  41.8 4.4 %collective-permute-start.13 = (s16[272,128]{1,0:T(8,128)(2,1)S(1)}, s16[272,128]{1,0:T(8,128)(2,1)S(1)}, u32[]{:S(2)}, u32[]{:S(2)}) collective-permute-start(s16[272,128]{1,0:T(8,128)(2,1)S(1)} %get-tuple-element.52), channel_id=1, source_target_pairs={{0,2},{1,3},{2,0},{3,1},{4,6},{5,7},{6,4},{7,5},{8,10},{9,11},{10,... | collective-permute-start | bytes 208904 | tf_op jit(solution)/shard_map/ppermute | solution.py:198
  46.2 5.3 %collective-permute-start.14 = (s16[144,256]{1,0:T(8,128)(2,1)S(1)}, s16[144,256]{1,0:T(8,128)(2,1)S(1)}, u32[]{:S(2)}, u32[]{:S(2)}) collective-permute-start(s16[144,256]{1,0:T(8,128)(2,1)S(1)} %get-tuple-element.54), channel_id=1, source_target_pairs={{0,8},{1,9},{2,10},{3,11},{4,12},{5,13},{6,14},{7,15},{8,0},{9,1},... | collective-permute-start | bytes 221192 | tf_op jit(solution)/shard_map/ppermute | solution.py:198

commit v7 on v6

--- a/solution.py
+++ b/solution.py
@@ -92,17 +92,15 @@
     )(me, block_mask, integrals)
 
 
-def product_kernel(me_ref, masked_ref, *refs):
-    *pieces, send_ref, keep_ref, all_ref = refs
+def product_kernel(slot, me_ref, masked_ref, *refs):
+    *pieces, out_ref, all_ref = refs
     mine, depth = pieces[0].shape
     chip = me_ref[0] // 2 % len(pieces)
     for k, piece in enumerate(pieces):
         all_ref[pl.ds(pl.multiple_of((chip ^ k) * mine, mine), mine), :] = piece[...]
-    for slot, out_ref in enumerate((send_ref, keep_ref)):
-        rows = masked_ref[slot].reshape(-1, depth)
-        out_ref[...] = lax.dot_general(
-            rows, all_ref[...], (((1,), (1,)), ((), ())), preferred_element_type=jnp.float32
-        ).reshape(out_ref.shape)
+    out_ref[...] = lax.dot_general(
+        masked_ref[slot].reshape(-1, depth), all_ref[...], (((1,), (1,)), ((), ())), preferred_element_type=jnp.float32
+    ).reshape(out_ref.shape)
 
 
 def chip_of(index, bits):
@@ -152,15 +150,6 @@
     for index in range(half):
         keep[index] = keep_ref[index] + got[index]
     pack([keep_ref[index] + got[index] for index in range(half, 2 * half)], send)
-
-
-def join_kernel(near_keep, near_got, far_keep, far_got, send, keep):
-    both = []
-    for c, (kept, got) in enumerate(((near_keep, near_got), (far_keep, far_got))):
-        mine, theirs = unpack(got)
-        keep[c] = kept[0] + mine
-        both.append(kept[1] + theirs)
-    pack([jnp.concatenate(both, axis=1)], send)
 
 
 def place_kernel(chips, me_ref, places_ref, out_ref):
@@ -175,12 +164,10 @@
             out_ref[start : start + pairs] = ones
 
 
-def last_kernel(keep_ref, got_ref, place_ref, out_ref):
-    pairs = keep_ref.shape[2]
-    got = unpack(got_ref)[0]
+def last_kernel(near_keep, near_got, far_keep, far_got, place_ref, out_ref):
     parts = []
-    for c in range(2):
-        rest = keep_ref[c] + got[:, (1 - c) * pairs : (2 - c) * pairs]
+    for keep_ref, got_ref in ((near_keep, far_got), (far_keep, near_got)):
+        rest = keep_ref[0] + unpack(got_ref)[0]
         for _ in range(3):
             parts.append(rest.astype(jnp.bfloat16))
             rest = rest - parts[-1].astype(jnp.float32)
@@ -218,29 +205,31 @@
 
     sums = []
     for first, order in ((0, bits), (half, bits[-2::-1] + bits[-1:])):
-        send, keep = call(
-            product_kernel, "product", [plain(chips, pairs)] * 2, me, masked,
-            *[received[k] for k in range(first, first + half)], scalars=1,
-            scratch=[pltpu.VMEM((pairs, depth), kind)],
-        )
+        send, keep = [
+            call(
+                functools.partial(product_kernel, slot), "product", [plain(chips, pairs)], me, masked,
+                *[received[k] for k in range(first, first + half)], scalars=1,
+                scratch=[pltpu.VMEM((pairs, depth), kind)],
+            )[0]
+            for slot in range(2)
+        ]
+        me = lax.optimization_barrier((me, keep))[0]
         got = swap(send, 1)
         blocks = half
         send, keep = call(
             functools.partial(first_kernel, order), "core_sum", [packed(blocks, pairs), plain(blocks, pairs)],
             keep, got,
         )
-        for bit in order[:-1]:
+        for bit in order:
             got = swap(send, 2 << bit)
-            if blocks > 2:
+            if blocks > 1:
                 blocks //= 2
                 send, keep = call(
                     halve_kernel, "halve", [packed(blocks, pairs), plain(blocks, pairs)],
                     keep, got,
                 )
         sums += [keep, got]
-    send, keep = call(join_kernel, "join", [packed(1, 2 * pairs), plain(2, pairs)], *sums)
-    got = swap(send, 2 << bits[-1])
-    return call(last_kernel, "last", [jax.ShapeDtypeStruct((TILE, 2 * pairs), jnp.float32)], keep, got, place)[0]
+    return call(last_kernel, "last", [jax.ShapeDtypeStruct((TILE, 2 * pairs), jnp.float32)], *sums, place)[0]
 
 
 def solution(mesh):

time: 52.6 us -> 51.9 us (0.987)
  waiting for transfers between devices: 16.4 us -> 13.4 us
  starting transfers between devices: 23 us -> 24.7 us
    ppermute x15 -> x16, waiting for transfers between devices: 16.4 us -> 13.4 us  [swap(): return lax.ppermute(value, 'ab', [(i, i ^ bits) for i in range(devices)])]
    ppermute x15 -> x16, starting transfers between devices: 23 us -> 24.7 us  [swap(): return lax.ppermute(value, 'ab', [(i, i ^ bits) for i in range(devices)])]
    pallas_call x11 -> x14, Pallas kernels: 6.28 us -> 6.8 us  [call(): pl.pallas_call(kernel, out_shape=outs, in_specs=[SCALARS] * scalars + [WH...]
  transfers between devices with their start and end apart: 15 -> 16, of which waited for: 9 -> 9; matrix products, arithmetic and copies ran while one was open for 0% -> 0% of each run, Pallas kernels for 18% -> 20%
where the time goes in v7:
time: 51.9 us; the launch traced here: 51.7 us
  starting transfers between devices  24.7 us (48%)
  waiting for transfers between devices  13.4 us (26%)
  Pallas kernels  11.2 us (22%)
  local copies, waits for them, and re-layouts  2.06 us (4%)
    ppermute x16, starting transfers between devices, swap(): return lax.ppermute(value, 'ab', [(i, i ^ bits) for i in range(devices)])  24.7 us
    ppermute x16, waiting for transfers between devices, swap(): return lax.ppermute(value, 'ab', [(i, i ^ bits) for i in range(devices)])  13.4 us
    pallas_call x14, Pallas kernels, call(): pl.pallas_call(kernel, out_shape=outs, in_specs=[SCALARS] * scalars + [WH...  6.8 us
    pallas_call x1, Pallas kernels, masked_rows(): pl.pallas_call(mask_kernel, in_specs=[SCALARS, SCALARS, pl.BlockSpec(memo...  4.45 us
    unnamed x6, local copies, waits for them, and re-layouts  1.93 us
  transfers between devices with their start and end apart: 16, of which 9 were waited for; matrix products, arithmetic and copies ran while one was open for 0% of the time, Pallas kernels for 20%

profile of v7, /device:TPU:0, one launch (start us, length us, event | category | flops | bytes accessed | tf_op | source)
XLA Modules:
  0.0 51.7 jit_solution(15549717531311749361)
XLA Ops:
  0.0 1.2 %copy-done = bf16[16,32768]{1,0:T(8,128)(2,1)S(1)} copy-done((bf16[16,32768]{1,0:T(8,128)(2,1)S(1)}, bf16[16,32768]{1,0:T(8,128)(2,1)}, u32[]{:S(2)}) %copy-start) | copy-done | bytes 1048600
  1.2 0.1 sort.1
  1.3 0.5 %collective-permute-start = (bf16[8,16,2048]{2,1,0:T(8,128)(2,1)S(1)}, bf16[8,16,2048]{2,1,0:T(8,128)(2,1)S(1)}, u32[]{:S(2)}, u32[]{:S(2)}) collective-permute-start(bf16[8,16,2048]{2,1,0:T(8,128)(2,1)S(1)} %get-tuple-element.30), channel_id=1, source_target_pairs={{0,1},{1,0},{2,3},{3,2},{4,5},{5,4},{6,7},{7,6},{8,9},{9,8},{10,11... | collective-permute-start | bytes 1572872 | tf_op jit(solution)/shard_map/ppermute | solution.py:185
  1.8 1.5 %collective-permute-done.got_ref = bf16[8,16,2048]{2,1,0:T(8,128)(2,1)S(1)} collective-permute-done((bf16[8,16,2048]{2,1,0:T(8,128)(2,1)S(1)}, bf16[8,16,2048]{2,1,0:T(8,128)(2,1)S(1)}, u32[]{:S(2)}, u32[]{:S(2)}) %collective-permute-start) | collective-permute-done | bytes 524320 | tf_op jit(solution)/shard_map/ppermute | solution.py:185
  3.4 0.1 pieces.1
  3.4 6.0 %collective-permute-start.1 = (bf16[32,2048]{1,0:T(8,128)(2,1)S(1)}, bf16[32,2048]{1,0:T(8,128)(2,1)S(1)}, u32[]{:S(2)}, u32[]{:S(2)}) collective-permute-start(bf16[32,2048]{1,0:T(8,128)(2,1)S(1)} %get-tuple-element.31), channel_id=1, source_target_pairs={{0,14},{1,15},{2,12},{3,13},{4,10},{5,11},{6,8},{7,9},{8,6},{9,7},... | collective-permute-start | bytes 393224 | tf_op jit(solution)/shard_map/ppermute | solution.py:185
  9.4 0.5 collective-permute-start.2
  9.9 0.0 collective-permute-start.3
  9.9 3.0 %collective-permute-start.4 = (bf16[32,2048]{1,0:T(8,128)(2,1)S(1)}, bf16[32,2048]{1,0:T(8,128)(2,1)S(1)}, u32[]{:S(2)}, u32[]{:S(2)}) collective-permute-start(bf16[32,2048]{1,0:T(8,128)(2,1)S(1)} %get-tuple-element.36), channel_id=1, source_target_pairs={{0,6},{1,7},{2,4},{3,5},{4,2},{5,3},{6,0},{7,1},{8,14},{9,15},{10,... | collective-permute-start | bytes 393224 | tf_op jit(solution)/shard_map/ppermute | solution.py:185
  12.9 0.0 collective-permute-start.9
  12.9 0.8 %collective-permute-done.1.refs_3_ = bf16[32,2048]{1,0:T(8,128)(2,1)S(1)} collective-permute-done((bf16[32,2048]{1,0:T(8,128)(2,1)S(1)}, bf16[32,2048]{1,0:T(8,128)(2,1)S(1)}, u32[]{:S(2)}, u32[]{:S(2)}) %collective-permute-start.1) | collective-permute-done | bytes 131104 | tf_op jit(solution)/shard_map/ppermute | solution.py:185
  13.8 4.9 %collective-permute-start.10 = (bf16[32,2048]{1,0:T(8,128)(2,1)S(1)}, bf16[32,2048]{1,0:T(8,128)(2,1)S(1)}, u32[]{:S(2)}, u32[]{:S(2)}) collective-permute-start(bf16[32,2048]{1,0:T(8,128)(2,1)S(1)} %get-tuple-element.45), channel_id=1, source_target_pairs={{0,10},{1,11},{2,8},{3,9},{4,14},{5,15},{6,12},{7,13},{8,2},{9,3},... | collective-permute-start | bytes 393224 | tf_op jit(solution)/shard_map/ppermute | solution.py:185
  18.6 0.0 collective-permute-done.2.refs_1_
  18.6 0.4 collective-permute-start.11
  19.0 0.7 %copy-done.1 = s32[16,16]{1,0:T(8,128)S(1)} copy-done((s32[16,16]{1,0:T(8,128)S(1)}, s32[16,16]{1,0:T(8,128)}, u32[]{:S(2)}) %copy-start.1) | copy-done | bytes 1048
  19.7 4.4 %mask.1.masked_ref = bf16[2,8,128,2048]{3,2,1,0:T(8,128)(2,1)S(1)} custom-call(s32[1]{0:T(128)} %bitcast.me_ref, s32[16,16]{1,0:T(8,128)S(1)} %copy-done.1, bf16[2048,2048]{1,0:T(8,128)(2,1)} %rows_ref.1), custom_call_target="tpu_custom_call" | custom-call | flops 4194304 | bytes 16777216 | tf_op jit(solution)/shard_map/mask/pallas_call | solution.py:83
  24.2 0.0 collective-permute-done.3.refs_2_
  24.2 0.0 collective-permute-done.4.refs_3_
  24.2 1.3 %product.5 = f32[8,128,128]{2,1,0:T(8,128)S(1)} custom-call(s32[1]{0:T(128)} %bitcast.me_ref, bf16[2,8,128,2048]{3,2,1,0:T(8,128)(2,1)S(1)} %mask.1.masked_ref, bf16[32,2048]{1,0:T(8,128)(2,1)S(1)} %get-tuple-element.33.refs_0_, bf16[32,2048]{1,0:T(8,128)(2,1)S(1)} %collective-permute-done.2.refs_1_, bf16[32,2048]{1,0:T(8,128)(2,1)S(1)} %collective-permute-done.3.refs_2_, ...), custom_call_target="tpu_custom_call" | custom-call | bytes 9437188 | tf_op jit(solution)/shard_map/product/pallas_call | solution.py:24
  25.5 0.1 collective-permute-start.5
  25.6 1.3 %product.4.keep_ref = f32[8,128,128]{2,1,0:T(8,128)S(1)} custom-call(s32[1]{0:T(128)} %bitcast.me_ref, bf16[2,8,128,2048]{3,2,1,0:T(8,128)(2,1)S(1)} %mask.1.masked_ref, bf16[32,2048]{1,0:T(8,128)(2,1)S(1)} %get-tuple-element.33.refs_0_, bf16[32,2048]{1,0:T(8,128)(2,1)S(1)} %collective-permute-done.2.refs_1_, ...), custom_call_target="tpu_custom_call" | custom-call | bytes 9437188 | tf_op jit(solution)/shard_map/product/pallas_call | solution.py:24
  26.9 1.7 %collective-permute-done.9.refs_0_ = bf16[32,2048]{1,0:T(8,128)(2,1)S(1)} collective-permute-done((bf16[32,2048]{1,0:T(8,128)(2,1)S(1)}, bf16[32,2048]{1,0:T(8,128)(2,1)S(1)}, u32[]{:S(2)}, u32[]{:S(2)}) %collective-permute-start.9) | collective-permute-done | bytes 131104 | tf_op jit(solution)/shard_map/ppermute | solution.py:185
  28.5 2.8 %collective-permute-done.10.refs_1_ = bf16[32,2048]{1,0:T(8,128)(2,1)S(1)} collective-permute-done((bf16[32,2048]{1,0:T(8,128)(2,1)S(1)}, bf16[32,2048]{1,0:T(8,128)(2,1)S(1)}, u32[]{:S(2)}, u32[]{:S(2)}) %collective-permute-start.10) | collective-permute-done | bytes 131104 | tf_op jit(solution)/shard_map/ppermute | solution.py:185
  31.3 0.0 collective-permute-done.11.refs_2_
  31.3 1.3 %product.7 = f32[8,128,128]{2,1,0:T(8,128)S(1)} custom-call(s32[1]{0:T(128)} %bitcast.me_ref, bf16[2,8,128,2048]{3,2,1,0:T(8,128)(2,1)S(1)} %mask.1.masked_ref, bf16[32,2048]{1,0:T(8,128)(2,1)S(1)} %collective-permute-done.9.refs_0_, bf16[32,2048]{1,0:T(8,128)(2,1)S(1)} %collective-permute-done.10.refs_1_, ...), custom_call_target="tpu_custom_call" | custom-call | bytes 9437188 | tf_op jit(solution)/shard_map/product/pallas_call | solution.py:24
  32.6 0.0 copy-start.2
  32.6 0.1 collective-permute-start.12
  32.7 0.1 core_sum.2
  32.8 1.1 %collective-permute-start.6 = (s16[528,128]{1,0:T(8,128)(2,1)S(1)}, s16[528,128]{1,0:T(8,128)(2,1)S(1)}, u32[]{:S(2)}, u32[]{:S(2)}) collective-permute-start(s16[528,128]{1,0:T(8,128)(2,1)S(1)} %get-tuple-element.38), channel_id=1, source_target_pairs={{0,2},{1,3},{2,0},{3,1},{4,6},{5,7},{6,4},{7,5},{8,10},{9,11},{10,... | collective-permute-start | bytes 405512 | tf_op jit(solution)/shard_map/ppermute | solution.py:185
  34.0 1.3 %product.6.keep_ref = f32[8,128,128]{2,1,0:T(8,128)S(1)} custom-call(s32[1]{0:T(128)} %bitcast.me_ref, bf16[2,8,128,2048]{3,2,1,0:T(8,128)(2,1)S(1)} %mask.1.masked_ref, bf16[32,2048]{1,0:T(8,128)(2,1)S(1)} %collective-permute-done.9.refs_0_, bf16[32,2048]{1,0:T(8,128)(2,1)S(1)} %collective-permute-done.10.refs_1_, ...), custom_call_target="tpu_custom_call" | custom-call | bytes 9437188 | tf_op jit(solution)/shard_map/product/pallas_call | solution.py:24
  35.3 0.1 core_sum.3
  35.4 1.5 %collective-permute-start.13 = (s16[528,128]{1,0:T(8,128)(2,1)S(1)}, s16[528,128]{1,0:T(8,128)(2,1)S(1)}, u32[]{:S(2)}, u32[]{:S(2)}) collective-permute-start(s16[528,128]{1,0:T(8,128)(2,1)S(1)} %get-tuple-element.48), channel_id=1, source_target_pairs={{0,4},{1,5},{2,6},{3,7},{4,0},{5,1},{6,2},{7,3},{8,12},{9,13},{10,... | collective-permute-start | bytes 405512 | tf_op jit(solution)/shard_map/ppermute | solution.py:185
  36.9 2.0 %collective-permute-done.6.got_ref = s16[528,128]{1,0:T(8,128)(2,1)S(1)} collective-permute-done((s16[528,128]{1,0:T(8,128)(2,1)S(1)}, s16[528,128]{1,0:T(8,128)(2,1)S(1)}, u32[]{:S(2)}, u32[]{:S(2)}) %collective-permute-start.6) | collective-permute-done | bytes 135200 | tf_op jit(solution)/shard_map/ppermute | solution.py:185
  38.9 0.1 halve.4
  39.0 1.6 %collective-permute-start.7 = (s16[272,128]{1,0:T(8,128)(2,1)S(1)}, s16[272,128]{1,0:T(8,128)(2,1)S(1)}, u32[]{:S(2)}, u32[]{:S(2)}) collective-permute-start(s16[272,128]{1,0:T(8,128)(2,1)S(1)} %get-tuple-element.40), channel_id=1, source_target_pairs={{0,4},{1,5},{2,6},{3,7},{4,0},{5,1},{6,2},{7,3},{8,12},{9,13},{10,... | collective-permute-start | bytes 208904 | tf_op jit(solution)/shard_map/ppermute | solution.py:185
  40.6 0.6 %collective-permute-done.13.got_ref = s16[528,128]{1,0:T(8,128)(2,1)S(1)} collective-permute-done((s16[528,128]{1,0:T(8,128)(2,1)S(1)}, s16[528,128]{1,0:T(8,128)(2,1)S(1)}, u32[]{:S(2)}, u32[]{:S(2)}) %collective-permute-start.13) | collective-permute-done | bytes 135200 | tf_op jit(solution)/shard_map/ppermute | solution.py:185
  41.2 0.1 halve.6
  41.3 1.0 %collective-permute-start.14 = (s16[272,128]{1,0:T(8,128)(2,1)S(1)}, s16[272,128]{1,0:T(8,128)(2,1)S(1)}, u32[]{:S(2)}, u32[]{:S(2)}) collective-permute-start(s16[272,128]{1,0:T(8,128)(2,1)S(1)} %get-tuple-element.50), channel_id=1, source_target_pairs={{0,2},{1,3},{2,0},{3,1},{4,6},{5,7},{6,4},{7,5},{8,10},{9,11},{10,... | collective-permute-start | bytes 208904 | tf_op jit(solution)/shard_map/ppermute | solution.py:185
  42.3 1.1 %collective-permute-done.7.got_ref = s16[272,128]{1,0:T(8,128)(2,1)S(1)} collective-permute-done((s16[272,128]{1,0:T(8,128)(2,1)S(1)}, s16[272,128]{1,0:T(8,128)(2,1)S(1)}, u32[]{:S(2)}, u32[]{:S(2)}) %collective-permute-start.7) | collective-permute-done | bytes 69664 | tf_op jit(solution)/shard_map/ppermute | solution.py:185
  43.3 0.1 halve.5
  43.4 2.4 %collective-permute-start.8 = (s16[144,128]{1,0:T(8,128)(2,1)S(1)}, s16[144,128]{1,0:T(8,128)(2,1)S(1)}, u32[]{:S(2)}, u32[]{:S(2)}) collective-permute-start(s16[144,128]{1,0:T(8,128)(2,1)S(1)} %get-tuple-element.42), channel_id=1, source_target_pairs={{0,8},{1,9},{2,10},{3,11},{4,12},{5,13},{6,14},{7,15},{8,0},{9,1},... | collective-permute-start | bytes 110600 | tf_op jit(solution)/shard_map/ppermute | solution.py:185
  45.8 0.1 halve.7
  45.9 1.6 %collective-permute-start.15 = (s16[144,128]{1,0:T(8,128)(2,1)S(1)}, s16[144,128]{1,0:T(8,128)(2,1)S(1)}, u32[]{:S(2)}, u32[]{:S(2)}) collective-permute-start(s16[144,128]{1,0:T(8,128)(2,1)S(1)} %get-tuple-element.52), channel_id=1, source_target_pairs={{0,8},{1,9},{2,10},{3,11},{4,12},{5,13},{6,14},{7,15},{8,0},{9,1},... | collective-permute-start | bytes 110600 | tf_op jit(solution)/shard_map/ppermute | solution.py:185
  47.5 0.1 copy.5.places_ref
  47.7 0.1 place.1.place_ref
  47.8 0.7 %collective-permute-done.8.near_got = s16[144,128]{1,0:T(8,128)(2,1)S(1)} collective-permute-done((s16[144,128]{1,0:T(8,128)(2,1)S(1)}, s16[144,128]{1,0:T(8,128)(2,1)S(1)}, u32[]{:S(2)}, u32[]{:S(2)}) %collective-permute-start.8) | collective-permute-done | bytes 36896 | tf_op jit(solution)/shard_map/ppermute | solution.py:185
  48.5 2.3 %collective-permute-done.15.far_got = s16[144,128]{1,0:T(8,128)(2,1)S(1)} collective-permute-done((s16[144,128]{1,0:T(8,128)(2,1)S(1)}, s16[144,128]{1,0:T(8,128)(2,1)S(1)}, u32[]{:S(2)}, u32[]{:S(2)}) %collective-permute-start.15) | collective-permute-done | bytes 36896 | tf_op jit(solution)/shard_map/ppermute | solution.py:185
  50.8 0.9 %last.1 = f32[128,256]{1,0:T(8,128)} custom-call(f32[1,128,128]{2,1,0:T(8,128)S(1)} %get-tuple-element.41.near_keep, s16[144,128]{1,0:T(8,128)(2,1)S(1)} %collective-permute-done.8.near_got, f32[1,128,128]{2,1,0:T(8,128)S(1)} %get-tuple-element.51.far_keep, s16[144,128]{1,0:T(8,128)(2,1)S(1)} %collective-permute-done.15.far_got, ...), custom_call_target="tpu_custom_call" | custom-call | bytes 729088 | tf_op jit(solution)/shard_map/last/pallas_call | solution.py:24
  (6 shorter events, 0.0 us)
Async XLA Ops:
  0.0 1.2 %copy-start = (bf16[16,32768]{1,0:T(8,128)(2,1)S(1)}, bf16[16,32768]{1,0:T(8,128)(2,1)}, u32[]{:S(2)}) copy-start(bf16[16,32768]{1,0:T(8,128)(2,1)} %amplitudes_ref.1) | copy-start | bytes 3145732
  1.3 2.1 %collective-permute-start = (bf16[8,16,2048]{2,1,0:T(8,128)(2,1)S(1)}, bf16[8,16,2048]{2,1,0:T(8,128)(2,1)S(1)}, u32[]{:S(2)}, u32[]{:S(2)}) collective-permute-start(bf16[8,16,2048]{2,1,0:T(8,128)(2,1)S(1)} %get-tuple-element.30), channel_id=1, source_target_pairs={{0,1},{1,0},{2,3},{3,2},{4,5},{5,4},{6,7},{7,6},{8,9},{9,8},{10,11... | collective-permute-start | bytes 1572872 | tf_op jit(solution)/shard_map/ppermute | solution.py:185
  3.4 10.3 %collective-permute-start.1 = (bf16[32,2048]{1,0:T(8,128)(2,1)S(1)}, bf16[32,2048]{1,0:T(8,128)(2,1)S(1)}, u32[]{:S(2)}, u32[]{:S(2)}) collective-permute-start(bf16[32,2048]{1,0:T(8,128)(2,1)S(1)} %get-tuple-element.31), channel_id=1, source_target_pairs={{0,14},{1,15},{2,12},{3,13},{4,10},{5,11},{6,8},{7,9},{8,6},{9,7},... | collective-permute-start | bytes 393224 | tf_op jit(solution)/shard_map/ppermute | solution.py:185
  9.4 9.2 %collective-permute-start.2 = (bf16[32,2048]{1,0:T(8,128)(2,1)S(1)}, bf16[32,2048]{1,0:T(8,128)(2,1)S(1)}, u32[]{:S(2)}, u32[]{:S(2)}) collective-permute-start(bf16[32,2048]{1,0:T(8,128)(2,1)S(1)} %get-tuple-element.34), channel_id=1, source_target_pairs={{0,2},{1,3},{2,0},{3,1},{4,6},{5,7},{6,4},{7,5},{8,10},{9,11},{10,... | collective-permute-start | bytes 393224 | tf_op jit(solution)/shard_map/ppermute | solution.py:185
  9.9 14.2 %collective-permute-start.3 = (bf16[32,2048]{1,0:T(8,128)(2,1)S(1)}, bf16[32,2048]{1,0:T(8,128)(2,1)S(1)}, u32[]{:S(2)}, u32[]{:S(2)}) collective-permute-start(bf16[32,2048]{1,0:T(8,128)(2,1)S(1)} %get-tuple-element.35), channel_id=1, source_target_pairs={{0,4},{1,5},{2,6},{3,7},{4,0},{5,1},{6,2},{7,3},{8,12},{9,13},{10,... | collective-permute-start | bytes 393224 | tf_op jit(solution)/shard_map/ppermute | solution.py:185
  9.9 14.2 %collective-permute-start.4 = (bf16[32,2048]{1,0:T(8,128)(2,1)S(1)}, bf16[32,2048]{1,0:T(8,128)(2,1)S(1)}, u32[]{:S(2)}, u32[]{:S(2)}) collective-permute-start(bf16[32,2048]{1,0:T(8,128)(2,1)S(1)} %get-tuple-element.36), channel_id=1, source_target_pairs={{0,6},{1,7},{2,4},{3,5},{4,2},{5,3},{6,0},{7,1},{8,14},{9,15},{10,... | collective-permute-start | bytes 393224 | tf_op jit(solution)/shard_map/ppermute | solution.py:185
  12.9 15.6 %collective-permute-start.9 = (bf16[32,2048]{1,0:T(8,128)(2,1)S(1)}, bf16[32,2048]{1,0:T(8,128)(2,1)S(1)}, u32[]{:S(2)}, u32[]{:S(2)}) collective-permute-start(bf16[32,2048]{1,0:T(8,128)(2,1)S(1)} %get-tuple-element.44), channel_id=1, source_target_pairs={{0,8},{1,9},{2,10},{3,11},{4,12},{5,13},{6,14},{7,15},{8,0},{9,1},... | collective-permute-start | bytes 393224 | tf_op jit(solution)/shard_map/ppermute | solution.py:185
  13.8 17.6 %collective-permute-start.10 = (bf16[32,2048]{1,0:T(8,128)(2,1)S(1)}, bf16[32,2048]{1,0:T(8,128)(2,1)S(1)}, u32[]{:S(2)}, u32[]{:S(2)}) collective-permute-start(bf16[32,2048]{1,0:T(8,128)(2,1)S(1)} %get-tuple-element.45), channel_id=1, source_target_pairs={{0,10},{1,11},{2,8},{3,9},{4,14},{5,15},{6,12},{7,13},{8,2},{9,3},... | collective-permute-start | bytes 393224 | tf_op jit(solution)/shard_map/ppermute | solution.py:185
  18.6 12.7 %collective-permute-start.11 = (bf16[32,2048]{1,0:T(8,128)(2,1)S(1)}, bf16[32,2048]{1,0:T(8,128)(2,1)S(1)}, u32[]{:S(2)}, u32[]{:S(2)}) collective-permute-start(bf16[32,2048]{1,0:T(8,128)(2,1)S(1)} %get-tuple-element.46), channel_id=1, source_target_pairs={{0,12},{1,13},{2,14},{3,15},{4,8},{5,9},{6,10},{7,11},{8,4},{9,5},... | collective-permute-start | bytes 393224 | tf_op jit(solution)/shard_map/ppermute | solution.py:185
  19.0 0.7 %copy-start.1 = (s32[16,16]{1,0:T(8,128)S(1)}, s32[16,16]{1,0:T(8,128)}, u32[]{:S(2)}) copy-start(s32[16,16]{1,0:T(8,128)} %mask_ref.1) | copy-start | bytes 3076
  25.5 7.2 %collective-permute-start.5 = (f32[8,128,128]{2,1,0:T(8,128)S(1)}, f32[8,128,128]{2,1,0:T(8,128)S(1)}, u32[]{:S(2)}, u32[]{:S(2)}) collective-permute-start(f32[8,128,128]{2,1,0:T(8,128)S(1)} %product.5), channel_id=1, source_target_pairs={{0,1},{1,0},{2,3},{3,2},{4,5},{5,4},{6,7},{7,6},{8,9},{9,8},{10,11... | collective-permute-start | bytes 1572872 | tf_op jit(solution)/shard_map/ppermute | solution.py:185
  32.6 14.9 %copy-start.2 = (s32[256]{0:T(256)S(1)}, s32[256]{0:T(256)}, u32[]{:S(2)}) copy-start(s32[256]{0:T(256)} %param.7) | copy-start | bytes 3076
  32.6 2.7 %collective-permute-start.12 = (f32[8,128,128]{2,1,0:T(8,128)S(1)}, f32[8,128,128]{2,1,0:T(8,128)S(1)}, u32[]{:S(2)}, u32[]{:S(2)}) collective-permute-start(f32[8,128,128]{2,1,0:T(8,128)S(1)} %product.7), channel_id=1, source_target_pairs={{0,1},{1,0},{2,3},{3,2},{4,5},{5,4},{6,7},{7,6},{8,9},{9,8},{10,11... | collective-permute-start | bytes 1572872 | tf_op jit(solution)/shard_map/ppermute | solution.py:185
  32.8 6.0 %collective-permute-start.6 = (s16[528,128]{1,0:T(8,128)(2,1)S(1)}, s16[528,128]{1,0:T(8,128)(2,1)S(1)}, u32[]{:S(2)}, u32[]{:S(2)}) collective-permute-start(s16[528,128]{1,0:T(8,128)(2,1)S(1)} %get-tuple-element.38), channel_id=1, source_target_pairs={{0,2},{1,3},{2,0},{3,1},{4,6},{5,7},{6,4},{7,5},{8,10},{9,11},{10,... | collective-permute-start | bytes 405512 | tf_op jit(solution)/shard_map/ppermute | solution.py:185
  35.4 5.8 %collective-permute-start.13 = (s16[528,128]{1,0:T(8,128)(2,1)S(1)}, s16[528,128]{1,0:T(8,128)(2,1)S(1)}, u32[]{:S(2)}, u32[]{:S(2)}) collective-permute-start(s16[528,128]{1,0:T(8,128)(2,1)S(1)} %get-tuple-element.48), channel_id=1, source_target_pairs={{0,4},{1,5},{2,6},{3,7},{4,0},{5,1},{6,2},{7,3},{8,12},{9,13},{10,... | collective-permute-start | bytes 405512 | tf_op jit(solution)/shard_map/ppermute | solution.py:185
  39.0 4.4 %collective-permute-start.7 = (s16[272,128]{1,0:T(8,128)(2,1)S(1)}, s16[272,128]{1,0:T(8,128)(2,1)S(1)}, u32[]{:S(2)}, u32[]{:S(2)}) collective-permute-start(s16[272,128]{1,0:T(8,128)(2,1)S(1)} %get-tuple-element.40), channel_id=1, source_target_pairs={{0,4},{1,5},{2,6},{3,7},{4,0},{5,1},{6,2},{7,3},{8,12},{9,13},{10,... | collective-permute-start | bytes 208904 | tf_op jit(solution)/shard_map/ppermute | solution.py:185
  41.3 4.5 %collective-permute-start.14 = (s16[272,128]{1,0:T(8,128)(2,1)S(1)}, s16[272,128]{1,0:T(8,128)(2,1)S(1)}, u32[]{:S(2)}, u32[]{:S(2)}) collective-permute-start(s16[272,128]{1,0:T(8,128)(2,1)S(1)} %get-tuple-element.50), channel_id=1, source_target_pairs={{0,2},{1,3},{2,0},{3,1},{4,6},{5,7},{6,4},{7,5},{8,10},{9,11},{10,... | collective-permute-start | bytes 208904 | tf_op jit(solution)/shard_map/ppermute | solution.py:185
  43.4 5.1 %collective-permute-start.8 = (s16[144,128]{1,0:T(8,128)(2,1)S(1)}, s16[144,128]{1,0:T(8,128)(2,1)S(1)}, u32[]{:S(2)}, u32[]{:S(2)}) collective-permute-start(s16[144,128]{1,0:T(8,128)(2,1)S(1)} %get-tuple-element.42), channel_id=1, source_target_pairs={{0,8},{1,9},{2,10},{3,11},{4,12},{5,13},{6,14},{7,15},{8,0},{9,1},... | collective-permute-start | bytes 110600 | tf_op jit(solution)/shard_map/ppermute | solution.py:185
  45.9 4.9 %collective-permute-start.15 = (s16[144,128]{1,0:T(8,128)(2,1)S(1)}, s16[144,128]{1,0:T(8,128)(2,1)S(1)}, u32[]{:S(2)}, u32[]{:S(2)}) collective-permute-start(s16[144,128]{1,0:T(8,128)(2,1)S(1)} %get-tuple-element.52), channel_id=1, source_target_pairs={{0,8},{1,9},{2,10},{3,11},{4,12},{5,13},{6,14},{7,15},{8,0},{9,1},... | collective-permute-start | bytes 110600 | tf_op jit(solution)/shard_map/ppermute | solution.py:185

commit v8 on v7

--- a/solution.py
+++ b/solution.py
@@ -164,10 +164,26 @@
             out_ref[start : start + pairs] = ones
 
 
-def last_kernel(near_keep, near_got, far_keep, far_got, place_ref, out_ref):
-    parts = []
-    for keep_ref, got_ref in ((near_keep, far_got), (far_keep, near_got)):
-        rest = keep_ref[0] + unpack(got_ref)[0]
+def split_kernel(keep_ref, got_ref, *outs):
+    got = unpack(got_ref)
+    for index, out in enumerate(outs):
+        if index:
+            pack([keep_ref[index] + got[index]], out)
+        else:
+            out[0] = keep_ref[0] + got[0]
+
+
+def last_kernel(counts, *refs):
+    *sums, place_ref, out_ref = refs
+    parts, start = [], 2
+    received = []
+    for count in counts:
+        received.append(sums[start : start + count])
+        start += count
+    for c in range(2):
+        rest = sums[c][0]
+        for got_ref in received[c]:
+            rest += unpack(got_ref)[0]
         for _ in range(3):
             parts.append(rest.astype(jnp.bfloat16))
             rest = rest - parts[-1].astype(jnp.float32)
@@ -203,8 +219,8 @@
     half = chips // 2
     bits = tuple(range((chips - 1).bit_length()))
 
-    sums = []
-    for first, order in ((0, bits), (half, bits[-2::-1] + bits[-1:])):
+    sums, parts = [], ([], [])
+    for first, order in ((0, bits[-2::-1] + bits[-1:]), (half, bits)):
         send, keep = [
             call(
                 functools.partial(product_kernel, slot), "product", [plain(chips, pairs)], me, masked,
@@ -220,16 +236,29 @@
             functools.partial(first_kernel, order), "core_sum", [packed(blocks, pairs), plain(blocks, pairs)],
             keep, got,
         )
-        for bit in order:
+        which = 0 if first == 0 else 1
+        for bit in order[:-2]:
             got = swap(send, 2 << bit)
-            if blocks > 1:
+            if blocks > 4:
                 blocks //= 2
-                send, keep = call(
-                    halve_kernel, "halve", [packed(blocks, pairs), plain(blocks, pairs)],
-                    keep, got,
-                )
-        sums += [keep, got]
-    return call(last_kernel, "last", [jax.ShapeDtypeStruct((TILE, 2 * pairs), jnp.float32)], *sums, place)[0]
+                send, keep = call(halve_kernel, "halve", [packed(blocks, pairs), plain(blocks, pairs)], keep, got)
+        one, last = 2 << order[-2], 2 << order[-1]
+        if which in (1,):
+            keep, *sends = call(
+                split_kernel, "split", [plain(1, pairs)] + [packed(1, pairs)] * 3, keep, got
+            )
+            for send, to in zip(sends, (last, one, one + last), strict=True):
+                parts[which ^ (to >= last)].append(swap(send, to))
+        else:
+            send, keep = call(halve_kernel, "halve", [packed(2, pairs), plain(2, pairs)], keep, got)
+            got = swap(send, one)
+            send, keep = call(halve_kernel, "halve", [packed(1, pairs), plain(1, pairs)], keep, got)
+            parts[1 - which].append(swap(send, last))
+        sums.append(keep)
+    return call(
+        functools.partial(last_kernel, [len(p) for p in parts]), "last",
+        [jax.ShapeDtypeStruct((TILE, 2 * pairs), jnp.float32)], *sums, *parts[0], *parts[1], place,
+    )[0]
 
 
 def solution(mesh):

time: 51.9 us -> 51.7 us (level)
    ppermute x16 -> x17, starting transfers between devices: 24.7 us -> 24.5 us  [swap(): return lax.ppermute(value, 'ab', [(i, i ^ bits) for i in range(devices)])]
    ppermute x16 -> x17, waiting for transfers between devices: 13.4 us -> 13.5 us  [swap(): return lax.ppermute(value, 'ab', [(i, i ^ bits) for i in range(devices)])]
    pallas_call x14 -> x13, Pallas kernels: 6.8 us -> 6.76 us  [call(): pl.pallas_call(kernel, out_shape=outs, in_specs=[SCALARS] * scalars + [WH...]
  transfers between devices with their start and end apart: 16 -> 17, of which waited for: 9 -> 8; matrix products, arithmetic and copies ran while one was open for 0% -> 0% of each run, Pallas kernels for 20% -> 20%
where the time goes in v8:
time: 51.7 us; the launch traced here: 51.5 us
  starting transfers between devices  24.5 us (47%)
  waiting for transfers between devices  13.5 us (26%)
  Pallas kernels  11.2 us (22%)
  local copies, waits for them, and re-layouts  2.06 us (4%)
    ppermute x17, starting transfers between devices, swap(): return lax.ppermute(value, 'ab', [(i, i ^ bits) for i in range(devices)])  24.5 us
    ppermute x17, waiting for transfers between devices, swap(): return lax.ppermute(value, 'ab', [(i, i ^ bits) for i in range(devices)])  13.5 us
    pallas_call x13, Pallas kernels, call(): pl.pallas_call(kernel, out_shape=outs, in_specs=[SCALARS] * scalars + [WH...  6.76 us
    pallas_call x1, Pallas kernels, masked_rows(): pl.pallas_call(mask_kernel, in_specs=[SCALARS, SCALARS, pl.BlockSpec(memo...  4.45 us
    unnamed x6, local copies, waits for them, and re-layouts  1.93 us
  transfers between devices with their start and end apart: 17, of which 8 were waited for; matrix products, arithmetic and copies ran while one was open for 0% of the time, Pallas kernels for 20%

profile of v8, /device:TPU:0, one launch (start us, length us, event | category | flops | bytes accessed | tf_op | source)
XLA Modules:
  0.0 51.5 jit_solution(11905965277400613881)
XLA Ops:
  0.0 1.2 %copy-done = bf16[16,32768]{1,0:T(8,128)(2,1)S(1)} copy-done((bf16[16,32768]{1,0:T(8,128)(2,1)S(1)}, bf16[16,32768]{1,0:T(8,128)(2,1)}, u32[]{:S(2)}) %copy-start) | copy-done | bytes 1048600
  1.2 0.1 sort.1
  1.3 0.5 %collective-permute-start = (bf16[8,16,2048]{2,1,0:T(8,128)(2,1)S(1)}, bf16[8,16,2048]{2,1,0:T(8,128)(2,1)S(1)}, u32[]{:S(2)}, u32[]{:S(2)}) collective-permute-start(bf16[8,16,2048]{2,1,0:T(8,128)(2,1)S(1)} %get-tuple-element.30), channel_id=1, source_target_pairs={{0,1},{1,0},{2,3},{3,2},{4,5},{5,4},{6,7},{7,6},{8,9},{9,8},{10,11... | collective-permute-start | bytes 1572872 | tf_op jit(solution)/shard_map/ppermute | solution.py:201
  1.8 1.5 %collective-permute-done.got_ref = bf16[8,16,2048]{2,1,0:T(8,128)(2,1)S(1)} collective-permute-done((bf16[8,16,2048]{2,1,0:T(8,128)(2,1)S(1)}, bf16[8,16,2048]{2,1,0:T(8,128)(2,1)S(1)}, u32[]{:S(2)}, u32[]{:S(2)}) %collective-permute-start) | collective-permute-done | bytes 524320 | tf_op jit(solution)/shard_map/ppermute | solution.py:201
  3.4 0.1 pieces.1
  3.4 6.0 %collective-permute-start.1 = (bf16[32,2048]{1,0:T(8,128)(2,1)S(1)}, bf16[32,2048]{1,0:T(8,128)(2,1)S(1)}, u32[]{:S(2)}, u32[]{:S(2)}) collective-permute-start(bf16[32,2048]{1,0:T(8,128)(2,1)S(1)} %get-tuple-element.31), channel_id=1, source_target_pairs={{0,14},{1,15},{2,12},{3,13},{4,10},{5,11},{6,8},{7,9},{8,6},{9,7},... | collective-permute-start | bytes 393224 | tf_op jit(solution)/shard_map/ppermute | solution.py:201
  9.4 0.5 collective-permute-start.2
  9.9 0.0 collective-permute-start.3
  9.9 3.0 %collective-permute-start.4 = (bf16[32,2048]{1,0:T(8,128)(2,1)S(1)}, bf16[32,2048]{1,0:T(8,128)(2,1)S(1)}, u32[]{:S(2)}, u32[]{:S(2)}) collective-permute-start(bf16[32,2048]{1,0:T(8,128)(2,1)S(1)} %get-tuple-element.36), channel_id=1, source_target_pairs={{0,6},{1,7},{2,4},{3,5},{4,2},{5,3},{6,0},{7,1},{8,14},{9,15},{10,... | collective-permute-start | bytes 393224 | tf_op jit(solution)/shard_map/ppermute | solution.py:201
  12.9 0.8 %collective-permute-done.1.refs_3_ = bf16[32,2048]{1,0:T(8,128)(2,1)S(1)} collective-permute-done((bf16[32,2048]{1,0:T(8,128)(2,1)S(1)}, bf16[32,2048]{1,0:T(8,128)(2,1)S(1)}, u32[]{:S(2)}, u32[]{:S(2)}) %collective-permute-start.1) | collective-permute-done | bytes 131104 | tf_op jit(solution)/shard_map/ppermute | solution.py:201
  13.8 4.9 %collective-permute-start.9 = (bf16[32,2048]{1,0:T(8,128)(2,1)S(1)}, bf16[32,2048]{1,0:T(8,128)(2,1)S(1)}, u32[]{:S(2)}, u32[]{:S(2)}) collective-permute-start(bf16[32,2048]{1,0:T(8,128)(2,1)S(1)} %get-tuple-element.44), channel_id=1, source_target_pairs={{0,10},{1,11},{2,8},{3,9},{4,14},{5,15},{6,12},{7,13},{8,2},{9,3},... | collective-permute-start | bytes 393224 | tf_op jit(solution)/shard_map/ppermute | solution.py:201
  18.6 0.0 collective-permute-done.2.refs_1_
  18.6 0.4 collective-permute-start.10
  19.0 0.7 %copy-done.1 = s32[16,16]{1,0:T(8,128)S(1)} copy-done((s32[16,16]{1,0:T(8,128)S(1)}, s32[16,16]{1,0:T(8,128)}, u32[]{:S(2)}) %copy-start.1) | copy-done | bytes 1048
  19.7 4.4 %mask.1.masked_ref = bf16[2,8,128,2048]{3,2,1,0:T(8,128)(2,1)S(1)} custom-call(s32[1]{0:T(128)} %bitcast.me_ref, s32[16,16]{1,0:T(8,128)S(1)} %copy-done.1, bf16[2048,2048]{1,0:T(8,128)(2,1)} %rows_ref.1), custom_call_target="tpu_custom_call" | custom-call | flops 4194304 | bytes 16777216 | tf_op jit(solution)/shard_map/mask/pallas_call | solution.py:83
  24.2 0.0 collective-permute-done.4.refs_3_
  24.2 1.3 %product.5 = f32[8,128,128]{2,1,0:T(8,128)S(1)} custom-call(s32[1]{0:T(128)} %bitcast.me_ref, bf16[2,8,128,2048]{3,2,1,0:T(8,128)(2,1)S(1)} %mask.1.masked_ref, bf16[32,2048]{1,0:T(8,128)(2,1)S(1)} %get-tuple-element.33.refs_0_, bf16[32,2048]{1,0:T(8,128)(2,1)S(1)} %collective-permute-done.2.refs_1_, bf16[32,2048]{1,0:T(8,128)(2,1)S(1)} %collective-permute-done.3.refs_2_, ...), custom_call_target="tpu_custom_call" | custom-call | bytes 9437188 | tf_op jit(solution)/shard_map/product/pallas_call | solution.py:24
  25.5 0.1 collective-permute-start.5
  25.6 1.3 %product.4.keep_ref = f32[8,128,128]{2,1,0:T(8,128)S(1)} custom-call(s32[1]{0:T(128)} %bitcast.me_ref, bf16[2,8,128,2048]{3,2,1,0:T(8,128)(2,1)S(1)} %mask.1.masked_ref, bf16[32,2048]{1,0:T(8,128)(2,1)S(1)} %get-tuple-element.33.refs_0_, bf16[32,2048]{1,0:T(8,128)(2,1)S(1)} %collective-permute-done.2.refs_1_, ...), custom_call_target="tpu_custom_call" | custom-call | bytes 9437188 | tf_op jit(solution)/shard_map/product/pallas_call | solution.py:24
  26.9 1.7 %collective-permute-done.8.refs_0_ = bf16[32,2048]{1,0:T(8,128)(2,1)S(1)} collective-permute-done((bf16[32,2048]{1,0:T(8,128)(2,1)S(1)}, bf16[32,2048]{1,0:T(8,128)(2,1)S(1)}, u32[]{:S(2)}, u32[]{:S(2)}) %collective-permute-start.8) | collective-permute-done | bytes 131104 | tf_op jit(solution)/shard_map/ppermute | solution.py:201
  28.5 2.8 %collective-permute-done.9.refs_1_ = bf16[32,2048]{1,0:T(8,128)(2,1)S(1)} collective-permute-done((bf16[32,2048]{1,0:T(8,128)(2,1)S(1)}, bf16[32,2048]{1,0:T(8,128)(2,1)S(1)}, u32[]{:S(2)}, u32[]{:S(2)}) %collective-permute-start.9) | collective-permute-done | bytes 131104 | tf_op jit(solution)/shard_map/ppermute | solution.py:201
  31.3 1.3 %product.7 = f32[8,128,128]{2,1,0:T(8,128)S(1)} custom-call(s32[1]{0:T(128)} %bitcast.me_ref, bf16[2,8,128,2048]{3,2,1,0:T(8,128)(2,1)S(1)} %mask.1.masked_ref, bf16[32,2048]{1,0:T(8,128)(2,1)S(1)} %collective-permute-done.8.refs_0_, bf16[32,2048]{1,0:T(8,128)(2,1)S(1)} %collective-permute-done.9.refs_1_, ...), custom_call_target="tpu_custom_call" | custom-call | bytes 9437188 | tf_op jit(solution)/shard_map/product/pallas_call | solution.py:24
  32.6 0.0 copy-start.2
  32.6 0.1 collective-permute-start.11
  32.7 0.0 collective-permute-done.5.got_ref
  32.7 0.1 core_sum.2
  32.8 1.6 %collective-permute-start.6 = (s16[528,128]{1,0:T(8,128)(2,1)S(1)}, s16[528,128]{1,0:T(8,128)(2,1)S(1)}, u32[]{:S(2)}, u32[]{:S(2)}) collective-permute-start(s16[528,128]{1,0:T(8,128)(2,1)S(1)} %get-tuple-element.38), channel_id=1, source_target_pairs={{0,4},{1,5},{2,6},{3,7},{4,0},{5,1},{6,2},{7,3},{8,12},{9,13},{10,... | collective-permute-start | bytes 405512 | tf_op jit(solution)/shard_map/ppermute | solution.py:201
  34.5 1.3 %product.6.keep_ref = f32[8,128,128]{2,1,0:T(8,128)S(1)} custom-call(s32[1]{0:T(128)} %bitcast.me_ref, bf16[2,8,128,2048]{3,2,1,0:T(8,128)(2,1)S(1)} %mask.1.masked_ref, bf16[32,2048]{1,0:T(8,128)(2,1)S(1)} %collective-permute-done.8.refs_0_, bf16[32,2048]{1,0:T(8,128)(2,1)S(1)} %collective-permute-done.9.refs_1_, ...), custom_call_target="tpu_custom_call" | custom-call | bytes 9437188 | tf_op jit(solution)/shard_map/product/pallas_call | solution.py:24
  35.8 0.1 core_sum.3
  35.9 1.0 %collective-permute-start.12 = (s16[528,128]{1,0:T(8,128)(2,1)S(1)}, s16[528,128]{1,0:T(8,128)(2,1)S(1)}, u32[]{:S(2)}, u32[]{:S(2)}) collective-permute-start(s16[528,128]{1,0:T(8,128)(2,1)S(1)} %get-tuple-element.47), channel_id=1, source_target_pairs={{0,2},{1,3},{2,0},{3,1},{4,6},{5,7},{6,4},{7,5},{8,10},{9,11},{10,... | collective-permute-start | bytes 405512 | tf_op jit(solution)/shard_map/ppermute | solution.py:201
  36.9 2.0 %collective-permute-done.6.got_ref = s16[528,128]{1,0:T(8,128)(2,1)S(1)} collective-permute-done((s16[528,128]{1,0:T(8,128)(2,1)S(1)}, s16[528,128]{1,0:T(8,128)(2,1)S(1)}, u32[]{:S(2)}, u32[]{:S(2)}) %collective-permute-start.6) | collective-permute-done | bytes 135200 | tf_op jit(solution)/shard_map/ppermute | solution.py:201
  38.9 0.1 halve.2
  39.0 1.1 %collective-permute-start.7 = (s16[272,128]{1,0:T(8,128)(2,1)S(1)}, s16[272,128]{1,0:T(8,128)(2,1)S(1)}, u32[]{:S(2)}, u32[]{:S(2)}) collective-permute-start(s16[272,128]{1,0:T(8,128)(2,1)S(1)} %get-tuple-element.40), channel_id=1, source_target_pairs={{0,2},{1,3},{2,0},{3,1},{4,6},{5,7},{6,4},{7,5},{8,10},{9,11},{10,... | collective-permute-start | bytes 208904 | tf_op jit(solution)/shard_map/ppermute | solution.py:201
  40.1 1.8 %collective-permute-done.12.got_ref = s16[528,128]{1,0:T(8,128)(2,1)S(1)} collective-permute-done((s16[528,128]{1,0:T(8,128)(2,1)S(1)}, s16[528,128]{1,0:T(8,128)(2,1)S(1)}, u32[]{:S(2)}, u32[]{:S(2)}) %collective-permute-start.12) | collective-permute-done | bytes 135200 | tf_op jit(solution)/shard_map/ppermute | solution.py:201
  42.0 0.1 split.1
  42.1 0.9 %collective-permute-start.13 = (s16[144,128]{1,0:T(8,128)(2,1)S(1)}, s16[144,128]{1,0:T(8,128)(2,1)S(1)}, u32[]{:S(2)}, u32[]{:S(2)}) collective-permute-start(s16[144,128]{1,0:T(8,128)(2,1)S(1)} %get-tuple-element.49), channel_id=1, source_target_pairs={{0,8},{1,9},{2,10},{3,11},{4,12},{5,13},{6,14},{7,15},{8,0},{9,1},... | collective-permute-start | bytes 110600 | tf_op jit(solution)/shard_map/ppermute | solution.py:201
  42.9 1.7 %collective-permute-start.14 = (s16[144,128]{1,0:T(8,128)(2,1)S(1)}, s16[144,128]{1,0:T(8,128)(2,1)S(1)}, u32[]{:S(2)}, u32[]{:S(2)}) collective-permute-start(s16[144,128]{1,0:T(8,128)(2,1)S(1)} %get-tuple-element.50), channel_id=1, source_target_pairs={{0,12},{1,13},{2,14},{3,15},{4,8},{5,9},{6,10},{7,11},{8,4},{9,5},... | collective-permute-start | bytes 110600 | tf_op jit(solution)/shard_map/ppermute | solution.py:201
  44.7 1.0 %collective-permute-start.16 = (s16[144,128]{1,0:T(8,128)(2,1)S(1)}, s16[144,128]{1,0:T(8,128)(2,1)S(1)}, u32[]{:S(2)}, u32[]{:S(2)}) collective-permute-start(s16[144,128]{1,0:T(8,128)(2,1)S(1)} %get-tuple-element.52), channel_id=1, source_target_pairs={{0,4},{1,5},{2,6},{3,7},{4,0},{5,1},{6,2},{7,3},{8,12},{9,13},{10,... | collective-permute-start | bytes 110600 | tf_op jit(solution)/shard_map/ppermute | solution.py:201
  45.6 0.0 collective-permute-done.7.got_ref
  45.6 0.1 halve.3
  45.7 1.8 %collective-permute-start.15 = (s16[144,128]{1,0:T(8,128)(2,1)S(1)}, s16[144,128]{1,0:T(8,128)(2,1)S(1)}, u32[]{:S(2)}, u32[]{:S(2)}) collective-permute-start(s16[144,128]{1,0:T(8,128)(2,1)S(1)} %get-tuple-element.51), channel_id=1, source_target_pairs={{0,8},{1,9},{2,10},{3,11},{4,12},{5,13},{6,14},{7,15},{8,0},{9,1},... | collective-permute-start | bytes 110600 | tf_op jit(solution)/shard_map/ppermute | solution.py:201
  47.4 0.1 copy.5.places_ref
  47.6 0.1 place.1.refs_6_
  47.7 0.0 collective-permute-done.13.refs_2_
  47.7 1.4 %collective-permute-done.14.refs_3_ = s16[144,128]{1,0:T(8,128)(2,1)S(1)} collective-permute-done((s16[144,128]{1,0:T(8,128)(2,1)S(1)}, s16[144,128]{1,0:T(8,128)(2,1)S(1)}, u32[]{:S(2)}, u32[]{:S(2)}) %collective-permute-start.14) | collective-permute-done | bytes 36896 | tf_op jit(solution)/shard_map/ppermute | solution.py:201
  49.1 0.0 collective-permute-done.16.refs_5_
  49.1 1.5 %collective-permute-done.15.refs_4_ = s16[144,128]{1,0:T(8,128)(2,1)S(1)} collective-permute-done((s16[144,128]{1,0:T(8,128)(2,1)S(1)}, s16[144,128]{1,0:T(8,128)(2,1)S(1)}, u32[]{:S(2)}, u32[]{:S(2)}) %collective-permute-start.15) | collective-permute-done | bytes 36896 | tf_op jit(solution)/shard_map/ppermute | solution.py:201
  50.6 0.9 %last.1 = f32[128,256]{1,0:T(8,128)} custom-call(f32[1,128,128]{2,1,0:T(8,128)S(1)} %get-tuple-element.41.refs_0_, f32[1,128,128]{2,1,0:T(8,128)S(1)} %get-tuple-element.48.refs_1_, s16[144,128]{1,0:T(8,128)(2,1)S(1)} %collective-permute-done.13.refs_2_, s16[144,128]{1,0:T(8,128)(2,1)S(1)} %collective-permute-done.14.refs_3_, ...), custom_call_target="tpu_custom_call" | custom-call | bytes 802816 | tf_op jit(solution)/shard_map/last/pallas_call | solution.py:24
  (7 shorter events, 0.0 us)
Async XLA Ops:
  0.0 1.2 %copy-start = (bf16[16,32768]{1,0:T(8,128)(2,1)S(1)}, bf16[16,32768]{1,0:T(8,128)(2,1)}, u32[]{:S(2)}) copy-start(bf16[16,32768]{1,0:T(8,128)(2,1)} %amplitudes_ref.1) | copy-start | bytes 3145732
  1.3 2.1 %collective-permute-start = (bf16[8,16,2048]{2,1,0:T(8,128)(2,1)S(1)}, bf16[8,16,2048]{2,1,0:T(8,128)(2,1)S(1)}, u32[]{:S(2)}, u32[]{:S(2)}) collective-permute-start(bf16[8,16,2048]{2,1,0:T(8,128)(2,1)S(1)} %get-tuple-element.30), channel_id=1, source_target_pairs={{0,1},{1,0},{2,3},{3,2},{4,5},{5,4},{6,7},{7,6},{8,9},{9,8},{10,11... | collective-permute-start | bytes 1572872 | tf_op jit(solution)/shard_map/ppermute | solution.py:201
  3.4 10.3 %collective-permute-start.1 = (bf16[32,2048]{1,0:T(8,128)(2,1)S(1)}, bf16[32,2048]{1,0:T(8,128)(2,1)S(1)}, u32[]{:S(2)}, u32[]{:S(2)}) collective-permute-start(bf16[32,2048]{1,0:T(8,128)(2,1)S(1)} %get-tuple-element.31), channel_id=1, source_target_pairs={{0,14},{1,15},{2,12},{3,13},{4,10},{5,11},{6,8},{7,9},{8,6},{9,7},... | collective-permute-start | bytes 393224 | tf_op jit(solution)/shard_map/ppermute | solution.py:201
  9.4 9.2 %collective-permute-start.2 = (bf16[32,2048]{1,0:T(8,128)(2,1)S(1)}, bf16[32,2048]{1,0:T(8,128)(2,1)S(1)}, u32[]{:S(2)}, u32[]{:S(2)}) collective-permute-start(bf16[32,2048]{1,0:T(8,128)(2,1)S(1)} %get-tuple-element.34), channel_id=1, source_target_pairs={{0,2},{1,3},{2,0},{3,1},{4,6},{5,7},{6,4},{7,5},{8,10},{9,11},{10,... | collective-permute-start | bytes 393224 | tf_op jit(solution)/shard_map/ppermute | solution.py:201
  9.9 14.2 %collective-permute-start.3 = (bf16[32,2048]{1,0:T(8,128)(2,1)S(1)}, bf16[32,2048]{1,0:T(8,128)(2,1)S(1)}, u32[]{:S(2)}, u32[]{:S(2)}) collective-permute-start(bf16[32,2048]{1,0:T(8,128)(2,1)S(1)} %get-tuple-element.35), channel_id=1, source_target_pairs={{0,4},{1,5},{2,6},{3,7},{4,0},{5,1},{6,2},{7,3},{8,12},{9,13},{10,... | collective-permute-start | bytes 393224 | tf_op jit(solution)/shard_map/ppermute | solution.py:201
  9.9 14.2 %collective-permute-start.4 = (bf16[32,2048]{1,0:T(8,128)(2,1)S(1)}, bf16[32,2048]{1,0:T(8,128)(2,1)S(1)}, u32[]{:S(2)}, u32[]{:S(2)}) collective-permute-start(bf16[32,2048]{1,0:T(8,128)(2,1)S(1)} %get-tuple-element.36), channel_id=1, source_target_pairs={{0,6},{1,7},{2,4},{3,5},{4,2},{5,3},{6,0},{7,1},{8,14},{9,15},{10,... | collective-permute-start | bytes 393224 | tf_op jit(solution)/shard_map/ppermute | solution.py:201
  12.9 15.6 %collective-permute-start.8 = (bf16[32,2048]{1,0:T(8,128)(2,1)S(1)}, bf16[32,2048]{1,0:T(8,128)(2,1)S(1)}, u32[]{:S(2)}, u32[]{:S(2)}) collective-permute-start(bf16[32,2048]{1,0:T(8,128)(2,1)S(1)} %get-tuple-element.43), channel_id=1, source_target_pairs={{0,8},{1,9},{2,10},{3,11},{4,12},{5,13},{6,14},{7,15},{8,0},{9,1},... | collective-permute-start | bytes 393224 | tf_op jit(solution)/shard_map/ppermute | solution.py:201
  13.8 17.6 %collective-permute-start.9 = (bf16[32,2048]{1,0:T(8,128)(2,1)S(1)}, bf16[32,2048]{1,0:T(8,128)(2,1)S(1)}, u32[]{:S(2)}, u32[]{:S(2)}) collective-permute-start(bf16[32,2048]{1,0:T(8,128)(2,1)S(1)} %get-tuple-element.44), channel_id=1, source_target_pairs={{0,10},{1,11},{2,8},{3,9},{4,14},{5,15},{6,12},{7,13},{8,2},{9,3},... | collective-permute-start | bytes 393224 | tf_op jit(solution)/shard_map/ppermute | solution.py:201
  18.6 12.7 %collective-permute-start.10 = (bf16[32,2048]{1,0:T(8,128)(2,1)S(1)}, bf16[32,2048]{1,0:T(8,128)(2,1)S(1)}, u32[]{:S(2)}, u32[]{:S(2)}) collective-permute-start(bf16[32,2048]{1,0:T(8,128)(2,1)S(1)} %get-tuple-element.45), channel_id=1, source_target_pairs={{0,12},{1,13},{2,14},{3,15},{4,8},{5,9},{6,10},{7,11},{8,4},{9,5},... | collective-permute-start | bytes 393224 | tf_op jit(solution)/shard_map/ppermute | solution.py:201
  19.0 0.7 %copy-start.1 = (s32[16,16]{1,0:T(8,128)S(1)}, s32[16,16]{1,0:T(8,128)}, u32[]{:S(2)}) copy-start(s32[16,16]{1,0:T(8,128)} %mask_ref.1) | copy-start | bytes 3076
  25.5 7.2 %collective-permute-start.5 = (f32[8,128,128]{2,1,0:T(8,128)S(1)}, f32[8,128,128]{2,1,0:T(8,128)S(1)}, u32[]{:S(2)}, u32[]{:S(2)}) collective-permute-start(f32[8,128,128]{2,1,0:T(8,128)S(1)} %product.5), channel_id=1, source_target_pairs={{0,1},{1,0},{2,3},{3,2},{4,5},{5,4},{6,7},{7,6},{8,9},{9,8},{10,11... | collective-permute-start | bytes 1572872 | tf_op jit(solution)/shard_map/ppermute | solution.py:201
  32.6 14.8 %copy-start.2 = (s32[256]{0:T(256)S(1)}, s32[256]{0:T(256)}, u32[]{:S(2)}) copy-start(s32[256]{0:T(256)} %param.7) | copy-start | bytes 3076
  32.6 3.2 %collective-permute-start.11 = (f32[8,128,128]{2,1,0:T(8,128)S(1)}, f32[8,128,128]{2,1,0:T(8,128)S(1)}, u32[]{:S(2)}, u32[]{:S(2)}) collective-permute-start(f32[8,128,128]{2,1,0:T(8,128)S(1)} %product.7), channel_id=1, source_target_pairs={{0,1},{1,0},{2,3},{3,2},{4,5},{5,4},{6,7},{7,6},{8,9},{9,8},{10,11... | collective-permute-start | bytes 1572872 | tf_op jit(solution)/shard_map/ppermute | solution.py:201
  32.8 6.0 %collective-permute-start.6 = (s16[528,128]{1,0:T(8,128)(2,1)S(1)}, s16[528,128]{1,0:T(8,128)(2,1)S(1)}, u32[]{:S(2)}, u32[]{:S(2)}) collective-permute-start(s16[528,128]{1,0:T(8,128)(2,1)S(1)} %get-tuple-element.38), channel_id=1, source_target_pairs={{0,4},{1,5},{2,6},{3,7},{4,0},{5,1},{6,2},{7,3},{8,12},{9,13},{10,... | collective-permute-start | bytes 405512 | tf_op jit(solution)/shard_map/ppermute | solution.py:201
  35.9 6.0 %collective-permute-start.12 = (s16[528,128]{1,0:T(8,128)(2,1)S(1)}, s16[528,128]{1,0:T(8,128)(2,1)S(1)}, u32[]{:S(2)}, u32[]{:S(2)}) collective-permute-start(s16[528,128]{1,0:T(8,128)(2,1)S(1)} %get-tuple-element.47), channel_id=1, source_target_pairs={{0,2},{1,3},{2,0},{3,1},{4,6},{5,7},{6,4},{7,5},{8,10},{9,11},{10,... | collective-permute-start | bytes 405512 | tf_op jit(solution)/shard_map/ppermute | solution.py:201
  39.0 6.6 %collective-permute-start.7 = (s16[272,128]{1,0:T(8,128)(2,1)S(1)}, s16[272,128]{1,0:T(8,128)(2,1)S(1)}, u32[]{:S(2)}, u32[]{:S(2)}) collective-permute-start(s16[272,128]{1,0:T(8,128)(2,1)S(1)} %get-tuple-element.40), channel_id=1, source_target_pairs={{0,2},{1,3},{2,0},{3,1},{4,6},{5,7},{6,4},{7,5},{8,10},{9,11},{10,... | collective-permute-start | bytes 208904 | tf_op jit(solution)/shard_map/ppermute | solution.py:201
  42.1 5.6 %collective-permute-start.13 = (s16[144,128]{1,0:T(8,128)(2,1)S(1)}, s16[144,128]{1,0:T(8,128)(2,1)S(1)}, u32[]{:S(2)}, u32[]{:S(2)}) collective-permute-start(s16[144,128]{1,0:T(8,128)(2,1)S(1)} %get-tuple-element.49), channel_id=1, source_target_pairs={{0,8},{1,9},{2,10},{3,11},{4,12},{5,13},{6,14},{7,15},{8,0},{9,1},... | collective-permute-start | bytes 110600 | tf_op jit(solution)/shard_map/ppermute | solution.py:201
  42.9 6.2 %collective-permute-start.14 = (s16[144,128]{1,0:T(8,128)(2,1)S(1)}, s16[144,128]{1,0:T(8,128)(2,1)S(1)}, u32[]{:S(2)}, u32[]{:S(2)}) collective-permute-start(s16[144,128]{1,0:T(8,128)(2,1)S(1)} %get-tuple-element.50), channel_id=1, source_target_pairs={{0,12},{1,13},{2,14},{3,15},{4,8},{5,9},{6,10},{7,11},{8,4},{9,5},... | collective-permute-start | bytes 110600 | tf_op jit(solution)/shard_map/ppermute | solution.py:201
  44.7 4.4 %collective-permute-start.16 = (s16[144,128]{1,0:T(8,128)(2,1)S(1)}, s16[144,128]{1,0:T(8,128)(2,1)S(1)}, u32[]{:S(2)}, u32[]{:S(2)}) collective-permute-start(s16[144,128]{1,0:T(8,128)(2,1)S(1)} %get-tuple-element.52), channel_id=1, source_target_pairs={{0,4},{1,5},{2,6},{3,7},{4,0},{5,1},{6,2},{7,3},{8,12},{9,13},{10,... | collective-permute-start | bytes 110600 | tf_op jit(solution)/shard_map/ppermute | solution.py:201
  45.7 4.9 %collective-permute-start.15 = (s16[144,128]{1,0:T(8,128)(2,1)S(1)}, s16[144,128]{1,0:T(8,128)(2,1)S(1)}, u32[]{:S(2)}, u32[]{:S(2)}) collective-permute-start(s16[144,128]{1,0:T(8,128)(2,1)S(1)} %get-tuple-element.51), channel_id=1, source_target_pairs={{0,8},{1,9},{2,10},{3,11},{4,12},{5,13},{6,14},{7,15},{8,0},{9,1},... | collective-permute-start | bytes 110600 | tf_op jit(solution)/shard_map/ppermute | solution.py:201
